TPU v7x, 256 devices: a whole 4x4x8 slice. The times are simulated.
256 devices in a mesh: rep: 16 (over y, z_lo), fsdp: 16 (over x, z_hi, core).
Axes of the slice: x: 4, y: 4, z: 8 (z_hi: 2, z_lo: 4; z = z_hi * 4 + z_lo), core: 2. Of those that a mesh axis runs over, the one named last changes fastest.
Arguments:
- hidden: bfloat16 [131072, 8192], P(('rep', 'fsdp')), may hold values from -6 to 6
- key_cotangent: bfloat16 [131072, 512], P(('rep', 'fsdp')), may hold values from -6 to 6
- local_weight: bfloat16 [16, 8192, 512], P('rep', 'fsdp'), may hold values from -0.0625 to 0.0625
- outer_delta: float32 [16, 8192, 512], P('rep', 'fsdp'), may hold values from -6 to 6
- global_params: float32 [2, 8192, 512], P(None, 'fsdp'), may hold values from -6 to 6
- momentum: float32 [2, 8192, 512], P(None, 'fsdp'), may hold values from -6 to 6
- outer_step: int32 [1], replicated, may hold values from 0 to 4095
Outputs:
- weight_grad: float32 [16, 8192, 512], P('rep', 'fsdp')
- new_global: float32 [8192, 512], P('fsdp')
- new_momentum: float32 [8192, 512], P('fsdp')
All inputs are finite; a program needn't handle non-finite values.
Results may differ from a plain program's by a relative error of at most 0.0029.
Values may be sent and summed in bfloat16 or wider, within the bound.
No kernel may reach another device: no remote copies, remote signals or barrier semaphores. Data moves between devices by JAX's collectives and lax.ppermute only.
A program may use at most 128 MiB of HBM per device.

v0:
```python
import jax
import jax.numpy as jnp
from jax import lax
from jax.experimental import pallas as pl
from jax.experimental.pallas import tpu as pltpu
from jax.sharding import PartitionSpec as P

HEAD_DIM = 128
FRAGS = 2
NX = 4
NY = 4
NZL = 4
F32 = jnp.float32
BF16 = jnp.bfloat16


def fsdp_perm(dx=0, dz=0, dc=0):
    pairs = []
    for f in range(16):
        x, z, c = f // 4, (f // 2) % 2, f % 2
        pairs.append((f, (((x + dx) % NX) * 2 + (z ^ dz)) * 2 + (c ^ dc)))
    return pairs


def rep_perm(dy=0, dz=0):
    pairs = []
    for r in range(16):
        y, z = r // NZL, r % NZL
        pairs.append((r, ((y + dy) % NY) * NZL + (z + dz) % NZL))
    return pairs


def send(value, **kw):
    return lax.ppermute(value, "fsdp", fsdp_perm(**kw))


def rep_send(value, **kw):
    return lax.ppermute(value, "rep", rep_perm(**kw))


def tie(*values):
    return lax.optimization_barrier(values)


ORDER = (2, 1, 3, 0)
TILE = 256
PARAMS = pltpu.CompilerParams(vmem_limit_bytes=48 * 1024 * 1024)


def rows_dot(a, b):
    return lax.dot_general(a, b, (((0,), (0,)), ((), ())), preferred_element_type=F32)


def backprop(projected, incoming):
    inverse_rms = lax.rsqrt(jnp.mean(projected * projected, axis=-1, keepdims=True) + 1e-06)
    normed = projected * inverse_rms
    incoming = incoming.astype(F32)
    along = jnp.mean(incoming * normed, axis=-1, keepdims=True)
    return (inverse_rms * (incoming - normed * along)).astype(BF16)


def forward_kernel(at_ref, own_ref, sib_ref, *refs):
    weights, out_ref = refs[:-1], refs[-1]
    step = pl.program_id(0)
    tokens = own_ref.shape[0]
    for i, w_ref in enumerate(weights):

        @pl.when(step == i)
        def _():
            for t, h_ref in enumerate((own_ref, sib_ref)):

                for n in range(0, tokens, TILE):
                    term = jnp.dot(h_ref[pl.ds(n, TILE), :], w_ref[...], preferred_element_type=F32)
                    where = pl.ds(t * tokens + n, TILE)
                    if i == 0:
                        out_ref[where, :] = term
                    else:
                        out_ref[where, :] += term


def forward_call(at, own, sib, weights):
    tokens = own.shape[0]
    depth, cols = weights[0].shape
    acts = pl.BlockSpec((tokens, depth), lambda i, at: (0, at[i]))
    whole = pl.BlockSpec((depth, cols), lambda i, at: (0, 0))
    return pl.pallas_call(
        forward_kernel,
        grid_spec=pltpu.PrefetchScalarGridSpec(
            num_scalar_prefetch=1,
            grid=(len(weights),),
            in_specs=[acts, acts] + [whole] * len(weights),
            out_specs=pl.BlockSpec((2 * tokens, cols), lambda i, at: (0, 0)),
        ),
        out_shape=jax.ShapeDtypeStruct((2 * tokens, cols), F32),
        compiler_params=PARAMS,
        cost_estimate=pl.CostEstimate(
            flops=16 * tokens * depth * cols, bytes_accessed=16 * tokens * depth, transcendentals=0
        ),
        name="own_forward",
    )(at, own, sib, *weights)


def middle_kernel(at_ref, own_ref, sib_ref, part_ref, cot_ref, *refs):
    weights, (back_ref, *outs), (held, acc, sems) = refs[:4], refs[4:9], refs[9:]
    tokens = own_ref.shape[0]
    depth = held.shape[2]

    def copy(i, t):
        start = pl.multiple_of(at_ref[i] * depth, depth)
        return pltpu.make_async_copy(
            (own_ref, sib_ref)[t].at[:, pl.ds(start, depth)],
            held.at[i, pl.ds(t * tokens, tokens), :],
            sems.at[i, t],
        )

    for i in range(4):
        for t in range(2):
            copy(i, t).start()
    for i in range(4):
        for t in range(2):
            copy(i, t).wait()

        for n in range(0, 2 * tokens, TILE):
            where = pl.ds(n, TILE)
            term = jnp.dot(held[i, where, :], weights[i][...], preferred_element_type=F32)
            if i == 0:
                acc[where, :] = part_ref[where, :] + term
            else:
                acc[where, :] += term

    for n in range(0, 2 * tokens, TILE):
        where = pl.ds(n, TILE)
        for h in range(0, acc.shape[1], HEAD_DIM):
            head = pl.ds(h, HEAD_DIM)
            back_ref[where, head] = backprop(acc[where, head], cot_ref[where, head])

    for i in range(4):
        for n in range(0, depth, TILE):
            where = pl.ds(n, TILE)
            outs[i][where, :] = rows_dot(held[i, :, where], back_ref[...]).astype(outs[i].dtype)


def middle_call(at, own, sib, part, cot, weights):
    tokens = own.shape[0]
    depth, cols = weights[0].shape
    vmem = pl.BlockSpec(memory_space=pltpu.VMEM)
    hbm = pl.BlockSpec(memory_space=pl.ANY)
    return pl.pallas_call(
        middle_kernel,
        in_specs=[pl.BlockSpec(memory_space=pltpu.SMEM), hbm, hbm] + [vmem] * 6,
        out_specs=[vmem] * 5,
        out_shape=[jax.ShapeDtypeStruct((2 * tokens, cols), BF16)]
        + [jax.ShapeDtypeStruct((depth, cols), t) for t in (BF16, BF16, BF16, F32)],
        scratch_shapes=[
            pltpu.VMEM((4, 2 * tokens, depth), BF16),
            pltpu.VMEM((2 * tokens, cols), F32),
            pltpu.SemaphoreType.DMA((4, 2)),
        ],
        compiler_params=PARAMS,
        cost_estimate=pl.CostEstimate(
            flops=32 * tokens * depth * cols, bytes_accessed=16 * tokens * depth, transcendentals=0
        ),
        name="middle",
    )(at, own, sib, part, cot, *weights)


def gradient_kernel(at_ref, own_ref, sib_ref, back_ref, *outs):
    step = pl.program_id(0)
    tokens, depth = own_ref.shape
    for i, out_ref in enumerate(outs):

        @pl.when(step == i)
        def _():
            for n in range(0, depth, TILE):
                where = pl.ds(n, TILE)
                term = rows_dot(own_ref[:, where], back_ref[:tokens, :])
                term += rows_dot(sib_ref[:, where], back_ref[tokens:, :])
                out_ref[where, :] = term.astype(out_ref.dtype)


def gradient_call(at, own, sib, back, depth):
    tokens = own.shape[0]
    cols = back.shape[1]
    acts = pl.BlockSpec((tokens, depth), lambda i, at: (0, at[i]))
    whole = lambda r: pl.BlockSpec((r, cols), lambda i, at: (0, 0))
    return pl.pallas_call(
        gradient_kernel,
        grid_spec=pltpu.PrefetchScalarGridSpec(
            num_scalar_prefetch=1,
            grid=(4,),
            in_specs=[acts, acts, whole(2 * tokens)],
            out_specs=[whole(depth)] * 4,
        ),
        out_shape=[jax.ShapeDtypeStruct((depth, cols), t) for t in (BF16, BF16, BF16, F32)],
        compiler_params=PARAMS,
        cost_estimate=pl.CostEstimate(
            flops=16 * tokens * depth * cols, bytes_accessed=16 * tokens * depth, transcendentals=0
        ),
        name="gradient",
    )(at, own, sib, back)


def block(value, index, size):
    return lax.dynamic_slice_in_dim(value, index * size, size, 0)


def rep_blocks(delta):
    y = lax.axis_index("rep") // NZL
    n = delta.shape[0] // NY
    return [block(delta, (y + k) % NY, n) for k in range(NY)]


def rep_rows(blocks):
    part = blocks[0]
    for k in (1, 3, 2):
        part = part + rep_send(blocks[k], dy=k)
    return part


def rep_average(part):
    z = lax.axis_index("rep") % NZL
    m = part.shape[0] // NZL
    mine = block(part, z, m)
    for k in (1, 3, 2):
        mine = mine + rep_send(block(part, (z + k) % NZL, m), dz=k)
    return (mine / (NY * NZL)).astype(BF16)


def rep_gather_z(average):
    z = lax.axis_index("rep") % NZL
    ring = jnp.stack([average] + [rep_send(average, dz=-k) for k in (1, 2, 3)])
    return jnp.concatenate([lax.dynamic_index_in_dim(ring, (k - z) % NZL, 0, keepdims=False) for k in range(NZL)])


def rep_gather_y(part):
    y = lax.axis_index("rep") // NZL
    ring = jnp.stack([part] + [rep_send(part, dy=-k) for k in (1, 2, 3)])
    return jnp.concatenate([lax.dynamic_index_in_dim(ring, (k - y) % NY, 0, keepdims=False) for k in range(NY)])


def per_device(hidden, key_cotangent, local_weight, outer_delta, global_params, momentum, outer_step):
    f = lax.axis_index("fsdp")
    x, zh, core = f // 4, (f // 2) % 2, f % 2
    weight = local_weight[0]
    rows, width = weight.shape
    half = width // 2
    chip_rows = 2 * rows
    chip_of = lambda dx, dz: ((x + dx) % NX) * 2 + (zh ^ dz)

    def mine(a):
        return lax.dynamic_slice_in_dim(a, core * half, half, 1)

    def theirs(a):
        return lax.dynamic_slice_in_dim(a, (1 - core) * half, half, 1)

    def in_order(own, other):
        return jnp.where(core == 0, jnp.concatenate([own, other]), jnp.concatenate([other, own]))

    from_sib = send(theirs(weight), dc=1)
    cot_sib = send(theirs(key_cotangent), dc=1)
    blocks = rep_blocks(outer_delta[0])
    here = in_order(mine(weight), from_sib)

    def spread(piece):
        return {0: piece, 3: send(piece, dx=1), 1: send(piece, dx=-1), 2: send(piece, dx=2)}

    away = send(here, dz=1)
    gathered = spread(here)
    here, *blocks = tie(here, *blocks)
    part = rep_rows(blocks)
    away, *gathered, part, hidden = tie(away, *[gathered[dx] for dx in ORDER], part, hidden)
    distant = spread(away)
    hidden_sib = send(hidden, dc=1)
    average = rep_average(part)
    at = lambda dz: jnp.stack([chip_of(dx, dz) for dx in ORDER]).astype(jnp.int32)
    partial = forward_call(at(0), hidden, hidden_sib, gathered)
    partial, average, *distant = tie(partial, average, *[distant[dx] for dx in ORDER])
    cots = jnp.concatenate([mine(key_cotangent), cot_sib])
    back, *found = middle_call(at(1), hidden, hidden_sib, partial, cots, distant)

    def gather(found):
        return [send(found[0], dx=2), send(found[1], dx=1), send(found[2], dx=-1), found[3]]

    def total(found):
        return found[3] + (found[1].astype(F32) + found[2].astype(F32)) + found[0].astype(F32)

    first = gather(found)
    back, average = tie(back, average)
    local = gradient_call(at(0), hidden, hidden_sib, back, chip_rows)
    average = rep_gather_z(average)
    *both, average = tie(*first, *local, average)
    away = send(total(both[:4]).astype(BF16), dz=1)
    local = gather(both[4:])
    average = rep_gather_y(average).astype(F32)
    fragment = outer_step[0] % FRAGS
    old_moment = lax.dynamic_index_in_dim(momentum, fragment, 0, keepdims=False)
    old_params = lax.dynamic_index_in_dim(global_params, fragment, 0, keepdims=False)
    new_momentum = 0.9 * old_moment + average
    new_global = old_params - 0.7 * (average + 0.9 * new_momentum)
    new_momentum, new_global, away, *local = tie(new_momentum, new_global, away, *local)
    local = total(local) + away.astype(F32)
    own = block(local, core, rows)
    other = send(block(local, 1 - core, rows), dc=1)
    grad = jnp.where(core == 0, jnp.concatenate([own, other], 1), jnp.concatenate([other, own], 1))

    return (grad[None], new_global, new_momentum)


def solution(mesh):
    in_specs = (
        P(("rep", "fsdp"), None),
        P(("rep", "fsdp"), None),
        P("rep", "fsdp", None),
        P("rep", "fsdp", None),
        P(None, "fsdp", None),
        P(None, "fsdp", None),
        P(),
    )
    out_specs = (P("rep", "fsdp", None), P("fsdp", None), P("fsdp", None))
    return jax.shard_map(
        per_device, mesh=mesh, in_specs=in_specs, out_specs=out_specs, check_vma=False
    )
```

profile of v0, /device:TPU:1, one launch (start us, length us, event | category | flops | bytes accessed | tf_op | source)
XLA Modules:
  0.0 146.7 jit_solution(2142453596952099230)
XLA Ops:
  0.7 1.1 dynamic-slice_bitcast_fusion.6
  1.7 3.3 %collective-permute-start = (bf16[512,256]{1,0:T(8,128)(2,1)S(1)}, bf16[512,256]{1,0:T(8,128)(2,1)S(1)}, u32[]{:S(2)}, u32[]{:S(2)}) collective-permute-start(bf16[512,256]{1,0:T(8,128)(2,1)S(1)} %get-tuple-element.106), channel_id=1, source_target_pairs={{0,1},{1,0},{2,3},{3,2},{4,5},{5,4},{6,7},{7,6},{8,9},{9,8},{10,11... | collective-permute-start | bytes 786440 | tf_op jit(solution)/shard_map/ppermute | solution.py:34
  5.1 1.3 dynamic-slice_bitcast_fusion.1
  6.4 0.2 maximum_select_fusion.1.refs_3_
  6.6 0.1 collective-permute-start.5
  6.7 2.7 %collective-permute-start.6 = (f32[128,512]{1,0:T(8,128)S(1)}, f32[128,512]{1,0:T(8,128)S(1)}, u32[]{:S(2)}, u32[]{:S(2)}) collective-permute-start(f32[128,512]{1,0:T(8,128)S(1)} %get-tuple-element.49), channel_id=1, source_target_pairs={{0,192},{16,208},{32,224},{48,240},{64,0},{80,16},{96,32},{112,48}... | collective-permute-start | bytes 786440 | tf_op jit(solution)/shard_map/ppermute | solution.py:38
  9.4 5.3 %collective-permute-start.1 = (bf16[1024,256]{1,0:T(8,128)(2,1)S(1)}, bf16[1024,256]{1,0:T(8,128)(2,1)S(1)}, u32[]{:S(2)}, u32[]{:S(2)}) collective-permute-start(bf16[1024,256]{1,0:T(8,128)(2,1)S(1)} %maximum_select_fusion.1.refs_3_), channel_id=1, source_target_pairs={{0,2},{1,3},{2,0},{3,1},{4,6},{5,7},{6,4},{7,5},{8,10},{9,11},{10,... | collective-permute-start | bytes 1572872 | tf_op jit(solution)/shard_map/ppermute | solution.py:34
  14.7 2.7 %collective-permute-start.2 = (bf16[1024,256]{1,0:T(8,128)(2,1)S(1)}, bf16[1024,256]{1,0:T(8,128)(2,1)S(1)}, u32[]{:S(2)}, u32[]{:S(2)}) collective-permute-start(bf16[1024,256]{1,0:T(8,128)(2,1)S(1)} %maximum_select_fusion.1.refs_3_), channel_id=1, source_target_pairs={{0,8},{1,9},{2,10},{3,11},{4,12},{5,13},{6,14},{7,15},{8,0},{9,1},... | collective-permute-start | bytes 1572872 | tf_op jit(solution)/shard_map/ppermute | solution.py:34
  17.4 0.9 collective-permute-start.3
  18.3 0.6 collective-permute-start.4
  18.9 1.6 %collective-permute-start.7 = (f32[128,512]{1,0:T(8,128)S(1)}, f32[128,512]{1,0:T(8,128)S(1)}, u32[]{:S(2)}, u32[]{:S(2)}) collective-permute-start(f32[128,512]{1,0:T(8,128)S(1)} %get-tuple-element.50), channel_id=1, source_target_pairs={{0,128},{16,144},{32,160},{48,176},{64,192},{80,208},{96,224},{112... | collective-permute-start | bytes 786440 | tf_op jit(solution)/shard_map/ppermute | solution.py:38
  20.5 6.0 %collective-permute-done.7 = f32[128,512]{1,0:T(8,128)S(1)} collective-permute-done((f32[128,512]{1,0:T(8,128)S(1)}, f32[128,512]{1,0:T(8,128)S(1)}, u32[]{:S(2)}, u32[]{:S(2)}) %collective-permute-start.7) | collective-permute-done | bytes 262176 | tf_op jit(solution)/shard_map/ppermute | solution.py:38
  26.5 0.1 add_add_fusion
  26.6 1.5 %collective-permute-done.1.refs_3_ = bf16[1024,256]{1,0:T(8,128)(2,1)S(1)} collective-permute-done((bf16[1024,256]{1,0:T(8,128)(2,1)S(1)}, bf16[1024,256]{1,0:T(8,128)(2,1)S(1)}, u32[]{:S(2)}, u32[]{:S(2)}) %collective-permute-start.1) | collective-permute-done | bytes 524320 | tf_op jit(solution)/shard_map/ppermute | solution.py:34
  28.1 0.7 collective-permute-done.2.refs_0_
  28.8 11.6 %collective-permute-done.3.refs_1_ = bf16[1024,256]{1,0:T(8,128)(2,1)S(1)} collective-permute-done((bf16[1024,256]{1,0:T(8,128)(2,1)S(1)}, bf16[1024,256]{1,0:T(8,128)(2,1)S(1)}, u32[]{:S(2)}, u32[]{:S(2)}) %collective-permute-start.3) | collective-permute-done | bytes 524320 | tf_op jit(solution)/shard_map/ppermute | solution.py:34
  40.3 0.9 collective-permute-done.4.refs_2_
  41.3 0.6 collective-permute-start.8
  41.9 0.1 collective-permute-start.15
  42.2 0.1 pad_add_fusion.1.at_ref
  42.3 1.7 %collective-permute-start.10 = (f32[32,512]{1,0:T(8,128)S(1)}, f32[32,512]{1,0:T(8,128)S(1)}, u32[]{:S(2)}, u32[]{:S(2)}) collective-permute-start(f32[32,512]{1,0:T(8,128)S(1)} %get-tuple-element.109), channel_id=1, source_target_pairs={{0,48},{16,0},{32,16},{48,32},{64,112},{80,64},{96,80},{112,96},{1... | collective-permute-start | bytes 196616 | tf_op jit(solution)/shard_map/ppermute | solution.py:38
  44.0 0.3 collective-permute-start.11
  44.3 0.1 pad_add_fusion.at_ref
  44.4 2.6 %collective-permute-start.12 = (bf16[1024,256]{1,0:T(8,128)(2,1)S(1)}, bf16[1024,256]{1,0:T(8,128)(2,1)S(1)}, u32[]{:S(2)}, u32[]{:S(2)}) collective-permute-start(bf16[1024,256]{1,0:T(8,128)(2,1)S(1)} %collective-permute-done.1.refs_3_), channel_id=1, source_target_pairs={{0,8},{1,9},{2,10},{3,11},{4,12},{5,13},{6,14},{7,15},{8,0},{9,1},... | collective-permute-start | bytes 1572872 | tf_op jit(solution)/shard_map/ppermute | solution.py:34
  47.0 2.8 %collective-permute-done.15 = bf16[512,256]{1,0:T(8,128)(2,1)} collective-permute-done((bf16[512,256]{1,0:T(8,128)(2,1)S(1)}, bf16[512,256]{1,0:T(8,128)(2,1)}, u32[]{:S(2)}, u32[]{:S(2)}) %collective-permute-start.15) | collective-permute-done | bytes 262176 | tf_op jit(solution)/shard_map/ppermute | solution.py:34
  49.8 2.2 %collective-permute-start.13 = (bf16[1024,256]{1,0:T(8,128)(2,1)S(1)}, bf16[1024,256]{1,0:T(8,128)(2,1)S(1)}, u32[]{:S(2)}, u32[]{:S(2)}) collective-permute-start(bf16[1024,256]{1,0:T(8,128)(2,1)S(1)} %collective-permute-done.1.refs_3_), channel_id=1, source_target_pairs={{0,12},{1,13},{2,14},{3,15},{4,0},{5,1},{6,2},{7,3},{8,4},{9,5},{1... | collective-permute-start | bytes 1572872 | tf_op jit(solution)/shard_map/ppermute | solution.py:34
  52.0 1.0 collective-permute-start.9
  53.0 1.0 pad_maximum_fusion.cot_ref
  54.0 3.5 %collective-permute-done.9 = f32[32,512]{1,0:T(8,128)S(1)} collective-permute-done((f32[32,512]{1,0:T(8,128)S(1)}, f32[32,512]{1,0:T(8,128)S(1)}, u32[]{:S(2)}, u32[]{:S(2)}) %collective-permute-start.9) | collective-permute-done | bytes 65568 | tf_op jit(solution)/shard_map/ppermute | solution.py:38
  57.5 6.0 %own_forward.1.part_ref = f32[1024,256]{1,0:T(8,128)S(1)} custom-call(s32[4]{0:T(128)S(1)} %pad_add_fusion.1.at_ref, bf16[512,8192]{1,0:T(8,128)(2,1)} %own_ref.2, bf16[512,8192]{1,0:T(8,128)(2,1)} %collective-permute-done.8.sib_ref, bf16[1024,256]{1,0:T(8,128)(2,1)S(1)} %collective-permute-done.2.refs_0_, ...), custom_call_target="tpu_custom_call" | custom-call | flops 2147483648 | bytes 8388608 | tf_op jit(solution)/shard_map/own_forward/pallas_call | solution.py:86
  63.6 0.0 copy-start
  63.6 1.0 copy-done
  64.6 5.4 %collective-permute-done.13.refs_1_ = bf16[1024,256]{1,0:T(8,128)(2,1)S(1)} collective-permute-done((bf16[1024,256]{1,0:T(8,128)(2,1)S(1)}, bf16[1024,256]{1,0:T(8,128)(2,1)S(1)}, u32[]{:S(2)}, u32[]{:S(2)}) %collective-permute-start.13) | collective-permute-done | bytes 524320 | tf_op jit(solution)/shard_map/ppermute | solution.py:34
  70.0 1.0 collective-permute-done.14.refs_2_
  71.0 8.8 %middle.1 = (bf16[1024,256]{1,0:T(8,128)(2,1)S(1)}, bf16[1024,256]{1,0:T(8,128)(2,1)}, bf16[1024,256]{1,0:T(8,128)(2,1)}, bf16[1024,256]{1,0:T(8,128)(2,1)}, f32[1024,256]{1,0:T(8,128)S(1)}) custom-call(s32[4]{0:T(128)S(1)} %pad_add_fusion.at_ref, bf16[512,8192]{1,0:T(8,128)(2,1)} %own_ref.2, bf16[512,8192]{1,0:T(8,128)(2,1)} %collective-permute-done.8.sib_ref, ...), custom_call_target="tpu_custom_call" | custom-call | flops 4294967296 | bytes 8388608 | tf_op jit(solution)/shard_map/middle/pallas_call | solution.py:148
  79.8 1.7 %collective-permute-start.19 = (bf16[32,512]{1,0:T(8,128)(2,1)S(1)}, bf16[32,512]{1,0:T(8,128)(2,1)S(1)}, u32[]{:S(2)}, u32[]{:S(2)}) collective-permute-start(bf16[32,512]{1,0:T(8,128)(2,1)S(1)} %multiply_convert_fusion), channel_id=1, source_target_pairs={{0,48},{16,0},{32,16},{48,32},{64,112},{80,64},{96,80},{112,96},{1... | collective-permute-start | bytes 98312 | tf_op jit(solution)/shard_map/ppermute | solution.py:38
  81.5 0.7 collective-permute-start.20
  82.2 1.3 collective-permute-start.21
  83.5 2.6 %collective-permute-start.16 = (bf16[1024,256]{1,0:T(8,128)(2,1)}, bf16[1024,256]{1,0:T(8,128)(2,1)S(1)}, u32[]{:S(2)}, u32[]{:S(2)}) collective-permute-start(bf16[1024,256]{1,0:T(8,128)(2,1)} %get-tuple-element.63), channel_id=1, source_target_pairs={{0,8},{1,9},{2,10},{3,11},{4,12},{5,13},{6,14},{7,15},{8,0},{9,1},... | collective-permute-start | bytes 1572872 | tf_op jit(solution)/shard_map/ppermute | solution.py:34
  86.1 0.3 collective-permute-start.17
  86.4 2.3 %collective-permute-start.18 = (bf16[1024,256]{1,0:T(8,128)(2,1)}, bf16[1024,256]{1,0:T(8,128)(2,1)S(1)}, u32[]{:S(2)}, u32[]{:S(2)}) collective-permute-start(bf16[1024,256]{1,0:T(8,128)(2,1)} %get-tuple-element.65), channel_id=1, source_target_pairs={{0,12},{1,13},{2,14},{3,15},{4,0},{5,1},{6,2},{7,3},{8,4},{9,5},{1... | collective-permute-start | bytes 1572872 | tf_op jit(solution)/shard_map/ppermute | solution.py:34
  88.8 7.2 %gradient.1 = (bf16[1024,256]{1,0:T(8,128)(2,1)}, bf16[1024,256]{1,0:T(8,128)(2,1)}, bf16[1024,256]{1,0:T(8,128)(2,1)S(1)}, f32[1024,256]{1,0:T(8,128)S(1)}) custom-call(s32[4]{0:T(128)S(1)} %pad_add_fusion.1.at_ref, bf16[512,8192]{1,0:T(8,128)(2,1)} %own_ref.2, bf16[512,8192]{1,0:T(8,128)(2,1)} %collective-permute-done.8.sib_ref, ...), custom_call_target="tpu_custom_call" | custom-call | flops 2147483648 | bytes 8388608 | tf_op jit(solution)/shard_map/gradient/pallas_call | solution.py:186
  96.0 1.3 collective-permute-done.16
  97.3 12.9 %collective-permute-done.17 = bf16[1024,256]{1,0:T(8,128)(2,1)S(1)} collective-permute-done((bf16[1024,256]{1,0:T(8,128)(2,1)}, bf16[1024,256]{1,0:T(8,128)(2,1)S(1)}, u32[]{:S(2)}, u32[]{:S(2)}) %collective-permute-start.17) | collective-permute-done | bytes 524320 | tf_op jit(solution)/shard_map/ppermute | solution.py:34
  110.3 1.4 collective-permute-start.22
  111.7 0.3 collective-permute-start.23
  112.0 0.7 collective-permute-start.24
  112.7 1.1 add_convert_fusion
  113.8 1.2 collective-permute-start.25
  114.9 0.9 collective-permute-start.26
  115.8 2.1 %collective-permute-start.27 = (bf16[1024,256]{1,0:T(8,128)(2,1)}, bf16[1024,256]{1,0:T(8,128)(2,1)}, u32[]{:S(2)}, u32[]{:S(2)}) collective-permute-start(bf16[1024,256]{1,0:T(8,128)(2,1)} %get-tuple-element.81), channel_id=1, source_target_pairs={{0,4},{1,5},{2,6},{3,7},{4,8},{5,9},{6,10},{7,11},{8,12},{9,13},{1... | collective-permute-start | bytes 1572872 | tf_op jit(solution)/shard_map/ppermute | solution.py:34
  117.9 1.9 %collective-permute-start.28 = (bf16[1024,256]{1,0:T(8,128)(2,1)S(1)}, bf16[1024,256]{1,0:T(8,128)(2,1)}, u32[]{:S(2)}, u32[]{:S(2)}) collective-permute-start(bf16[1024,256]{1,0:T(8,128)(2,1)S(1)} %get-tuple-element.82), channel_id=1, source_target_pairs={{0,12},{1,13},{2,14},{3,15},{4,0},{5,1},{6,2},{7,3},{8,4},{9,5},{1... | collective-permute-start | bytes 1572872 | tf_op jit(solution)/shard_map/ppermute | solution.py:34
  120.5 0.0 copy-start.1
  120.5 1.0 collective-permute-done.24
  121.5 1.0 pad_maximum_fusion.1
  122.5 0.1 dynamic-slice_bitcast_fusion.10
  122.5 2.9 %fusion.1 = (f32[512,512]{1,0:T(8,128)}, f32[512,512]{1,0:T(8,128)}) fusion(f32[2,512,512]{2,1,0:T(8,128)S(1)} %copy-done.1, s32[]{:T(128)S(6)} %select_n.219, bf16[128,512]{1,0:T(8,128)(2,1)S(1)} %get-tuple-element.100, bf16[128,512]{1,0:T(8,128)(2,1)S(1)} %get-tuple-element.101, bf16[128,512]{1,0:T(8,128)(2,1)S(1)} %get-tuple-element.102, ...), kind=kLoop, calls=%fused_computation.3 | loop fusion | flops 3670016 | bytes 4718596 | tf_op jit(solution)/shard_map/sub | solution.py:299
  125.4 13.0 %collective-permute-done.25 = bf16[1024,256]{1,0:T(8,128)(2,1)S(1)} collective-permute-done((bf16[1024,256]{1,0:T(8,128)(2,1)}, bf16[1024,256]{1,0:T(8,128)(2,1)S(1)}, u32[]{:S(2)}, u32[]{:S(2)}) %collective-permute-start.25) | collective-permute-done | bytes 524320 | tf_op jit(solution)/shard_map/ppermute | solution.py:34
  138.4 3.4 %collective-permute-done.27 = bf16[1024,256]{1,0:T(8,128)(2,1)} collective-permute-done((bf16[1024,256]{1,0:T(8,128)(2,1)}, bf16[1024,256]{1,0:T(8,128)(2,1)}, u32[]{:S(2)}, u32[]{:S(2)}) %collective-permute-start.27) | collective-permute-done | bytes 524320 | tf_op jit(solution)/shard_map/ppermute | solution.py:34
  141.8 1.5 %convert_add_fusion.2 = f32[1024,256]{1,0:T(8,128)S(1)} fusion(bf16[1024,256]{1,0:T(8,128)(2,1)S(1)} %collective-permute-done.25, bf16[1024,256]{1,0:T(8,128)(2,1)S(1)} %collective-permute-done.26, f32[1024,256]{1,0:T(8,128)S(1)} %get-tuple-element.84, bf16[1024,256]{1,0:T(8,128)(2,1)} %collective-permute-done.28, bf16[1024,256]{1,0:T(8,128)(2,1)} %collective-permute-done.27), kind=kLoop, calls=%fused_computation.5 | loop fusion | flops 2097152 | bytes 4194304 | tf_op jit(solution)/shard_map/add | solution.py:301
  143.3 0.1 dynamic-slice_bitcast_fusion
  143.4 0.6 collective-permute-start.29
  144.0 1.5 %collective-permute-done.29 = f32[512,256]{1,0:T(8,128)S(1)} collective-permute-done((f32[512,256]{1,0:T(8,128)S(1)}, f32[512,256]{1,0:T(8,128)S(1)}, u32[]{:S(2)}, u32[]{:S(2)}) %collective-permute-start.29) | collective-permute-done | bytes 524320 | tf_op jit(solution)/shard_map/ppermute | solution.py:34
  145.6 1.1 maximum_select_fusion
  (25 shorter events, 0.2 us)
Async XLA Ops:
  1.7 4.6 %collective-permute-start = (bf16[512,256]{1,0:T(8,128)(2,1)S(1)}, bf16[512,256]{1,0:T(8,128)(2,1)S(1)}, u32[]{:S(2)}, u32[]{:S(2)}) collective-permute-start(bf16[512,256]{1,0:T(8,128)(2,1)S(1)} %get-tuple-element.106), channel_id=1, source_target_pairs={{0,1},{1,0},{2,3},{3,2},{4,5},{5,4},{6,7},{7,6},{8,9},{9,8},{10,11... | collective-permute-start | bytes 786440 | tf_op jit(solution)/shard_map/ppermute | solution.py:34
  5.1 36.9 %copy-start.2 = (bf16[512,512]{1,0:T(8,128)(2,1)S(1)}, bf16[512,512]{1,0:T(8,128)(2,1)}, u32[]{:S(2)}) copy-start(bf16[512,512]{1,0:T(8,128)(2,1)} %param.8) | copy-start | bytes 1572868
  6.6 11.7 %collective-permute-start.5 = (f32[128,512]{1,0:T(8,128)S(1)}, f32[128,512]{1,0:T(8,128)S(1)}, u32[]{:S(2)}, u32[]{:S(2)}) collective-permute-start(f32[128,512]{1,0:T(8,128)S(1)} %get-tuple-element.48), channel_id=1, source_target_pairs={{0,64},{16,80},{32,96},{48,112},{64,128},{80,144},{96,160},{112,17... | collective-permute-start | bytes 786440 | tf_op jit(solution)/shard_map/ppermute | solution.py:38
  6.7 12.2 %collective-permute-start.6 = (f32[128,512]{1,0:T(8,128)S(1)}, f32[128,512]{1,0:T(8,128)S(1)}, u32[]{:S(2)}, u32[]{:S(2)}) collective-permute-start(f32[128,512]{1,0:T(8,128)S(1)} %get-tuple-element.49), channel_id=1, source_target_pairs={{0,192},{16,208},{32,224},{48,240},{64,0},{80,16},{96,32},{112,48}... | collective-permute-start | bytes 786440 | tf_op jit(solution)/shard_map/ppermute | solution.py:38
  9.4 18.7 %collective-permute-start.1 = (bf16[1024,256]{1,0:T(8,128)(2,1)S(1)}, bf16[1024,256]{1,0:T(8,128)(2,1)S(1)}, u32[]{:S(2)}, u32[]{:S(2)}) collective-permute-start(bf16[1024,256]{1,0:T(8,128)(2,1)S(1)} %maximum_select_fusion.1.refs_3_), channel_id=1, source_target_pairs={{0,2},{1,3},{2,0},{3,1},{4,6},{5,7},{6,4},{7,5},{8,10},{9,11},{10,... | collective-permute-start | bytes 1572872 | tf_op jit(solution)/shard_map/ppermute | solution.py:34
  14.7 14.1 %collective-permute-start.2 = (bf16[1024,256]{1,0:T(8,128)(2,1)S(1)}, bf16[1024,256]{1,0:T(8,128)(2,1)S(1)}, u32[]{:S(2)}, u32[]{:S(2)}) collective-permute-start(bf16[1024,256]{1,0:T(8,128)(2,1)S(1)} %maximum_select_fusion.1.refs_3_), channel_id=1, source_target_pairs={{0,8},{1,9},{2,10},{3,11},{4,12},{5,13},{6,14},{7,15},{8,0},{9,1},... | collective-permute-start | bytes 1572872 | tf_op jit(solution)/shard_map/ppermute | solution.py:34
  17.4 22.9 %collective-permute-start.3 = (bf16[1024,256]{1,0:T(8,128)(2,1)S(1)}, bf16[1024,256]{1,0:T(8,128)(2,1)S(1)}, u32[]{:S(2)}, u32[]{:S(2)}) collective-permute-start(bf16[1024,256]{1,0:T(8,128)(2,1)S(1)} %maximum_select_fusion.1.refs_3_), channel_id=1, source_target_pairs={{0,12},{1,13},{2,14},{3,15},{4,0},{5,1},{6,2},{7,3},{8,4},{9,5},{1... | collective-permute-start | bytes 1572872 | tf_op jit(solution)/shard_map/ppermute | solution.py:34
  18.3 23.0 %collective-permute-start.4 = (bf16[1024,256]{1,0:T(8,128)(2,1)S(1)}, bf16[1024,256]{1,0:T(8,128)(2,1)S(1)}, u32[]{:S(2)}, u32[]{:S(2)}) collective-permute-start(bf16[1024,256]{1,0:T(8,128)(2,1)S(1)} %maximum_select_fusion.1.refs_3_), channel_id=1, source_target_pairs={{0,4},{1,5},{2,6},{3,7},{4,8},{5,9},{6,10},{7,11},{8,12},{9,13},{1... | collective-permute-start | bytes 1572872 | tf_op jit(solution)/shard_map/ppermute | solution.py:34
  18.9 7.6 %collective-permute-start.7 = (f32[128,512]{1,0:T(8,128)S(1)}, f32[128,512]{1,0:T(8,128)S(1)}, u32[]{:S(2)}, u32[]{:S(2)}) collective-permute-start(f32[128,512]{1,0:T(8,128)S(1)} %get-tuple-element.50), channel_id=1, source_target_pairs={{0,128},{16,144},{32,160},{48,176},{64,192},{80,208},{96,224},{112... | collective-permute-start | bytes 786440 | tf_op jit(solution)/shard_map/ppermute | solution.py:38
  41.3 16.3 %collective-permute-start.8 = (bf16[512,8192]{1,0:T(8,128)(2,1)}, bf16[512,8192]{1,0:T(8,128)(2,1)}, u32[]{:S(2)}, u32[]{:S(2)}) collective-permute-start(bf16[512,8192]{1,0:T(8,128)(2,1)} %own_ref.2), channel_id=1, source_target_pairs={{0,1},{1,0},{2,3},{3,2},{4,5},{5,4},{6,7},{7,6},{8,9},{9,8},{10,11... | collective-permute-start | bytes 25165832 | tf_op jit(solution)/shard_map/ppermute | solution.py:34
  41.9 7.8 %collective-permute-start.15 = (bf16[512,256]{1,0:T(8,128)(2,1)S(1)}, bf16[512,256]{1,0:T(8,128)(2,1)}, u32[]{:S(2)}, u32[]{:S(2)}) collective-permute-start(bf16[512,256]{1,0:T(8,128)(2,1)S(1)} %get-tuple-element.104), channel_id=1, source_target_pairs={{0,1},{1,0},{2,3},{3,2},{4,5},{5,4},{6,7},{7,6},{8,9},{9,8},{10,11... | collective-permute-start | bytes 786440 | tf_op jit(solution)/shard_map/ppermute | solution.py:34
  42.3 9.7 %collective-permute-start.10 = (f32[32,512]{1,0:T(8,128)S(1)}, f32[32,512]{1,0:T(8,128)S(1)}, u32[]{:S(2)}, u32[]{:S(2)}) collective-permute-start(f32[32,512]{1,0:T(8,128)S(1)} %get-tuple-element.109), channel_id=1, source_target_pairs={{0,48},{16,0},{32,16},{48,32},{64,112},{80,64},{96,80},{112,96},{1... | collective-permute-start | bytes 196616 | tf_op jit(solution)/shard_map/ppermute | solution.py:38
  44.0 8.0 %collective-permute-start.11 = (f32[32,512]{1,0:T(8,128)S(1)}, f32[32,512]{1,0:T(8,128)S(1)}, u32[]{:S(2)}, u32[]{:S(2)}) collective-permute-start(f32[32,512]{1,0:T(8,128)S(1)} %get-tuple-element.108), channel_id=1, source_target_pairs={{0,32},{16,48},{32,0},{48,16},{64,96},{80,112},{96,64},{112,80},{1... | collective-permute-start | bytes 196616 | tf_op jit(solution)/shard_map/ppermute | solution.py:38
  44.4 20.2 %collective-permute-start.12 = (bf16[1024,256]{1,0:T(8,128)(2,1)S(1)}, bf16[1024,256]{1,0:T(8,128)(2,1)S(1)}, u32[]{:S(2)}, u32[]{:S(2)}) collective-permute-start(bf16[1024,256]{1,0:T(8,128)(2,1)S(1)} %collective-permute-done.1.refs_3_), channel_id=1, source_target_pairs={{0,8},{1,9},{2,10},{3,11},{4,12},{5,13},{6,14},{7,15},{8,0},{9,1},... | collective-permute-start | bytes 1572872 | tf_op jit(solution)/shard_map/ppermute | solution.py:34
  49.8 20.2 %collective-permute-start.13 = (bf16[1024,256]{1,0:T(8,128)(2,1)S(1)}, bf16[1024,256]{1,0:T(8,128)(2,1)S(1)}, u32[]{:S(2)}, u32[]{:S(2)}) collective-permute-start(bf16[1024,256]{1,0:T(8,128)(2,1)S(1)} %collective-permute-done.1.refs_3_), channel_id=1, source_target_pairs={{0,12},{1,13},{2,14},{3,15},{4,0},{5,1},{6,2},{7,3},{8,4},{9,5},{1... | collective-permute-start | bytes 1572872 | tf_op jit(solution)/shard_map/ppermute | solution.py:34
  52.0 19.0 %collective-permute-start.14 = (bf16[1024,256]{1,0:T(8,128)(2,1)S(1)}, bf16[1024,256]{1,0:T(8,128)(2,1)S(1)}, u32[]{:S(2)}, u32[]{:S(2)}) collective-permute-start(bf16[1024,256]{1,0:T(8,128)(2,1)S(1)} %collective-permute-done.1.refs_3_), channel_id=1, source_target_pairs={{0,4},{1,5},{2,6},{3,7},{4,8},{5,9},{6,10},{7,11},{8,12},{9,13},{1... | collective-permute-start | bytes 1572872 | tf_op jit(solution)/shard_map/ppermute | solution.py:34
  52.0 5.5 %collective-permute-start.9 = (f32[32,512]{1,0:T(8,128)S(1)}, f32[32,512]{1,0:T(8,128)S(1)}, u32[]{:S(2)}, u32[]{:S(2)}) collective-permute-start(f32[32,512]{1,0:T(8,128)S(1)} %get-tuple-element.107), channel_id=1, source_target_pairs={{0,16},{16,32},{32,48},{48,0},{64,80},{80,96},{96,112},{112,64},{1... | collective-permute-start | bytes 196616 | tf_op jit(solution)/shard_map/ppermute | solution.py:38
  63.6 1.0 copy-start
  79.8 6.6 %collective-permute-start.19 = (bf16[32,512]{1,0:T(8,128)(2,1)S(1)}, bf16[32,512]{1,0:T(8,128)(2,1)S(1)}, u32[]{:S(2)}, u32[]{:S(2)}) collective-permute-start(bf16[32,512]{1,0:T(8,128)(2,1)S(1)} %multiply_convert_fusion), channel_id=1, source_target_pairs={{0,48},{16,0},{32,16},{48,32},{64,112},{80,64},{96,80},{112,96},{1... | collective-permute-start | bytes 98312 | tf_op jit(solution)/shard_map/ppermute | solution.py:38
  81.5 14.4 %collective-permute-start.20 = (bf16[32,512]{1,0:T(8,128)(2,1)S(1)}, bf16[32,512]{1,0:T(8,128)(2,1)S(1)}, u32[]{:S(2)}, u32[]{:S(2)}) collective-permute-start(bf16[32,512]{1,0:T(8,128)(2,1)S(1)} %multiply_convert_fusion), channel_id=1, source_target_pairs={{0,32},{16,48},{32,0},{48,16},{64,96},{80,112},{96,64},{112,80},{1... | collective-permute-start | bytes 98312 | tf_op jit(solution)/shard_map/ppermute | solution.py:38
  82.2 13.8 %collective-permute-start.21 = (bf16[32,512]{1,0:T(8,128)(2,1)S(1)}, bf16[32,512]{1,0:T(8,128)(2,1)S(1)}, u32[]{:S(2)}, u32[]{:S(2)}) collective-permute-start(bf16[32,512]{1,0:T(8,128)(2,1)S(1)} %multiply_convert_fusion), channel_id=1, source_target_pairs={{0,16},{16,32},{32,48},{48,0},{64,80},{80,96},{96,112},{112,64},{1... | collective-permute-start | bytes 98312 | tf_op jit(solution)/shard_map/ppermute | solution.py:38
  83.5 13.9 %collective-permute-start.16 = (bf16[1024,256]{1,0:T(8,128)(2,1)}, bf16[1024,256]{1,0:T(8,128)(2,1)S(1)}, u32[]{:S(2)}, u32[]{:S(2)}) collective-permute-start(bf16[1024,256]{1,0:T(8,128)(2,1)} %get-tuple-element.63), channel_id=1, source_target_pairs={{0,8},{1,9},{2,10},{3,11},{4,12},{5,13},{6,14},{7,15},{8,0},{9,1},... | collective-permute-start | bytes 1572872 | tf_op jit(solution)/shard_map/ppermute | solution.py:34
  86.1 24.2 %collective-permute-start.17 = (bf16[1024,256]{1,0:T(8,128)(2,1)}, bf16[1024,256]{1,0:T(8,128)(2,1)S(1)}, u32[]{:S(2)}, u32[]{:S(2)}) collective-permute-start(bf16[1024,256]{1,0:T(8,128)(2,1)} %get-tuple-element.64), channel_id=1, source_target_pairs={{0,4},{1,5},{2,6},{3,7},{4,8},{5,9},{6,10},{7,11},{8,12},{9,13},{1... | collective-permute-start | bytes 1572872 | tf_op jit(solution)/shard_map/ppermute | solution.py:34
  86.4 23.8 %collective-permute-start.18 = (bf16[1024,256]{1,0:T(8,128)(2,1)}, bf16[1024,256]{1,0:T(8,128)(2,1)S(1)}, u32[]{:S(2)}, u32[]{:S(2)}) collective-permute-start(bf16[1024,256]{1,0:T(8,128)(2,1)} %get-tuple-element.65), channel_id=1, source_target_pairs={{0,12},{1,13},{2,14},{3,15},{4,0},{5,1},{6,2},{7,3},{8,4},{9,5},{1... | collective-permute-start | bytes 1572872 | tf_op jit(solution)/shard_map/ppermute | solution.py:34
  110.3 5.5 %collective-permute-start.22 = (bf16[128,512]{1,0:T(8,128)(2,1)S(1)}, bf16[128,512]{1,0:T(8,128)(2,1)S(1)}, u32[]{:S(2)}, u32[]{:S(2)}) collective-permute-start(bf16[128,512]{1,0:T(8,128)(2,1)S(1)} %pad_maximum_fusion.4), channel_id=1, source_target_pairs={{0,192},{16,208},{32,224},{48,240},{64,0},{80,16},{96,32},{112,48}... | collective-permute-start | bytes 393224 | tf_op jit(solution)/shard_map/ppermute | solution.py:38
  111.7 6.2 %collective-permute-start.23 = (bf16[128,512]{1,0:T(8,128)(2,1)S(1)}, bf16[128,512]{1,0:T(8,128)(2,1)S(1)}, u32[]{:S(2)}, u32[]{:S(2)}) collective-permute-start(bf16[128,512]{1,0:T(8,128)(2,1)S(1)} %pad_maximum_fusion.4), channel_id=1, source_target_pairs={{0,128},{16,144},{32,160},{48,176},{64,192},{80,208},{96,224},{112... | collective-permute-start | bytes 393224 | tf_op jit(solution)/shard_map/ppermute | solution.py:38
  112.0 9.5 %collective-permute-start.24 = (bf16[128,512]{1,0:T(8,128)(2,1)S(1)}, bf16[128,512]{1,0:T(8,128)(2,1)}, u32[]{:S(2)}, u32[]{:S(2)}) collective-permute-start(bf16[128,512]{1,0:T(8,128)(2,1)S(1)} %pad_maximum_fusion.4), channel_id=1, source_target_pairs={{0,64},{16,80},{32,96},{48,112},{64,128},{80,144},{96,160},{112,17... | collective-permute-start | bytes 393224 | tf_op jit(solution)/shard_map/ppermute | solution.py:38
  113.8 24.6 %collective-permute-start.25 = (bf16[1024,256]{1,0:T(8,128)(2,1)}, bf16[1024,256]{1,0:T(8,128)(2,1)S(1)}, u32[]{:S(2)}, u32[]{:S(2)}) collective-permute-start(bf16[1024,256]{1,0:T(8,128)(2,1)} %add_convert_fusion), channel_id=1, source_target_pairs={{0,2},{1,3},{2,0},{3,1},{4,6},{5,7},{6,4},{7,5},{8,10},{9,11},{10,... | collective-permute-start | bytes 1572872 | tf_op jit(solution)/shard_map/ppermute | solution.py:34
  114.9 23.5 %collective-permute-start.26 = (bf16[1024,256]{1,0:T(8,128)(2,1)}, bf16[1024,256]{1,0:T(8,128)(2,1)S(1)}, u32[]{:S(2)}, u32[]{:S(2)}) collective-permute-start(bf16[1024,256]{1,0:T(8,128)(2,1)} %get-tuple-element.80), channel_id=1, source_target_pairs={{0,8},{1,9},{2,10},{3,11},{4,12},{5,13},{6,14},{7,15},{8,0},{9,1},... | collective-permute-start | bytes 1572872 | tf_op jit(solution)/shard_map/ppermute | solution.py:34
  115.8 26.0 %collective-permute-start.27 = (bf16[1024,256]{1,0:T(8,128)(2,1)}, bf16[1024,256]{1,0:T(8,128)(2,1)}, u32[]{:S(2)}, u32[]{:S(2)}) collective-permute-start(bf16[1024,256]{1,0:T(8,128)(2,1)} %get-tuple-element.81), channel_id=1, source_target_pairs={{0,4},{1,5},{2,6},{3,7},{4,8},{5,9},{6,10},{7,11},{8,12},{9,13},{1... | collective-permute-start | bytes 1572872 | tf_op jit(solution)/shard_map/ppermute | solution.py:34
  117.9 23.9 %collective-permute-start.28 = (bf16[1024,256]{1,0:T(8,128)(2,1)S(1)}, bf16[1024,256]{1,0:T(8,128)(2,1)}, u32[]{:S(2)}, u32[]{:S(2)}) collective-permute-start(bf16[1024,256]{1,0:T(8,128)(2,1)S(1)} %get-tuple-element.82), channel_id=1, source_target_pairs={{0,12},{1,13},{2,14},{3,15},{4,0},{5,1},{6,2},{7,3},{8,4},{9,5},{1... | collective-permute-start | bytes 1572872 | tf_op jit(solution)/shard_map/ppermute | solution.py:34
  120.5 2.1 %copy-start.1 = (f32[2,512,512]{2,1,0:T(8,128)S(1)}, f32[2,512,512]{2,1,0:T(8,128)}, u32[]{:S(2)}) copy-start(f32[2,512,512]{2,1,0:T(8,128)} %param.11) | copy-start | bytes 6291460
  143.4 2.2 %collective-permute-start.29 = (f32[512,256]{1,0:T(8,128)S(1)}, f32[512,256]{1,0:T(8,128)S(1)}, u32[]{:S(2)}, u32[]{:S(2)}) collective-permute-start(f32[512,256]{1,0:T(8,128)S(1)} %get-tuple-element.94), channel_id=1, source_target_pairs={{0,1},{1,0},{2,3},{3,2},{4,5},{5,4},{6,7},{7,6},{8,9},{9,8},{10,11... | collective-permute-start | bytes 1572872 | tf_op jit(solution)/shard_map/ppermute | solution.py:34
where the time goes:
time: 147 us
  waiting for transfers between devices  66.6 us (45%)
  starting transfers between devices  43.7 us (30%)
  Pallas kernels  22.1 us (15%)
  other arithmetic  9.02 us (6%)
  local copies, waits for them, and re-layouts  3.57 us (2%)
  between operations  1.67 us (1%)
    ppermute x18, waiting for transfers between devices, send(): return lax.ppermute(value, 'fsdp', fsdp_perm(**kw))  56.1 us
    ppermute x18, starting transfers between devices, send(): return lax.ppermute(value, 'fsdp', fsdp_perm(**kw))  30.4 us
    ppermute x12, starting transfers between devices, rep_send(): return lax.ppermute(value, 'rep', rep_perm(**kw))  13.3 us
    ppermute x12, waiting for transfers between devices, rep_send(): return lax.ppermute(value, 'rep', rep_perm(**kw))  10.5 us
    pallas_call x1, Pallas kernels, middle_call(): pl.pallas_call(middle_kernel, in_specs=[pl.BlockSpec(memory_space=pltpu.S...  8.85 us
    pallas_call x1, Pallas kernels, gradient_call(): pl.pallas_call(gradient_kernel, grid_spec=pltpu.PrefetchScalarGridSpec(nu...  7.18 us
    pallas_call x1, Pallas kernels, forward_call(): pl.pallas_call(forward_kernel, grid_spec=pltpu.PrefetchScalarGridSpec(num...  6.04 us
  transfers between devices with their start and end apart: 30, of which 15 were waited for; matrix products, arithmetic and copies ran while one was open for 5% of the time, Pallas kernels for 9%

commit v1 on v0

v1 whole, which is shorter than its diff:
```python
import jax
import jax.numpy as jnp
from jax import lax
from jax.experimental import pallas as pl
from jax.experimental.pallas import tpu as pltpu
from jax.sharding import PartitionSpec as P

HEAD_DIM = 128
FRAGS = 2
NX = 4
NY = 4
NZL = 4
F32 = jnp.float32
BF16 = jnp.bfloat16


def fsdp_perm(dx=0, dz=0, dc=0):
    pairs = []
    for f in range(16):
        x, z, c = f // 4, (f // 2) % 2, f % 2
        pairs.append((f, (((x + dx) % NX) * 2 + (z ^ dz)) * 2 + (c ^ dc)))
    return pairs


def rep_perm(dy=0, dz=0):
    pairs = []
    for r in range(16):
        y, z = r // NZL, r % NZL
        pairs.append((r, ((y + dy) % NY) * NZL + (z + dz) % NZL))
    return pairs


def flip_perm(bit):
    return [(r, (r // NZL ^ bit) * NZL + r % NZL) for r in range(16)]


def send(value, **kw):
    return lax.ppermute(value, "fsdp", fsdp_perm(**kw))


def rep_send(value, **kw):
    return lax.ppermute(value, "rep", rep_perm(**kw))


def tie(*values):
    return lax.optimization_barrier(values)


ORDER = (2, 1, 3, 0)
TILE = 256
PARAMS = pltpu.CompilerParams(vmem_limit_bytes=22 * 1024 * 1024)


def rows_dot(a, b):
    return lax.dot_general(a, b, (((0,), (0,)), ((), ())), preferred_element_type=F32)


def backprop(projected, incoming):
    inverse_rms = lax.rsqrt(jnp.mean(projected * projected, axis=-1, keepdims=True) + 1e-06)
    normed = projected * inverse_rms
    incoming = incoming.astype(F32)
    along = jnp.mean(incoming * normed, axis=-1, keepdims=True)
    return (inverse_rms * (incoming - normed * along)).astype(BF16)


def forward_kernel(at_ref, own_ref, sib_ref, *refs):
    weights, (out_ref, held, acts, sems) = refs[:4], refs[4:]
    tokens = own_ref.shape[0]
    depth = held.shape[2]

    def copy(i, t):
        start = pl.multiple_of(at_ref[i] * depth, depth)
        kept = (acts if i < 4 else held).at[i % 4, pl.ds(t * tokens, tokens), :]
        return pltpu.make_async_copy((own_ref, sib_ref)[t].at[:, pl.ds(start, depth)], kept, sems.at[i, t])

    for i in range(8):
        for t in range(2):
            copy(i, t).start()
    for i in range(4):
        for t in range(2):
            copy(i, t).wait()
        for n in range(0, 2 * tokens, TILE):
            where = pl.ds(n, TILE)
            term = jnp.dot(acts[i, where, :], weights[i][...], preferred_element_type=F32)
            if i == 0:
                out_ref[where, :] = term
            else:
                out_ref[where, :] += term
    for i in range(4, 8):
        for t in range(2):
            copy(i, t).wait()


def forward_call(at, own, sib, weights):
    tokens = own.shape[0]
    depth, cols = weights[0].shape
    vmem = pl.BlockSpec(memory_space=pltpu.VMEM)
    hbm = pl.BlockSpec(memory_space=pltpu.HBM)
    return pl.pallas_call(
        forward_kernel,
        in_specs=[pl.BlockSpec(memory_space=pltpu.SMEM), hbm, hbm] + [vmem] * 4,
        out_specs=[vmem, vmem],
        out_shape=[
            jax.ShapeDtypeStruct((2 * tokens, cols), F32),
            jax.ShapeDtypeStruct((4, 2 * tokens, depth), BF16),
        ],
        scratch_shapes=[pltpu.VMEM((4, 2 * tokens, depth), BF16), pltpu.SemaphoreType.DMA((8, 2))],
        compiler_params=PARAMS,
        cost_estimate=pl.CostEstimate(
            flops=16 * tokens * depth * cols, bytes_accessed=0, transcendentals=0
        ),
        name="own_forward",
    )(at, own, sib, *weights)


def middle_kernel(held, part_ref, cot_ref, *refs):
    weights, (back_ref, *outs), acc = refs[:8], refs[8:16], refs[16]
    tokens = held.shape[1] // 2
    depth = held.shape[2]
    for i in range(4):
        for n in range(0, 2 * tokens, TILE):
            where = pl.ds(n, TILE)
            term = sum(
                jnp.dot(held[i, where, pl.ds(h * depth // 2, depth // 2)], weights[2 * i + h][...], preferred_element_type=F32)
                for h in range(2)
            )
            if i == 0:
                acc[where, :] = part_ref[where, :] + term
            else:
                acc[where, :] += term

    for n in range(0, 2 * tokens, TILE):
        where = pl.ds(n, TILE)
        for h in range(0, acc.shape[1], HEAD_DIM):
            head = pl.ds(h, HEAD_DIM)
            back_ref[where, head] = backprop(acc[where, head], cot_ref[where, head])

    for i in range(4):
        for n in range(0, depth, TILE):
            term = rows_dot(held[i, :, pl.ds(n, TILE)], back_ref[...])
            if i == 3:
                outs[6][pl.ds(n, TILE), :] = term
            else:
                out_ref = outs[2 * i + n // (depth // 2)]
                out_ref[pl.ds(n % (depth // 2), TILE), :] = term.astype(out_ref.dtype)


def middle_call(held, part, cot, weights):
    tokens, depth = held.shape[1] // 2, held.shape[2]
    cols = weights[0].shape[1]
    halves = (BF16, BF16, F32, BF16, BF16, F32)
    vmem = pl.BlockSpec(memory_space=pltpu.VMEM)
    return pl.pallas_call(
        middle_kernel,
        in_specs=[vmem] * 11,
        out_specs=[vmem] * 8,
        out_shape=[jax.ShapeDtypeStruct((2 * tokens, cols), BF16)]
        + [jax.ShapeDtypeStruct((depth // 2, cols), t) for t in halves]
        + [jax.ShapeDtypeStruct((depth, cols), F32)],
        scratch_shapes=[pltpu.VMEM((2 * tokens, cols), F32)],
        compiler_params=PARAMS,
        cost_estimate=pl.CostEstimate(
            flops=32 * tokens * depth * cols, bytes_accessed=0, transcendentals=0
        ),
        name="middle",
    )(held, part, cot, *weights)


def gradient_kernel(at_ref, own_ref, sib_ref, back_ref, *refs):
    outs, (acts, sems) = refs[:4], refs[4:]
    tokens = own_ref.shape[0]
    depth = acts.shape[2]

    def copy(i, t):
        start = pl.multiple_of(at_ref[i] * depth, depth)
        kept = acts.at[i, pl.ds(t * tokens, tokens), :]
        return pltpu.make_async_copy((own_ref, sib_ref)[t].at[:, pl.ds(start, depth)], kept, sems.at[i, t])

    for i in range(4):
        for t in range(2):
            copy(i, t).start()
    for i in range(4):
        for t in range(2):
            copy(i, t).wait()
        for n in range(0, depth, TILE):
            where = pl.ds(n, TILE)
            outs[i][where, :] = rows_dot(acts[i, :, where], back_ref[...]).astype(outs[i].dtype)


def gradient_call(at, own, sib, back, depth):
    tokens = own.shape[0]
    cols = back.shape[1]
    vmem = pl.BlockSpec(memory_space=pltpu.VMEM)
    hbm = pl.BlockSpec(memory_space=pltpu.HBM)
    return pl.pallas_call(
        gradient_kernel,
        in_specs=[pl.BlockSpec(memory_space=pltpu.SMEM), hbm, hbm, vmem],
        out_specs=[vmem] * 4,
        out_shape=[jax.ShapeDtypeStruct((depth, cols), t) for t in (BF16, BF16, BF16, F32)],
        scratch_shapes=[pltpu.VMEM((4, 2 * tokens, depth), BF16), pltpu.SemaphoreType.DMA((4, 2))],
        compiler_params=PARAMS,
        cost_estimate=pl.CostEstimate(
            flops=16 * tokens * depth * cols, bytes_accessed=0, transcendentals=0
        ),
        name="gradient",
    )(at, own, sib, back)


def block(value, index, size):
    return lax.dynamic_slice_in_dim(value, index * size, size, 0)


def rep_halves(value, bit):
    n = value.shape[0] // 2
    return block(value, bit, n), block(value, 1 - bit, n).astype(BF16)


def rep_rows(delta):
    y = lax.axis_index("rep") // NZL
    for bit in (1, 2):
        kept, given = rep_halves(delta, (y // bit) % 2)
        delta = kept, lax.ppermute(given, "rep", flip_perm(bit))
        if bit == 1:
            delta = delta[0] + delta[1].astype(F32)
    return delta


def rep_parts(pieces):
    part = pieces[0] + pieces[1].astype(F32)
    z = lax.axis_index("rep") % NZL
    m = part.shape[0] // NZL
    return [block(part, z, m)] + [rep_send(block(part, (z + k) % NZL, m), dz=k) for k in (1, 2, 3)]


def rep_average(pieces):
    total = pieces[0] + pieces[1] + pieces[3] + pieces[2]
    average = (total / (NY * NZL)).astype(BF16)
    return [average] + [rep_send(average, dz=-k) for k in (1, 2, 3)]


def ordered(pieces, index, holders):
    ring = jnp.stack(pieces)
    n = len(pieces)
    return jnp.concatenate([lax.dynamic_index_in_dim(ring, (k - index) % n, 0, keepdims=False) for k in holders])


def rep_gather(pieces):
    part = ordered(pieces, lax.axis_index("rep") % NZL, range(NZL))
    return [part] + [rep_send(part, dy=-k) for k in (1, 2, 3)]


def per_device(hidden, key_cotangent, local_weight, outer_delta, global_params, momentum, outer_step):
    f = lax.axis_index("fsdp")
    x, zh, core = f // 4, (f // 2) % 2, f % 2
    weight = local_weight[0]
    rows, width = weight.shape
    half = width // 2
    chip_rows = 2 * rows
    chip_of = lambda dx, dz: ((x + dx) % NX) * 2 + (zh ^ dz)

    def mine(a):
        return lax.dynamic_slice_in_dim(a, core * half, half, 1)

    def theirs(a):
        return lax.dynamic_slice_in_dim(a, (1 - core) * half, half, 1)

    def in_order(own, other):
        return jnp.where(core == 0, jnp.concatenate([own, other]), jnp.concatenate([other, own]))

    from_sib = send(jnp.concatenate([theirs(weight), theirs(key_cotangent)]), dc=1)
    cots = jnp.concatenate([mine(key_cotangent), from_sib[rows:]])
    here = in_order(mine(weight), from_sib[:rows])

    def spread(piece):
        return {0: piece, 3: send(piece, dx=1), 1: send(piece, dx=-1), 2: send(piece, dx=2)}

    away = send(here, dz=1)
    gathered = spread(here)
    far, right, left, away, here, cots, hidden, *blocks = tie(
        gathered[2], gathered[1], gathered[3], away, here, cots, hidden, *rep_rows(outer_delta[0])
    )
    gathered = [far, right, left, here]
    top, bottom = away[:rows], away[rows:]
    from_left, from_right = send(top, dx=1), send(bottom, dx=-1)
    far = [send(from_left, dx=1), send(from_right, dx=-1)]
    distant = [*far, send(top, dx=-1), from_right, from_left, send(bottom, dx=1), top, bottom]
    hidden_sib = send(hidden, dc=1)
    blocks = rep_parts(blocks)
    at = lambda dz: jnp.stack([chip_of(dx, dz) for dx in ORDER]).astype(jnp.int32)
    both = jnp.concatenate([at(0), at(1)])
    partial, held = forward_call(both, hidden, hidden_sib, gathered)
    partial, held, *rest = tie(partial, held, *distant, *blocks)
    distant, blocks = rest[:8], rest[8:]
    back, *found = middle_call(held, partial, cots, distant)

    def gather(found):
        return [send(found[0], dx=2), send(found[1], dx=1), send(found[2], dx=-1), found[3]]

    def total(found):
        found = [v.astype(F32) for v in found]
        return found[3] + (found[1] + found[2]) + found[0]

    up, down = send(found[0], dx=1), send(found[1], dx=-1)
    bottom, top = send(found[3], dx=1), send(found[4], dx=-1)
    up = send((found[2] + up.astype(F32)).astype(BF16), dx=1)
    down = send((found[5] + down.astype(F32)).astype(BF16), dx=-1)
    first = (up, down, bottom, top, found[6])
    back, *blocks = tie(back, *blocks)
    local = gradient_call(at(0), hidden, hidden_sib, back, chip_rows)
    rest = tie(*first, *local, *rep_average(blocks))
    (up, down, bottom, top, mid), local, blocks = rest[:5], rest[5:9], rest[9:]
    added = jnp.concatenate([up.astype(F32) + top.astype(F32), bottom.astype(F32) + down.astype(F32)])
    away = send((mid + added).astype(BF16), dz=1)
    local = gather(local)
    summed = [total([block(v, index, rows) for v in local]) for index in (core, 1 - core)]
    here, there, away, *blocks = tie(*summed, away, *rep_gather(blocks))
    finish = [v + block(away, index, rows).astype(F32) for v, index in zip((here, there), (core, 1 - core))]
    own, other = finish[0], send(finish[1], dc=1)
    average = ordered(blocks, lax.axis_index("rep") // NZL, (0, 2, 1, 3)).astype(F32)
    fragment = outer_step[0] % FRAGS
    old_moment = lax.dynamic_index_in_dim(momentum, fragment, 0, keepdims=False)
    old_params = lax.dynamic_index_in_dim(global_params, fragment, 0, keepdims=False)
    new_momentum = 0.9 * old_moment + average
    new_global = old_params - 0.7 * (average + 0.9 * new_momentum)
    grad = jnp.where(core == 0, jnp.concatenate([own, other], 1), jnp.concatenate([other, own], 1))

    return (grad[None], new_global, new_momentum)


def solution(mesh):
    in_specs = (
        P(("rep", "fsdp"), None),
        P(("rep", "fsdp"), None),
        P("rep", "fsdp", None),
        P("rep", "fsdp", None),
        P(None, "fsdp", None),
        P(None, "fsdp", None),
        P(),
    )
    out_specs = (P("rep", "fsdp", None), P("fsdp", None), P("fsdp", None))
    return jax.shard_map(
        per_device, mesh=mesh, in_specs=in_specs, out_specs=out_specs, check_vma=False
    )
```

time: 147 us -> 137 us (0.932)
  waiting for transfers between devices: 66.6 us -> 30.1 us
  starting transfers between devices: 43.7 us -> 68.5 us
  local copies, waits for them, and re-layouts: 3.57 us -> 9.75 us
  Pallas kernels: 22.1 us -> 16.6 us
    ppermute x18 -> x23, waiting for transfers between devices: 56.1 us -> 26.4 us  [send(): return lax.ppermute(value, 'fsdp', fsdp_perm(**kw))]
    ppermute x18 -> x23, starting transfers between devices: 30.4 us -> 47.1 us  [send(): return lax.ppermute(value, 'fsdp', fsdp_perm(**kw))]
    ppermute x12 -> x9, waiting for transfers between devices: 10.5 us -> 1.31 us  [rep_send(): return lax.ppermute(value, 'rep', rep_perm(**kw))]
    pallas_call x3, Pallas kernels: 22.1 us -> 16.6 us  [the longest x1 6.69 us: middle_call(): pl.pallas_call(middle_kernel, in_specs=[vmem] * 11, out_specs=[vmem] * 8,...]
    ppermute x12 -> x9, starting transfers between devices: 13.3 us -> 18.6 us  [rep_send(): return lax.ppermute(value, 'rep', rep_perm(**kw))]
    unnamed x6 -> x16, local copies, waits for them, and re-layouts: 0.97 us -> 3.87 us
    ppermute x0 -> x2, starting transfers between devices: none -> 2.8 us  [rep_rows(): delta = (kept, lax.ppermute(given, 'rep', flip_perm(bit)))]
    ppermute x0 -> x2, waiting for transfers between devices: none -> 2.35 us  [rep_rows(): delta = (kept, lax.ppermute(given, 'rep', flip_perm(bit)))]
  transfers between devices with their start and end apart: 30 -> 34, of which waited for: 15 -> 11; matrix products, arithmetic and copies ran while one was open for 5% -> 9% of each run, Pallas kernels for 9% -> 7%
where the time goes in v1:
time: 137 us
  starting transfers between devices  68.5 us (50%)
  waiting for transfers between devices  30.1 us (22%)
  Pallas kernels  16.6 us (12%)
  other arithmetic  10 us (7%)
  local copies, waits for them, and re-layouts  9.75 us (7%)
  between operations  1.86 us (1%)
    ppermute x23, starting transfers between devices, send(): return lax.ppermute(value, 'fsdp', fsdp_perm(**kw))  47.1 us
    ppermute x23, waiting for transfers between devices, send(): return lax.ppermute(value, 'fsdp', fsdp_perm(**kw))  26.4 us
    ppermute x9, starting transfers between devices, rep_send(): return lax.ppermute(value, 'rep', rep_perm(**kw))  18.6 us
    pallas_call x1, Pallas kernels, middle_call(): pl.pallas_call(middle_kernel, in_specs=[vmem] * 11, out_specs=[vmem] * 8,...  6.69 us
    pallas_call x1, Pallas kernels, gradient_call(): pl.pallas_call(gradient_kernel, in_specs=[pl.BlockSpec(memory_space=pltpu...  5.11 us
    pallas_call x1, Pallas kernels, forward_call(): pl.pallas_call(forward_kernel, in_specs=[pl.BlockSpec(memory_space=pltpu....  4.75 us
    unnamed x16, local copies, waits for them, and re-layouts  3.87 us
    ppermute x2, starting transfers between devices, rep_rows(): delta = (kept, lax.ppermute(given, 'rep', flip_perm(bit)))  2.8 us
  transfers between devices with their start and end apart: 34, of which 11 were waited for; matrix products, arithmetic and copies ran while one was open for 9% of the time, Pallas kernels for 7%

profile of v1, /device:TPU:1, one launch (start us, length us, event | category | flops | bytes accessed | tf_op | source)
XLA Modules:
  0.0 136.7 jit_solution(272613052887833463)
XLA Ops:
  0.7 1.1 dynamic-slice_bitcast_fusion.1
  1.7 1.1 constant_dynamic-slice_fusion.5
  2.8 3.3 %collective-permute-start = (bf16[1024,256]{1,0:T(8,128)(2,1)S(1)}, bf16[1024,256]{1,0:T(8,128)(2,1)S(1)}, u32[]{:S(2)}, u32[]{:S(2)}) collective-permute-start(bf16[1024,256]{1,0:T(8,128)(2,1)S(1)} %pad_maximum_fusion), channel_id=1, source_target_pairs={{0,1},{1,0},{2,3},{3,2},{4,5},{5,4},{6,7},{7,6},{8,9},{9,8},{10,11... | collective-permute-start | bytes 1572872 | tf_op jit(solution)/shard_map/ppermute | solution.py:38
  6.2 1.1 fusion.3
  7.3 0.1 collective-permute-start.5
  7.4 0.3 collective-permute-done
  7.7 0.2 maximum_select_fusion.1.refs_3_
  8.0 2.0 %collective-permute-start.1 = (bf16[1024,256]{1,0:T(8,128)(2,1)S(1)}, bf16[1024,256]{1,0:T(8,128)(2,1)S(1)}, u32[]{:S(2)}, u32[]{:S(2)}) collective-permute-start(bf16[1024,256]{1,0:T(8,128)(2,1)S(1)} %maximum_select_fusion.1.refs_3_), channel_id=1, source_target_pairs={{0,8},{1,9},{2,10},{3,11},{4,12},{5,13},{6,14},{7,15},{8,0},{9,1},... | collective-permute-start | bytes 1572872 | tf_op jit(solution)/shard_map/ppermute | solution.py:38
  10.0 0.9 collective-permute-start.2
  10.9 0.6 collective-permute-start.3
  11.5 6.9 %collective-permute-start.4 = (bf16[1024,256]{1,0:T(8,128)(2,1)S(1)}, bf16[1024,256]{1,0:T(8,128)(2,1)}, u32[]{:S(2)}, u32[]{:S(2)}) collective-permute-start(bf16[1024,256]{1,0:T(8,128)(2,1)S(1)} %maximum_select_fusion.1.refs_3_), channel_id=1, source_target_pairs={{0,2},{1,3},{2,0},{3,1},{4,6},{5,7},{6,4},{7,5},{8,10},{9,11},{10,... | collective-permute-start | bytes 1572872 | tf_op jit(solution)/shard_map/ppermute | solution.py:38
  18.4 1.1 bitcast_add_fusion
  19.5 2.7 %collective-permute-start.6 = (bf16[128,512]{1,0:T(8,128)(2,1)S(1)}, bf16[128,512]{1,0:T(8,128)(2,1)S(1)}, u32[]{:S(2)}, u32[]{:S(2)}) collective-permute-start(bf16[128,512]{1,0:T(8,128)(2,1)S(1)} %dynamic-slice_convert_fusion.1), channel_id=1, source_target_pairs={{0,128},{16,144},{32,160},{48,176},{64,192},{80,208},{96,224},{112... | collective-permute-start | bytes 393224 | tf_op jit(solution)/shard_map/ppermute | solution.py:222
  22.2 0.7 constant_dynamic-slice_fusion.4
  23.0 2.3 %collective-permute-done.6 = bf16[128,512]{1,0:T(8,128)(2,1)S(1)} collective-permute-done((bf16[128,512]{1,0:T(8,128)(2,1)S(1)}, bf16[128,512]{1,0:T(8,128)(2,1)S(1)}, u32[]{:S(2)}, u32[]{:S(2)}) %collective-permute-start.6) | collective-permute-done | bytes 131104 | tf_op jit(solution)/shard_map/ppermute | solution.py:222
  25.4 8.0 %collective-permute-done.2.refs_1_ = bf16[1024,256]{1,0:T(8,128)(2,1)S(1)} collective-permute-done((bf16[1024,256]{1,0:T(8,128)(2,1)S(1)}, bf16[1024,256]{1,0:T(8,128)(2,1)S(1)}, u32[]{:S(2)}, u32[]{:S(2)}) %collective-permute-start.2) | collective-permute-done | bytes 524320 | tf_op jit(solution)/shard_map/ppermute | solution.py:38
  33.3 1.3 collective-permute-done.3.refs_2_
  34.7 0.5 collective-permute-start.7
  35.2 1.1 fusion.4
  36.2 1.8 %collective-permute-start.10 = (bf16[512,256]{1,0:T(8,128)(2,1)S(1)}, bf16[512,256]{1,0:T(8,128)(2,1)S(1)}, u32[]{:S(2)}, u32[]{:S(2)}) collective-permute-start(bf16[512,256]{1,0:T(8,128)(2,1)S(1)} %get-tuple-element.85.refs_7_), channel_id=1, source_target_pairs={{0,12},{1,13},{2,14},{3,15},{4,0},{5,1},{6,2},{7,3},{8,4},{9,5},{1... | collective-permute-start | bytes 786440 | tf_op jit(solution)/shard_map/ppermute | solution.py:38
  38.0 1.0 convert_add_fusion.7
  39.0 0.7 constant_dynamic-slice_fusion
  39.6 8.7 %collective-permute-start.14 = (f32[32,512]{1,0:T(8,128)S(1)}, f32[32,512]{1,0:T(8,128)S(1)}, u32[]{:S(2)}, u32[]{:S(2)}) collective-permute-start(f32[32,512]{1,0:T(8,128)S(1)} %get-tuple-element.147), channel_id=1, source_target_pairs={{0,16},{16,32},{32,48},{48,0},{64,80},{80,96},{96,112},{112,64},{1... | collective-permute-start | bytes 196616 | tf_op jit(solution)/shard_map/ppermute | solution.py:42
  48.3 0.7 collective-permute-start.15
  49.1 0.6 collective-permute-done.14
  49.7 2.7 %collective-permute-start.12 = (bf16[512,256]{1,0:T(8,128)(2,1)S(1)}, bf16[512,256]{1,0:T(8,128)(2,1)}, u32[]{:S(2)}, u32[]{:S(2)}) collective-permute-start(bf16[512,256]{1,0:T(8,128)(2,1)S(1)} %get-tuple-element.84.refs_6_), channel_id=1, source_target_pairs={{0,12},{1,13},{2,14},{3,15},{4,0},{5,1},{6,2},{7,3},{8,4},{9,5},{1... | collective-permute-start | bytes 786440 | tf_op jit(solution)/shard_map/ppermute | solution.py:38
  52.3 0.0 collective-permute-done.15
  52.4 2.7 %collective-permute-start.11 = (bf16[512,256]{1,0:T(8,128)(2,1)S(1)}, bf16[512,256]{1,0:T(8,128)(2,1)}, u32[]{:S(2)}, u32[]{:S(2)}) collective-permute-start(bf16[512,256]{1,0:T(8,128)(2,1)S(1)} %collective-permute-done.10.refs_3_), channel_id=1, source_target_pairs={{0,12},{1,13},{2,14},{3,15},{4,0},{5,1},{6,2},{7,3},{8,4},{9,5},{1... | collective-permute-start | bytes 786440 | tf_op jit(solution)/shard_map/ppermute | solution.py:38
  55.2 0.1 concatenate.48.at_ref
  55.3 3.7 %collective-permute-start.16 = (f32[32,512]{1,0:T(8,128)}, f32[32,512]{1,0:T(8,128)S(1)}, u32[]{:S(2)}, u32[]{:S(2)}) collective-permute-start(f32[32,512]{1,0:T(8,128)} %get-tuple-element.145), channel_id=1, source_target_pairs={{0,48},{16,0},{32,16},{48,32},{64,112},{80,64},{96,80},{112,96},{1... | collective-permute-start | bytes 196616 | tf_op jit(solution)/shard_map/ppermute | solution.py:42
  59.0 3.4 %copy-done = bf16[512,8192]{1,0:T(8,128)(2,1)S(1)} copy-done((bf16[512,8192]{1,0:T(8,128)(2,1)S(1)}, bf16[512,8192]{1,0:T(8,128)(2,1)}, u32[]{:S(2)}) %copy-start) | copy-done | bytes 8388632
  62.4 4.8 %own_forward.1 = (f32[1024,256]{1,0:T(8,128)S(1)}, bf16[4,1024,1024]{2,1,0:T(8,128)(2,1)S(1)}) custom-call(s32[8]{0:T(128)S(1)} %concatenate.48.at_ref, bf16[512,8192]{1,0:T(8,128)(2,1)S(1)} %copy-done, bf16[512,8192]{1,0:T(8,128)(2,1)} %collective-permute-done.7.sib_ref, bf16[1024,256]{1,0:T(8,128)(2,1)S(1)} %collective-permute-done.1.refs_0_, ...), custom_call_target="tpu_custom_call" | custom-call | flops 2147483648 | tf_op jit(solution)/shard_map/own_forward/pallas_call | solution.py:99
  67.2 0.0 slice-start
  67.2 0.0 copy-start.5
  67.3 6.7 %middle.1 = (bf16[1024,256]{1,0:T(8,128)(2,1)S(1)}, bf16[512,256]{1,0:T(8,128)(2,1)S(1)}, bf16[512,256]{1,0:T(8,128)(2,1)S(1)}, f32[512,256]{1,0:T(8,128)S(1)}, ...) custom-call(bf16[4,1024,1024]{2,1,0:T(8,128)(2,1)S(1)} %get-tuple-el, ...), custom_call_target="tpu_custom_call" | custom-call | flops 4294967296 | tf_op jit(solution)/shard_map/middle/pallas_call | solution.py:153
  74.0 2.6 %collective-permute-start.19 = (bf16[512,256]{1,0:T(8,128)(2,1)S(1)}, bf16[512,256]{1,0:T(8,128)(2,1)S(1)}, u32[]{:S(2)}, u32[]{:S(2)}) collective-permute-start(bf16[512,256]{1,0:T(8,128)(2,1)S(1)} %get-tuple-element.89), channel_id=1, source_target_pairs={{0,12},{1,13},{2,14},{3,15},{4,0},{5,1},{6,2},{7,3},{8,4},{9,5},{1... | collective-permute-start | bytes 786440 | tf_op jit(solution)/shard_map/ppermute | solution.py:38
  76.6 0.9 collective-permute-start.23
  77.6 2.3 %collective-permute-done.19 = bf16[512,256]{1,0:T(8,128)(2,1)S(1)} collective-permute-done((bf16[512,256]{1,0:T(8,128)(2,1)S(1)}, bf16[512,256]{1,0:T(8,128)(2,1)S(1)}, u32[]{:S(2)}, u32[]{:S(2)}) %collective-permute-start.19) | collective-permute-done | bytes 262176 | tf_op jit(solution)/shard_map/ppermute | solution.py:38
  79.9 3.1 %collective-permute-start.22 = (bf16[512,256]{1,0:T(8,128)(2,1)S(1)}, bf16[512,256]{1,0:T(8,128)(2,1)S(1)}, u32[]{:S(2)}, u32[]{:S(2)}) collective-permute-start(bf16[512,256]{1,0:T(8,128)(2,1)S(1)} %get-tuple-element.91), channel_id=1, source_target_pairs={{0,12},{1,13},{2,14},{3,15},{4,0},{5,1},{6,2},{7,3},{8,4},{9,5},{1... | collective-permute-start | bytes 786440 | tf_op jit(solution)/shard_map/ppermute | solution.py:38
  83.0 0.1 add_convert_fusion
  83.1 0.1 collective-permute-start.20
  83.2 0.1 add_convert_fusion.1
  83.3 1.8 %collective-permute-start.18 = (bf16[512,256]{1,0:T(8,128)(2,1)S(1)}, bf16[512,256]{1,0:T(8,128)(2,1)S(1)}, u32[]{:S(2)}, u32[]{:S(2)}) collective-permute-start(bf16[512,256]{1,0:T(8,128)(2,1)S(1)} %add_convert_fusion.1), channel_id=1, source_target_pairs={{0,4},{1,5},{2,6},{3,7},{4,8},{5,9},{6,10},{7,11},{8,12},{9,13},{1... | collective-permute-start | bytes 786440 | tf_op jit(solution)/shard_map/ppermute | solution.py:38
  85.0 0.1 pad_add_fusion.at_ref
  85.1 0.0 collective-permute-start.25
  85.2 5.1 %gradient.1 = (bf16[1024,256]{1,0:T(8,128)(2,1)S(1)}, bf16[1024,256]{1,0:T(8,128)(2,1)S(1)}, bf16[1024,256]{1,0:T(8,128)(2,1)S(1)}, f32[1024,256]{1,0:T(8,128)S(1)}) custom-call(s32[4]{0:T(128)S(1)} %pad_add_fusion.at_ref, bf16[512,8192]{1,0:T(8,128)(2,1)S(1)} %bitcast.53, bf16[512,8192]{1,0:T(8,128)(2,1)} %collective-permute-done.7.sib_ref, ...), custom_call_target="tpu_custom_call" | custom-call | flops 2147483648 | tf_op jit(solution)/shard_map/gradient/pallas_call | solution.py:195
  90.3 0.7 collective-permute-done.20
  91.1 3.0 %collective-permute-done.18 = bf16[512,256]{1,0:T(8,128)(2,1)S(1)} collective-permute-done((bf16[512,256]{1,0:T(8,128)(2,1)S(1)}, bf16[512,256]{1,0:T(8,128)(2,1)S(1)}, u32[]{:S(2)}, u32[]{:S(2)}) %collective-permute-start.18) | collective-permute-done | bytes 262176 | tf_op jit(solution)/shard_map/ppermute | solution.py:38
  94.1 2.7 %collective-permute-start.27 = (bf16[1024,256]{1,0:T(8,128)(2,1)S(1)}, bf16[1024,256]{1,0:T(8,128)(2,1)}, u32[]{:S(2)}, u32[]{:S(2)}) collective-permute-start(bf16[1024,256]{1,0:T(8,128)(2,1)S(1)} %get-tuple-element.109), channel_id=1, source_target_pairs={{0,12},{1,13},{2,14},{3,15},{4,0},{5,1},{6,2},{7,3},{8,4},{9,5},{1... | collective-permute-start | bytes 1572872 | tf_op jit(solution)/shard_map/ppermute | solution.py:38
  96.7 0.1 convert_add_fusion.3
  96.9 0.9 fusion.2
  97.8 8.0 %collective-permute-start.29 = (bf16[1024,256]{1,0:T(8,128)(2,1)}, bf16[1024,256]{1,0:T(8,128)(2,1)S(1)}, u32[]{:S(2)}, u32[]{:S(2)}) collective-permute-start(bf16[1024,256]{1,0:T(8,128)(2,1)} %fusion.2), channel_id=1, source_target_pairs={{0,2},{1,3},{2,0},{3,1},{4,6},{5,7},{6,4},{7,5},{8,10},{9,11},{10,... | collective-permute-start | bytes 1572872 | tf_op jit(solution)/shard_map/ppermute | solution.py:38
  105.8 2.0 %collective-permute-start.30 = (bf16[128,512]{1,0:T(8,128)(2,1)S(1)}, bf16[128,512]{1,0:T(8,128)(2,1)S(1)}, u32[]{:S(2)}, u32[]{:S(2)}) collective-permute-start(bf16[128,512]{1,0:T(8,128)(2,1)S(1)} %pad_maximum_fusion.5), channel_id=1, source_target_pairs={{0,192},{16,208},{32,224},{48,240},{64,0},{80,16},{96,32},{112,48}... | collective-permute-start | bytes 393224 | tf_op jit(solution)/shard_map/ppermute | solution.py:42
  107.8 2.5 %collective-permute-start.31 = (bf16[128,512]{1,0:T(8,128)(2,1)S(1)}, bf16[128,512]{1,0:T(8,128)(2,1)S(1)}, u32[]{:S(2)}, u32[]{:S(2)}) collective-permute-start(bf16[128,512]{1,0:T(8,128)(2,1)S(1)} %pad_maximum_fusion.5), channel_id=1, source_target_pairs={{0,128},{16,144},{32,160},{48,176},{64,192},{80,208},{96,224},{112... | collective-permute-start | bytes 393224 | tf_op jit(solution)/shard_map/ppermute | solution.py:42
  110.3 3.1 %collective-permute-done.28 = bf16[1024,256]{1,0:T(8,128)(2,1)} collective-permute-done((bf16[1024,256]{1,0:T(8,128)(2,1)S(1)}, bf16[1024,256]{1,0:T(8,128)(2,1)}, u32[]{:S(2)}, u32[]{:S(2)}) %collective-permute-start.28) | collective-permute-done | bytes 524320 | tf_op jit(solution)/shard_map/ppermute | solution.py:38
  113.5 1.6 %convert_add_fusion.5 = (f32[512,256]{1,0:T(8,128)S(1)}, f32[512,256]{1,0:T(8,128)S(1)}) fusion(f32[1024,256]{1,0:T(8,128)S(1)} %get-tuple-element.107, s32[]{:T(128)S(6)} %select_n.250, bf16[1024,256]{1,0:T(8,128)(2,1)} %collective-permute-done.28, bf16[1024,256]{1,0:T(8,128)(2,1)} %collective-permute-done.27, ...), kind=kLoop, calls=%fused_computation.17 | loop fusion | flops 1572864 | bytes 3670024 | tf_op jit(solution)/shard_map/add | solution.py:301
  115.1 0.7 collective-permute-done.32
  115.8 7.6 %collective-permute-done.29 = bf16[1024,256]{1,0:T(8,128)(2,1)S(1)} collective-permute-done((bf16[1024,256]{1,0:T(8,128)(2,1)}, bf16[1024,256]{1,0:T(8,128)(2,1)S(1)}, u32[]{:S(2)}, u32[]{:S(2)}) %collective-permute-start.29) | collective-permute-done | bytes 524320 | tf_op jit(solution)/shard_map/ppermute | solution.py:38
  123.3 0.9 add_bitcast_fusion
  124.2 7.4 %collective-permute-start.33 = (f32[512,256]{1,0:T(8,128)}, f32[512,256]{1,0:T(8,128)S(1)}, u32[]{:S(2)}, u32[]{:S(2)}) collective-permute-start(f32[512,256]{1,0:T(8,128)} %get-tuple-element.136), channel_id=1, source_target_pairs={{0,1},{1,0},{2,3},{3,2},{4,5},{5,4},{6,7},{7,6},{8,9},{9,8},{10,11... | collective-permute-start | bytes 1572872 | tf_op jit(solution)/shard_map/ppermute | solution.py:38
  132.3 1.1 pad_maximum_fusion.2
  133.5 0.5 copy-done.2
  133.9 1.6 %fusion.1 = (f32[512,512]{1,0:T(8,128)}, f32[512,512]{1,0:T(8,128)}) fusion(f32[2,512,512]{2,1,0:T(8,128)S(1)} %copy-done.1, s32[]{:T(128)S(6)} %select_n.261, bf16[128,512]{1,0:T(8,128)(2,1)S(1)} %get-tuple-element.132, bf16[128,512]{1,0:T(8,128)(2,1)S(1)} %get-tuple-element.133, bf16[128,512]{1,0:T(8,128)(2,1)S(1)} %get-tuple-element.134, ...), kind=kLoop, calls=%fused_computation.3 | loop fusion | flops 3670016 | bytes 4718596 | tf_op jit(solution)/shard_map/sub | solution.py:324
  135.6 1.1 maximum_select_fusion
  (53 shorter events, 0.4 us)
Async XLA Ops:
  2.8 4.9 %collective-permute-start = (bf16[1024,256]{1,0:T(8,128)(2,1)S(1)}, bf16[1024,256]{1,0:T(8,128)(2,1)S(1)}, u32[]{:S(2)}, u32[]{:S(2)}) collective-permute-start(bf16[1024,256]{1,0:T(8,128)(2,1)S(1)} %pad_maximum_fusion), channel_id=1, source_target_pairs={{0,1},{1,0},{2,3},{3,2},{4,5},{5,4},{6,7},{7,6},{8,9},{9,8},{10,11... | collective-permute-start | bytes 1572872 | tf_op jit(solution)/shard_map/ppermute | solution.py:38
  7.3 11.1 %collective-permute-start.5 = (bf16[256,512]{1,0:T(8,128)(2,1)S(1)}, bf16[256,512]{1,0:T(8,128)(2,1)S(1)}, u32[]{:S(2)}, u32[]{:S(2)}) collective-permute-start(bf16[256,512]{1,0:T(8,128)(2,1)S(1)} %fusion.3), channel_id=1, source_target_pairs={{0,64},{16,80},{32,96},{48,112},{64,0},{80,16},{96,32},{112,48},{1... | collective-permute-start | bytes 786440 | tf_op jit(solution)/shard_map/ppermute | solution.py:222
  8.0 17.4 %collective-permute-start.1 = (bf16[1024,256]{1,0:T(8,128)(2,1)S(1)}, bf16[1024,256]{1,0:T(8,128)(2,1)S(1)}, u32[]{:S(2)}, u32[]{:S(2)}) collective-permute-start(bf16[1024,256]{1,0:T(8,128)(2,1)S(1)} %maximum_select_fusion.1.refs_3_), channel_id=1, source_target_pairs={{0,8},{1,9},{2,10},{3,11},{4,12},{5,13},{6,14},{7,15},{8,0},{9,1},... | collective-permute-start | bytes 1572872 | tf_op jit(solution)/shard_map/ppermute | solution.py:38
  10.0 23.3 %collective-permute-start.2 = (bf16[1024,256]{1,0:T(8,128)(2,1)S(1)}, bf16[1024,256]{1,0:T(8,128)(2,1)S(1)}, u32[]{:S(2)}, u32[]{:S(2)}) collective-permute-start(bf16[1024,256]{1,0:T(8,128)(2,1)S(1)} %maximum_select_fusion.1.refs_3_), channel_id=1, source_target_pairs={{0,12},{1,13},{2,14},{3,15},{4,0},{5,1},{6,2},{7,3},{8,4},{9,5},{1... | collective-permute-start | bytes 1572872 | tf_op jit(solution)/shard_map/ppermute | solution.py:38
  10.9 23.8 %collective-permute-start.3 = (bf16[1024,256]{1,0:T(8,128)(2,1)S(1)}, bf16[1024,256]{1,0:T(8,128)(2,1)S(1)}, u32[]{:S(2)}, u32[]{:S(2)}) collective-permute-start(bf16[1024,256]{1,0:T(8,128)(2,1)S(1)} %maximum_select_fusion.1.refs_3_), channel_id=1, source_target_pairs={{0,4},{1,5},{2,6},{3,7},{4,8},{5,9},{6,10},{7,11},{8,12},{9,13},{1... | collective-permute-start | bytes 1572872 | tf_op jit(solution)/shard_map/ppermute | solution.py:38
  11.5 23.2 %collective-permute-start.4 = (bf16[1024,256]{1,0:T(8,128)(2,1)S(1)}, bf16[1024,256]{1,0:T(8,128)(2,1)}, u32[]{:S(2)}, u32[]{:S(2)}) collective-permute-start(bf16[1024,256]{1,0:T(8,128)(2,1)S(1)} %maximum_select_fusion.1.refs_3_), channel_id=1, source_target_pairs={{0,2},{1,3},{2,0},{3,1},{4,6},{5,7},{6,4},{7,5},{8,10},{9,11},{10,... | collective-permute-start | bytes 1572872 | tf_op jit(solution)/shard_map/ppermute | solution.py:38
  19.5 5.8 %collective-permute-start.6 = (bf16[128,512]{1,0:T(8,128)(2,1)S(1)}, bf16[128,512]{1,0:T(8,128)(2,1)S(1)}, u32[]{:S(2)}, u32[]{:S(2)}) collective-permute-start(bf16[128,512]{1,0:T(8,128)(2,1)S(1)} %dynamic-slice_convert_fusion.1), channel_id=1, source_target_pairs={{0,128},{16,144},{32,160},{48,176},{64,192},{80,208},{96,224},{112... | collective-permute-start | bytes 393224 | tf_op jit(solution)/shard_map/ppermute | solution.py:222
  34.7 20.7 %collective-permute-start.7 = (bf16[512,8192]{1,0:T(8,128)(2,1)}, bf16[512,8192]{1,0:T(8,128)(2,1)}, u32[]{:S(2)}, u32[]{:S(2)}) collective-permute-start(bf16[512,8192]{1,0:T(8,128)(2,1)} %own_ref.1), channel_id=1, source_target_pairs={{0,1},{1,0},{2,3},{3,2},{4,5},{5,4},{6,7},{7,6},{8,9},{9,8},{10,11... | collective-permute-start | bytes 25165832 | tf_op jit(solution)/shard_map/ppermute | solution.py:38
  36.2 16.1 %collective-permute-start.10 = (bf16[512,256]{1,0:T(8,128)(2,1)S(1)}, bf16[512,256]{1,0:T(8,128)(2,1)S(1)}, u32[]{:S(2)}, u32[]{:S(2)}) collective-permute-start(bf16[512,256]{1,0:T(8,128)(2,1)S(1)} %get-tuple-element.85.refs_7_), channel_id=1, source_target_pairs={{0,12},{1,13},{2,14},{3,15},{4,0},{5,1},{6,2},{7,3},{8,4},{9,5},{1... | collective-permute-start | bytes 786440 | tf_op jit(solution)/shard_map/ppermute | solution.py:38
  38.0 17.1 %collective-permute-start.8 = (bf16[512,256]{1,0:T(8,128)(2,1)S(1)}, bf16[512,256]{1,0:T(8,128)(2,1)}, u32[]{:S(2)}, u32[]{:S(2)}) collective-permute-start(bf16[512,256]{1,0:T(8,128)(2,1)S(1)} %get-tuple-element.84.refs_6_), channel_id=1, source_target_pairs={{0,4},{1,5},{2,6},{3,7},{4,8},{5,9},{6,10},{7,11},{8,12},{9,13},{1... | collective-permute-start | bytes 786440 | tf_op jit(solution)/shard_map/ppermute | solution.py:38
  39.6 10.0 %collective-permute-start.14 = (f32[32,512]{1,0:T(8,128)S(1)}, f32[32,512]{1,0:T(8,128)S(1)}, u32[]{:S(2)}, u32[]{:S(2)}) collective-permute-start(f32[32,512]{1,0:T(8,128)S(1)} %get-tuple-element.147), channel_id=1, source_target_pairs={{0,16},{16,32},{32,48},{48,0},{64,80},{80,96},{96,112},{112,64},{1... | collective-permute-start | bytes 196616 | tf_op jit(solution)/shard_map/ppermute | solution.py:42
  48.3 4.0 %collective-permute-start.15 = (f32[32,512]{1,0:T(8,128)S(1)}, f32[32,512]{1,0:T(8,128)S(1)}, u32[]{:S(2)}, u32[]{:S(2)}) collective-permute-start(f32[32,512]{1,0:T(8,128)S(1)} %get-tuple-element.146), channel_id=1, source_target_pairs={{0,32},{16,48},{32,0},{48,16},{64,96},{80,112},{96,64},{112,80},{1... | collective-permute-start | bytes 196616 | tf_op jit(solution)/shard_map/ppermute | solution.py:42
  49.7 17.5 %collective-permute-start.12 = (bf16[512,256]{1,0:T(8,128)(2,1)S(1)}, bf16[512,256]{1,0:T(8,128)(2,1)}, u32[]{:S(2)}, u32[]{:S(2)}) collective-permute-start(bf16[512,256]{1,0:T(8,128)(2,1)S(1)} %get-tuple-element.84.refs_6_), channel_id=1, source_target_pairs={{0,12},{1,13},{2,14},{3,15},{4,0},{5,1},{6,2},{7,3},{8,4},{9,5},{1... | collective-permute-start | bytes 786440 | tf_op jit(solution)/shard_map/ppermute | solution.py:38
  52.3 2.8 %copy-start.4 = (f32[32,512]{1,0:T(8,128)}, f32[32,512]{1,0:T(8,128)S(1)}, u32[]{:S(2)}) copy-start(f32[32,512]{1,0:T(8,128)S(1)} %collective-permute-done.15) | copy-start | bytes 196612
  52.4 14.9 %collective-permute-start.13 = (bf16[512,256]{1,0:T(8,128)(2,1)S(1)}, bf16[512,256]{1,0:T(8,128)(2,1)}, u32[]{:S(2)}, u32[]{:S(2)}) collective-permute-start(bf16[512,256]{1,0:T(8,128)(2,1)S(1)} %get-tuple-element.85.refs_7_), channel_id=1, source_target_pairs={{0,4},{1,5},{2,6},{3,7},{4,8},{5,9},{6,10},{7,11},{8,12},{9,13},{1... | collective-permute-start | bytes 786440 | tf_op jit(solution)/shard_map/ppermute | solution.py:38
  52.4 14.9 %collective-permute-start.11 = (bf16[512,256]{1,0:T(8,128)(2,1)S(1)}, bf16[512,256]{1,0:T(8,128)(2,1)}, u32[]{:S(2)}, u32[]{:S(2)}) collective-permute-start(bf16[512,256]{1,0:T(8,128)(2,1)S(1)} %collective-permute-done.10.refs_3_), channel_id=1, source_target_pairs={{0,12},{1,13},{2,14},{3,15},{4,0},{5,1},{6,2},{7,3},{8,4},{9,5},{1... | collective-permute-start | bytes 786440 | tf_op jit(solution)/shard_map/ppermute | solution.py:38
  55.1 12.1 %collective-permute-start.9 = (bf16[512,256]{1,0:T(8,128)(2,1)}, bf16[512,256]{1,0:T(8,128)(2,1)}, u32[]{:S(2)}, u32[]{:S(2)}) collective-permute-start(bf16[512,256]{1,0:T(8,128)(2,1)} %collective-permute-done.8.refs_4_), channel_id=1, source_target_pairs={{0,4},{1,5},{2,6},{3,7},{4,8},{5,9},{6,10},{7,11},{8,12},{9,13},{1... | collective-permute-start | bytes 786440 | tf_op jit(solution)/shard_map/ppermute | solution.py:38
  55.3 11.9 %collective-permute-start.16 = (f32[32,512]{1,0:T(8,128)}, f32[32,512]{1,0:T(8,128)S(1)}, u32[]{:S(2)}, u32[]{:S(2)}) collective-permute-start(f32[32,512]{1,0:T(8,128)} %get-tuple-element.145), channel_id=1, source_target_pairs={{0,48},{16,0},{32,16},{48,32},{64,112},{80,64},{96,80},{112,96},{1... | collective-permute-start | bytes 196616 | tf_op jit(solution)/shard_map/ppermute | solution.py:42
  59.0 3.4 %copy-start = (bf16[512,8192]{1,0:T(8,128)(2,1)S(1)}, bf16[512,8192]{1,0:T(8,128)(2,1)}, u32[]{:S(2)}) copy-start(bf16[512,8192]{1,0:T(8,128)(2,1)} %own_ref.1) | copy-start | bytes 25165828
  67.2 17.9 %slice-start = ((s8[8388608]{0:T(1024)(128)(4,1)}), s8[4194304]{0:T(1024)(128)(4,1)S(1)}, s32[]{:S(2)}) async-start(s8[8388608]{0:T(1024)(128)(4,1)} %bitcast.52), calls=%async_computation | async-start | bytes 8388608
  67.2 9.4 %copy-start.5 = (f32[32,512]{1,0:T(8,128)S(1)}, f32[32,512]{1,0:T(8,128)}, u32[]{:S(2)}) copy-start(f32[32,512]{1,0:T(8,128)} %copy-done.4) | copy-start | bytes 196612
  67.3 17.9 %slice-start.1 = ((s8[8388608]{0:T(1024)(128)(4,1)}), s8[4194304]{0:T(1024)(128)(4,1)S(1)}, s32[]{:S(2)}) async-start(s8[8388608]{0:T(1024)(128)(4,1)} %bitcast.52), calls=%async_computation.1 | async-start | bytes 8388608
  74.0 6.0 %collective-permute-start.19 = (bf16[512,256]{1,0:T(8,128)(2,1)S(1)}, bf16[512,256]{1,0:T(8,128)(2,1)S(1)}, u32[]{:S(2)}, u32[]{:S(2)}) collective-permute-start(bf16[512,256]{1,0:T(8,128)(2,1)S(1)} %get-tuple-element.89), channel_id=1, source_target_pairs={{0,12},{1,13},{2,14},{3,15},{4,0},{5,1},{6,2},{7,3},{8,4},{9,5},{1... | collective-permute-start | bytes 786440 | tf_op jit(solution)/shard_map/ppermute | solution.py:38
  76.6 6.5 %collective-permute-start.17 = (bf16[512,256]{1,0:T(8,128)(2,1)S(1)}, bf16[512,256]{1,0:T(8,128)(2,1)S(1)}, u32[]{:S(2)}, u32[]{:S(2)}) collective-permute-start(bf16[512,256]{1,0:T(8,128)(2,1)S(1)} %get-tuple-element.87), channel_id=1, source_target_pairs={{0,4},{1,5},{2,6},{3,7},{4,8},{5,9},{6,10},{7,11},{8,12},{9,13},{1... | collective-permute-start | bytes 786440 | tf_op jit(solution)/shard_map/ppermute | solution.py:38
  76.6 6.6 %collective-permute-start.23 = (bf16[32,512]{1,0:T(8,128)(2,1)S(1)}, bf16[32,512]{1,0:T(8,128)(2,1)S(1)}, u32[]{:S(2)}, u32[]{:S(2)}) collective-permute-start(bf16[32,512]{1,0:T(8,128)(2,1)S(1)} %multiply_convert_fusion), channel_id=1, source_target_pairs={{0,48},{16,0},{32,16},{48,32},{64,112},{80,64},{96,80},{112,96},{1... | collective-permute-start | bytes 98312 | tf_op jit(solution)/shard_map/ppermute | solution.py:42
  77.6 7.5 %collective-permute-start.24 = (bf16[32,512]{1,0:T(8,128)(2,1)S(1)}, bf16[32,512]{1,0:T(8,128)(2,1)S(1)}, u32[]{:S(2)}, u32[]{:S(2)}) collective-permute-start(bf16[32,512]{1,0:T(8,128)(2,1)S(1)} %multiply_convert_fusion), channel_id=1, source_target_pairs={{0,32},{16,48},{32,0},{48,16},{64,96},{80,112},{96,64},{112,80},{1... | collective-permute-start | bytes 98312 | tf_op jit(solution)/shard_map/ppermute | solution.py:42
  77.6 12.7 %collective-permute-start.21 = (bf16[512,256]{1,0:T(8,128)(2,1)S(1)}, bf16[512,256]{1,0:T(8,128)(2,1)S(1)}, u32[]{:S(2)}, u32[]{:S(2)}) collective-permute-start(bf16[512,256]{1,0:T(8,128)(2,1)S(1)} %get-tuple-element.90), channel_id=1, source_target_pairs={{0,4},{1,5},{2,6},{3,7},{4,8},{5,9},{6,10},{7,11},{8,12},{9,13},{1... | collective-permute-start | bytes 786440 | tf_op jit(solution)/shard_map/ppermute | solution.py:38
  79.9 10.4 %collective-permute-start.22 = (bf16[512,256]{1,0:T(8,128)(2,1)S(1)}, bf16[512,256]{1,0:T(8,128)(2,1)S(1)}, u32[]{:S(2)}, u32[]{:S(2)}) collective-permute-start(bf16[512,256]{1,0:T(8,128)(2,1)S(1)} %get-tuple-element.91), channel_id=1, source_target_pairs={{0,12},{1,13},{2,14},{3,15},{4,0},{5,1},{6,2},{7,3},{8,4},{9,5},{1... | collective-permute-start | bytes 786440 | tf_op jit(solution)/shard_map/ppermute | solution.py:38
  83.1 8.0 %collective-permute-start.20 = (bf16[512,256]{1,0:T(8,128)(2,1)S(1)}, bf16[512,256]{1,0:T(8,128)(2,1)S(1)}, u32[]{:S(2)}, u32[]{:S(2)}) collective-permute-start(bf16[512,256]{1,0:T(8,128)(2,1)S(1)} %add_convert_fusion), channel_id=1, source_target_pairs={{0,12},{1,13},{2,14},{3,15},{4,0},{5,1},{6,2},{7,3},{8,4},{9,5},{1... | collective-permute-start | bytes 786440 | tf_op jit(solution)/shard_map/ppermute | solution.py:38
  83.3 10.8 %collective-permute-start.18 = (bf16[512,256]{1,0:T(8,128)(2,1)S(1)}, bf16[512,256]{1,0:T(8,128)(2,1)S(1)}, u32[]{:S(2)}, u32[]{:S(2)}) collective-permute-start(bf16[512,256]{1,0:T(8,128)(2,1)S(1)} %add_convert_fusion.1), channel_id=1, source_target_pairs={{0,4},{1,5},{2,6},{3,7},{4,8},{5,9},{6,10},{7,11},{8,12},{9,13},{1... | collective-permute-start | bytes 786440 | tf_op jit(solution)/shard_map/ppermute | solution.py:38
  85.1 5.2 %collective-permute-start.25 = (bf16[32,512]{1,0:T(8,128)(2,1)S(1)}, bf16[32,512]{1,0:T(8,128)(2,1)S(1)}, u32[]{:S(2)}, u32[]{:S(2)}) collective-permute-start(bf16[32,512]{1,0:T(8,128)(2,1)S(1)} %multiply_convert_fusion), channel_id=1, source_target_pairs={{0,16},{16,32},{32,48},{48,0},{64,80},{80,96},{96,112},{112,64},{1... | collective-permute-start | bytes 98312 | tf_op jit(solution)/shard_map/ppermute | solution.py:42
  94.1 13.8 %collective-permute-start.26 = (bf16[1024,256]{1,0:T(8,128)(2,1)S(1)}, bf16[1024,256]{1,0:T(8,128)(2,1)}, u32[]{:S(2)}, u32[]{:S(2)}) collective-permute-start(bf16[1024,256]{1,0:T(8,128)(2,1)S(1)} %get-tuple-element.108), channel_id=1, source_target_pairs={{0,4},{1,5},{2,6},{3,7},{4,8},{5,9},{6,10},{7,11},{8,12},{9,13},{1... | collective-permute-start | bytes 1572872 | tf_op jit(solution)/shard_map/ppermute | solution.py:38
  94.1 16.3 %collective-permute-start.27 = (bf16[1024,256]{1,0:T(8,128)(2,1)S(1)}, bf16[1024,256]{1,0:T(8,128)(2,1)}, u32[]{:S(2)}, u32[]{:S(2)}) collective-permute-start(bf16[1024,256]{1,0:T(8,128)(2,1)S(1)} %get-tuple-element.109), channel_id=1, source_target_pairs={{0,12},{1,13},{2,14},{3,15},{4,0},{5,1},{6,2},{7,3},{8,4},{9,5},{1... | collective-permute-start | bytes 1572872 | tf_op jit(solution)/shard_map/ppermute | solution.py:38
  96.7 16.7 %collective-permute-start.28 = (bf16[1024,256]{1,0:T(8,128)(2,1)S(1)}, bf16[1024,256]{1,0:T(8,128)(2,1)}, u32[]{:S(2)}, u32[]{:S(2)}) collective-permute-start(bf16[1024,256]{1,0:T(8,128)(2,1)S(1)} %get-tuple-element.110), channel_id=1, source_target_pairs={{0,8},{1,9},{2,10},{3,11},{4,12},{5,13},{6,14},{7,15},{8,0},{9,1},... | collective-permute-start | bytes 1572872 | tf_op jit(solution)/shard_map/ppermute | solution.py:38
  97.8 25.5 %collective-permute-start.29 = (bf16[1024,256]{1,0:T(8,128)(2,1)}, bf16[1024,256]{1,0:T(8,128)(2,1)S(1)}, u32[]{:S(2)}, u32[]{:S(2)}) collective-permute-start(bf16[1024,256]{1,0:T(8,128)(2,1)} %fusion.2), channel_id=1, source_target_pairs={{0,2},{1,3},{2,0},{3,1},{4,6},{5,7},{6,4},{7,5},{8,10},{9,11},{10,... | collective-permute-start | bytes 1572872 | tf_op jit(solution)/shard_map/ppermute | solution.py:38
  105.8 9.2 %collective-permute-start.30 = (bf16[128,512]{1,0:T(8,128)(2,1)S(1)}, bf16[128,512]{1,0:T(8,128)(2,1)S(1)}, u32[]{:S(2)}, u32[]{:S(2)}) collective-permute-start(bf16[128,512]{1,0:T(8,128)(2,1)S(1)} %pad_maximum_fusion.5), channel_id=1, source_target_pairs={{0,192},{16,208},{32,224},{48,240},{64,0},{80,16},{96,32},{112,48}... | collective-permute-start | bytes 393224 | tf_op jit(solution)/shard_map/ppermute | solution.py:42
  107.8 7.2 %collective-permute-start.31 = (bf16[128,512]{1,0:T(8,128)(2,1)S(1)}, bf16[128,512]{1,0:T(8,128)(2,1)S(1)}, u32[]{:S(2)}, u32[]{:S(2)}) collective-permute-start(bf16[128,512]{1,0:T(8,128)(2,1)S(1)} %pad_maximum_fusion.5), channel_id=1, source_target_pairs={{0,128},{16,144},{32,160},{48,176},{64,192},{80,208},{96,224},{112... | collective-permute-start | bytes 393224 | tf_op jit(solution)/shard_map/ppermute | solution.py:42
  110.3 5.4 %collective-permute-start.32 = (bf16[128,512]{1,0:T(8,128)(2,1)S(1)}, bf16[128,512]{1,0:T(8,128)(2,1)S(1)}, u32[]{:S(2)}, u32[]{:S(2)}) collective-permute-start(bf16[128,512]{1,0:T(8,128)(2,1)S(1)} %pad_maximum_fusion.5), channel_id=1, source_target_pairs={{0,64},{16,80},{32,96},{48,112},{64,128},{80,144},{96,160},{112,17... | collective-permute-start | bytes 393224 | tf_op jit(solution)/shard_map/ppermute | solution.py:42
  115.8 7.6 %copy-start.3 = (bf16[128,512]{1,0:T(8,128)(2,1)}, bf16[128,512]{1,0:T(8,128)(2,1)S(1)}, u32[]{:S(2)}) copy-start(bf16[128,512]{1,0:T(8,128)(2,1)S(1)} %collective-permute-done.32) | copy-start | bytes 393220
  123.3 10.1 %copy-start.1 = (f32[2,512,512]{2,1,0:T(8,128)S(1)}, f32[2,512,512]{2,1,0:T(8,128)}, u32[]{:S(2)}) copy-start(f32[2,512,512]{2,1,0:T(8,128)} %param.11) | copy-start | bytes 6291460
  124.2 11.3 %collective-permute-start.33 = (f32[512,256]{1,0:T(8,128)}, f32[512,256]{1,0:T(8,128)S(1)}, u32[]{:S(2)}, u32[]{:S(2)}) collective-permute-start(f32[512,256]{1,0:T(8,128)} %get-tuple-element.136), channel_id=1, source_target_pairs={{0,1},{1,0},{2,3},{3,2},{4,5},{5,4},{6,7},{7,6},{8,9},{9,8},{10,11... | collective-permute-start | bytes 1572872 | tf_op jit(solution)/shard_map/ppermute | solution.py:38
  132.3 1.7 %copy-start.2 = (f32[2,512,512]{2,1,0:T(8,128)S(1)}, f32[2,512,512]{2,1,0:T(8,128)}, u32[]{:S(2)}) copy-start(f32[2,512,512]{2,1,0:T(8,128)} %param.12) | copy-start | bytes 6291460

commit v2 on v1

--- a/solution.py
+++ b/solution.py
@@ -63,23 +63,20 @@
     return (inverse_rms * (incoming - normed * along)).astype(BF16)
 
 
-def forward_kernel(at_ref, own_ref, sib_ref, *refs):
+def forward_kernel(at_ref, acts_ref, *refs):
     weights, (out_ref, held, acts, sems) = refs[:4], refs[4:]
-    tokens = own_ref.shape[0]
     depth = held.shape[2]
 
-    def copy(i, t):
+    def copy(i):
         start = pl.multiple_of(at_ref[i] * depth, depth)
-        kept = (acts if i < 4 else held).at[i % 4, pl.ds(t * tokens, tokens), :]
-        return pltpu.make_async_copy((own_ref, sib_ref)[t].at[:, pl.ds(start, depth)], kept, sems.at[i, t])
+        kept = (acts if i < 4 else held).at[i % 4]
+        return pltpu.make_async_copy(acts_ref.at[:, pl.ds(start, depth)], kept, sems.at[i])
 
     for i in range(8):
-        for t in range(2):
-            copy(i, t).start()
-    for i in range(4):
-        for t in range(2):
-            copy(i, t).wait()
-        for n in range(0, 2 * tokens, TILE):
+        copy(i).start()
+    for i in range(4):
+        copy(i).wait()
+        for n in range(0, out_ref.shape[0], TILE):
             where = pl.ds(n, TILE)
             term = jnp.dot(acts[i, where, :], weights[i][...], preferred_element_type=F32)
             if i == 0:
@@ -87,83 +84,83 @@
             else:
                 out_ref[where, :] += term
     for i in range(4, 8):
-        for t in range(2):
-            copy(i, t).wait()
-
-
-def forward_call(at, own, sib, weights):
-    tokens = own.shape[0]
+        copy(i).wait()
+
+
+def forward_call(at, acts, weights):
+    tokens = acts.shape[0]
     depth, cols = weights[0].shape
     vmem = pl.BlockSpec(memory_space=pltpu.VMEM)
     hbm = pl.BlockSpec(memory_space=pltpu.HBM)
     return pl.pallas_call(
         forward_kernel,
-        in_specs=[pl.BlockSpec(memory_space=pltpu.SMEM), hbm, hbm] + [vmem] * 4,
+        in_specs=[pl.BlockSpec(memory_space=pltpu.SMEM), hbm] + [vmem] * 4,
         out_specs=[vmem, vmem],
         out_shape=[
-            jax.ShapeDtypeStruct((2 * tokens, cols), F32),
-            jax.ShapeDtypeStruct((4, 2 * tokens, depth), BF16),
+            jax.ShapeDtypeStruct((tokens, cols), F32),
+            jax.ShapeDtypeStruct((4, tokens, depth), BF16),
         ],
-        scratch_shapes=[pltpu.VMEM((4, 2 * tokens, depth), BF16), pltpu.SemaphoreType.DMA((8, 2))],
+        scratch_shapes=[pltpu.VMEM((4, tokens, depth), BF16), pltpu.SemaphoreType.DMA((8,))],
         compiler_params=PARAMS,
-        cost_estimate=pl.CostEstimate(
-            flops=16 * tokens * depth * cols, bytes_accessed=0, transcendentals=0
-        ),
+        cost_estimate=pl.CostEstimate(flops=8 * tokens * depth * cols, bytes_accessed=0, transcendentals=0),
         name="own_forward",
-    )(at, own, sib, *weights)
-
-
-def middle_kernel(held, part_ref, cot_ref, *refs):
-    weights, (back_ref, *outs), acc = refs[:8], refs[8:16], refs[16]
-    tokens = held.shape[1] // 2
-    depth = held.shape[2]
-    for i in range(4):
-        for n in range(0, 2 * tokens, TILE):
-            where = pl.ds(n, TILE)
-            term = sum(
-                jnp.dot(held[i, where, pl.ds(h * depth // 2, depth // 2)], weights[2 * i + h][...], preferred_element_type=F32)
-                for h in range(2)
-            )
-            if i == 0:
-                acc[where, :] = part_ref[where, :] + term
-            else:
-                acc[where, :] += term
-
+    )(at, acts, *weights)
+
+
+def middle_kernel(*refs):
+    held, parts, cot_ref, weights = refs[:2], refs[2:4], refs[4], refs[5:13]
+    back_ref, outs, acc = refs[13], refs[14:21], refs[21]
+    tokens, depth = held[0].shape[1:]
+    half = depth // 2
+    for i in range(4):
+        for t in range(2):
+            for n in range(0, tokens, TILE):
+                where, near = pl.ds(t * tokens + n, TILE), pl.ds(n, TILE)
+                term = sum(
+                    jnp.dot(
+                        held[t][i, near, pl.ds(h * half, half)],
+                        weights[2 * i + h][...],
+                        preferred_element_type=F32,
+                    )
+                    for h in range(2)
+                )
+                if i == 0:
+                    acc[where, :] = parts[t][near, :] + term
+                else:
+                    acc[where, :] += term
     for n in range(0, 2 * tokens, TILE):
         where = pl.ds(n, TILE)
         for h in range(0, acc.shape[1], HEAD_DIM):
             head = pl.ds(h, HEAD_DIM)
             back_ref[where, head] = backprop(acc[where, head], cot_ref[where, head])
-
     for i in range(4):
         for n in range(0, depth, TILE):
-            term = rows_dot(held[i, :, pl.ds(n, TILE)], back_ref[...])
+            term = rows_dot(held[0][i, :, pl.ds(n, TILE)], back_ref[:tokens, :])
+            term += rows_dot(held[1][i, :, pl.ds(n, TILE)], back_ref[tokens:, :])
             if i == 3:
                 outs[6][pl.ds(n, TILE), :] = term
             else:
-                out_ref = outs[2 * i + n // (depth // 2)]
-                out_ref[pl.ds(n % (depth // 2), TILE), :] = term.astype(out_ref.dtype)
-
-
-def middle_call(held, part, cot, weights):
-    tokens, depth = held.shape[1] // 2, held.shape[2]
+                out_ref = outs[2 * i + n // half]
+                out_ref[pl.ds(n % half, TILE), :] = term.astype(out_ref.dtype)
+
+
+def middle_call(held, parts, cot, weights):
+    tokens, depth = held[0].shape[1:]
     cols = weights[0].shape[1]
     halves = (BF16, BF16, F32, BF16, BF16, F32)
     vmem = pl.BlockSpec(memory_space=pltpu.VMEM)
     return pl.pallas_call(
         middle_kernel,
-        in_specs=[vmem] * 11,
+        in_specs=[vmem] * 13,
         out_specs=[vmem] * 8,
         out_shape=[jax.ShapeDtypeStruct((2 * tokens, cols), BF16)]
         + [jax.ShapeDtypeStruct((depth // 2, cols), t) for t in halves]
         + [jax.ShapeDtypeStruct((depth, cols), F32)],
         scratch_shapes=[pltpu.VMEM((2 * tokens, cols), F32)],
         compiler_params=PARAMS,
-        cost_estimate=pl.CostEstimate(
-            flops=32 * tokens * depth * cols, bytes_accessed=0, transcendentals=0
-        ),
+        cost_estimate=pl.CostEstimate(flops=32 * tokens * depth * cols, bytes_accessed=0, transcendentals=0),
         name="middle",
-    )(held, part, cot, *weights)
+    )(*held, *parts, cot, *weights)
 
 
 def gradient_kernel(at_ref, own_ref, sib_ref, back_ref, *refs):
@@ -282,16 +279,20 @@
     gathered = [far, right, left, here]
     top, bottom = away[:rows], away[rows:]
     from_left, from_right = send(top, dx=1), send(bottom, dx=-1)
+    from_left, *blocks = tie(from_left, *blocks)
     far = [send(from_left, dx=1), send(from_right, dx=-1)]
     distant = [*far, send(top, dx=-1), from_right, from_left, send(bottom, dx=1), top, bottom]
     hidden_sib = send(hidden, dc=1)
-    blocks = rep_parts(blocks)
     at = lambda dz: jnp.stack([chip_of(dx, dz) for dx in ORDER]).astype(jnp.int32)
     both = jnp.concatenate([at(0), at(1)])
-    partial, held = forward_call(both, hidden, hidden_sib, gathered)
-    partial, held, *rest = tie(partial, held, *distant, *blocks)
+    part_own, held_own = forward_call(both, hidden, gathered)
+    part_own, hidden_sib = tie(part_own, hidden_sib)
+    part_sib, held_sib = forward_call(both, hidden_sib, gathered)
+    parts, held = [part_own, part_sib], [held_own, held_sib]
+    rest = tie(*parts, *held, *distant, *rep_parts(blocks))
+    parts, held, rest = rest[:2], rest[2:4], rest[4:]
     distant, blocks = rest[:8], rest[8:]
-    back, *found = middle_call(held, partial, cots, distant)
+    back, *found = middle_call(held, parts, cots, distant)
 
     def gather(found):
         return [send(found[0], dx=2), send(found[1], dx=1), send(found[2], dx=-1), found[3]]

time: 137 us -> 133 us (0.971)
  waiting for transfers between devices: 30.1 us -> 26.5 us
  Pallas kernels: 16.6 us -> 18.9 us
  local copies, waits for them, and re-layouts: 9.75 us -> 7.61 us
    pallas_call x1 -> x2, Pallas kernels: 4.75 us -> 7.63 us  [forward_call(): pl.pallas_call(forward_kernel, in_specs=[pl.BlockSpec(memory_space=pltpu....]
    ppermute x23, waiting for transfers between devices: 26.4 us -> 24.3 us  [send(): return lax.ppermute(value, 'fsdp', fsdp_perm(**kw))]
    sub x1, other arithmetic: 1.64 us -> 3.22 us  [per_device(): new_global = old_params - 0.7 * (average + 0.9 * new_momentum)]
    ppermute x23, starting transfers between devices: 47.1 us -> 48.5 us  [send(): return lax.ppermute(value, 'fsdp', fsdp_perm(**kw))]
    unnamed x16 -> x8, local copies, waits for them, and re-layouts: 3.87 us -> 3.4 us
  transfers between devices with their start and end apart: 34 -> 34, of which waited for: 11 -> 9; matrix products, arithmetic and copies ran while one was open for 9% -> 7% of each run, Pallas kernels for 7% -> 10%
where the time goes in v2:
time: 133 us
  starting transfers between devices  69.1 us (52%)
  waiting for transfers between devices  26.5 us (20%)
  Pallas kernels  18.9 us (14%)
  other arithmetic  8.83 us (7%)
  local copies, waits for them, and re-layouts  7.61 us (6%)
  between operations  1.76 us (1%)
    ppermute x23, starting transfers between devices, send(): return lax.ppermute(value, 'fsdp', fsdp_perm(**kw))  48.5 us
    ppermute x23, waiting for transfers between devices, send(): return lax.ppermute(value, 'fsdp', fsdp_perm(**kw))  24.3 us
    ppermute x9, starting transfers between devices, rep_send(): return lax.ppermute(value, 'rep', rep_perm(**kw))  17.8 us
    pallas_call x2, Pallas kernels, forward_call(): pl.pallas_call(forward_kernel, in_specs=[pl.BlockSpec(memory_space=pltpu....  7.63 us
    pallas_call x1, Pallas kernels, middle_call(): pl.pallas_call(middle_kernel, in_specs=[vmem] * 13, out_specs=[vmem] * 8,...  6.21 us
    pallas_call x1, Pallas kernels, gradient_call(): pl.pallas_call(gradient_kernel, in_specs=[pl.BlockSpec(memory_space=pltpu...  5.11 us
    unnamed x8, local copies, waits for them, and re-layouts  3.4 us
    sub x1, other arithmetic, per_device(): new_global = old_params - 0.7 * (average + 0.9 * new_momentum)  3.22 us
  transfers between devices with their start and end apart: 34, of which 9 were waited for; matrix products, arithmetic and copies ran while one was open for 7% of the time, Pallas kernels for 10%

profile of v2, /device:TPU:1, one launch (start us, length us, event | category | flops | bytes accessed | tf_op | source)
XLA Modules:
  0.0 132.8 jit_solution(6137284041402601503)
XLA Ops:
  0.7 1.1 dynamic-slice_bitcast_fusion.1
  1.7 1.1 constant_dynamic-slice_fusion.5
  2.8 3.3 %collective-permute-start = (bf16[1024,256]{1,0:T(8,128)(2,1)S(1)}, bf16[1024,256]{1,0:T(8,128)(2,1)S(1)}, u32[]{:S(2)}, u32[]{:S(2)}) collective-permute-start(bf16[1024,256]{1,0:T(8,128)(2,1)S(1)} %pad_maximum_fusion), channel_id=1, source_target_pairs={{0,1},{1,0},{2,3},{3,2},{4,5},{5,4},{6,7},{7,6},{8,9},{9,8},{10,11... | collective-permute-start | bytes 1572872 | tf_op jit(solution)/shard_map/ppermute | solution.py:38
  6.2 1.1 fusion.3
  7.3 0.1 collective-permute-start.5
  7.4 0.3 collective-permute-done
  7.7 0.2 maximum_select_fusion.1.refs_3_
  8.0 2.0 %collective-permute-start.1 = (bf16[1024,256]{1,0:T(8,128)(2,1)S(1)}, bf16[1024,256]{1,0:T(8,128)(2,1)S(1)}, u32[]{:S(2)}, u32[]{:S(2)}) collective-permute-start(bf16[1024,256]{1,0:T(8,128)(2,1)S(1)} %maximum_select_fusion.1.refs_3_), channel_id=1, source_target_pairs={{0,8},{1,9},{2,10},{3,11},{4,12},{5,13},{6,14},{7,15},{8,0},{9,1},... | collective-permute-start | bytes 1572872 | tf_op jit(solution)/shard_map/ppermute | solution.py:38
  10.0 0.9 collective-permute-start.2
  10.9 0.6 collective-permute-start.3
  11.5 6.9 %collective-permute-start.4 = (bf16[1024,256]{1,0:T(8,128)(2,1)S(1)}, bf16[1024,256]{1,0:T(8,128)(2,1)S(1)}, u32[]{:S(2)}, u32[]{:S(2)}) collective-permute-start(bf16[1024,256]{1,0:T(8,128)(2,1)S(1)} %maximum_select_fusion.1.refs_3_), channel_id=1, source_target_pairs={{0,2},{1,3},{2,0},{3,1},{4,6},{5,7},{6,4},{7,5},{8,10},{9,11},{10,... | collective-permute-start | bytes 1572872 | tf_op jit(solution)/shard_map/ppermute | solution.py:38
  18.4 1.1 bitcast_add_fusion
  19.5 2.7 %collective-permute-start.6 = (bf16[128,512]{1,0:T(8,128)(2,1)S(1)}, bf16[128,512]{1,0:T(8,128)(2,1)S(1)}, u32[]{:S(2)}, u32[]{:S(2)}) collective-permute-start(bf16[128,512]{1,0:T(8,128)(2,1)S(1)} %dynamic-slice_convert_fusion.1), channel_id=1, source_target_pairs={{0,128},{16,144},{32,160},{48,176},{64,192},{80,208},{96,224},{112... | collective-permute-start | bytes 393224 | tf_op jit(solution)/shard_map/ppermute | solution.py:219
  22.2 0.7 constant_dynamic-slice_fusion.4
  23.0 2.2 %collective-permute-done.6 = bf16[128,512]{1,0:T(8,128)(2,1)S(1)} collective-permute-done((bf16[128,512]{1,0:T(8,128)(2,1)S(1)}, bf16[128,512]{1,0:T(8,128)(2,1)S(1)}, u32[]{:S(2)}, u32[]{:S(2)}) %collective-permute-start.6) | collective-permute-done | bytes 131104 | tf_op jit(solution)/shard_map/ppermute | solution.py:219
  25.2 0.0 collective-permute-done.1.refs_0_
  25.2 8.1 %collective-permute-done.2.refs_1_ = bf16[1024,256]{1,0:T(8,128)(2,1)S(1)} collective-permute-done((bf16[1024,256]{1,0:T(8,128)(2,1)S(1)}, bf16[1024,256]{1,0:T(8,128)(2,1)S(1)}, u32[]{:S(2)}, u32[]{:S(2)}) %collective-permute-start.2) | collective-permute-done | bytes 524320 | tf_op jit(solution)/shard_map/ppermute | solution.py:38
  33.3 1.3 %collective-permute-done.3.refs_2_ = bf16[1024,256]{1,0:T(8,128)(2,1)S(1)} collective-permute-done((bf16[1024,256]{1,0:T(8,128)(2,1)S(1)}, bf16[1024,256]{1,0:T(8,128)(2,1)S(1)}, u32[]{:S(2)}, u32[]{:S(2)}) %collective-permute-start.3) | collective-permute-done | bytes 524320 | tf_op jit(solution)/shard_map/ppermute | solution.py:38
  34.7 0.5 collective-permute-start.7
  35.2 0.6 collective-permute-start.8
  35.7 2.2 %collective-permute-start.10 = (bf16[512,256]{1,0:T(8,128)(2,1)S(1)}, bf16[512,256]{1,0:T(8,128)(2,1)}, u32[]{:S(2)}, u32[]{:S(2)}) collective-permute-start(bf16[512,256]{1,0:T(8,128)(2,1)S(1)} %get-tuple-element.103.refs_12_), channel_id=1, source_target_pairs={{0,12},{1,13},{2,14},{3,15},{4,0},{5,1},{6,2},{7,3},{8,4},{9,5},{1... | collective-permute-start | bytes 786440 | tf_op jit(solution)/shard_map/ppermute | solution.py:38
  37.9 0.1 concatenate.48.at_ref
  38.0 0.5 collective-permute-start.12
  38.5 1.0 collective-permute-start.13
  39.5 3.4 %copy-done = bf16[512,8192]{1,0:T(8,128)(2,1)S(1)} copy-done((bf16[512,8192]{1,0:T(8,128)(2,1)S(1)}, bf16[512,8192]{1,0:T(8,128)(2,1)}, u32[]{:S(2)}) %copy-start) | copy-done | bytes 8388632
  42.9 3.6 %own_forward.2 = (f32[512,256]{1,0:T(8,128)S(1)}, bf16[4,512,1024]{2,1,0:T(8,128)(2,1)S(1)}) custom-call(s32[8]{0:T(128)S(1)} %concatenate.48.at_ref, bf16[512,8192]{1,0:T(8,128)(2,1)S(1)} %copy-done, bf16[1024,256]{1,0:T(8,128)(2,1)S(1)} %collective-permute-done.1.refs_0_, bf16[1024,256]{1,0:T(8,128)(2,1)S(1)} %collective-permute-done.2.refs_1_, ...), custom_call_target="tpu_custom_call" | custom-call | flops 1073741824 | tf_op jit(solution)/shard_map/own_forward/pallas_call | solution.py:95
  46.5 0.1 collective-permute-start.9
  46.6 2.7 %collective-permute-start.11 = (bf16[512,256]{1,0:T(8,128)(2,1)}, bf16[512,256]{1,0:T(8,128)(2,1)S(1)}, u32[]{:S(2)}, u32[]{:S(2)}) collective-permute-start(bf16[512,256]{1,0:T(8,128)(2,1)} %collective-permute-done.10.refs_8_), channel_id=1, source_target_pairs={{0,12},{1,13},{2,14},{3,15},{4,0},{5,1},{6,2},{7,3},{8,4},{9,5},{1... | collective-permute-start | bytes 786440 | tf_op jit(solution)/shard_map/ppermute | solution.py:38
  49.3 8.5 %collective-permute-start.14 = (f32[32,512]{1,0:T(8,128)S(1)}, f32[32,512]{1,0:T(8,128)S(1)}, u32[]{:S(2)}, u32[]{:S(2)}) collective-permute-start(f32[32,512]{1,0:T(8,128)S(1)} %get-tuple-element.165), channel_id=1, source_target_pairs={{0,16},{16,32},{32,48},{48,0},{64,80},{80,96},{96,112},{112,64},{1... | collective-permute-start | bytes 196616 | tf_op jit(solution)/shard_map/ppermute | solution.py:42
  57.8 0.0 collective-permute-done.12.refs_7_
  57.8 0.8 collective-permute-start.15
  58.7 0.0 collective-permute-done.13.refs_10_
  58.7 2.3 %collective-permute-start.16 = (f32[32,512]{1,0:T(8,128)S(1)}, f32[32,512]{1,0:T(8,128)S(1)}, u32[]{:S(2)}, u32[]{:S(2)}) collective-permute-start(f32[32,512]{1,0:T(8,128)S(1)} %get-tuple-element.163), channel_id=1, source_target_pairs={{0,48},{16,0},{32,16},{48,32},{64,112},{80,64},{96,80},{112,96},{1... | collective-permute-start | bytes 196616 | tf_op jit(solution)/shard_map/ppermute | solution.py:42
  60.9 4.0 %own_forward.3 = (f32[512,256]{1,0:T(8,128)S(1)}, bf16[4,512,1024]{2,1,0:T(8,128)(2,1)S(1)}) custom-call(s32[8]{0:T(128)S(1)} %concatenate.48.at_ref, bf16[512,8192]{1,0:T(8,128)(2,1)} %collective-permute-done.7.acts_ref.sib_ref, bf16[1024,256]{1,0:T(8,128)(2,1)S(1)} %collective-permute-done.1.refs_0_, bf16[1024,256]{1,0:T(8,128)(2,1)S(1)} %collective-permute-done.2.refs_1_, ...), custom_call_target="tpu_custom_call" | custom-call | flops 1073741824 | tf_op jit(solution)/shard_map/own_forward/pallas_call | solution.py:95
  65.0 0.0 collective-permute-done.14
  65.0 0.0 slice-start
  65.1 6.2 %middle.1 = (bf16[1024,256]{1,0:T(8,128)(2,1)S(1)}, bf16[512,256]{1,0:T(8,128)(2,1)S(1)}, bf16[512,256]{1,0:T(8,128)(2,1)S(1)}, f32[512,256]{1,0:T(8,128)S(1)}, ...) custom-call(bf16[4,512,1024]{2,1,0:T(8,128)(2,1)S(1)} %get-tuple-ele, ...), custom_call_target="tpu_custom_call" | custom-call | flops 4294967296 | tf_op jit(solution)/shard_map/middle/pallas_call | solution.py:152
  71.3 1.8 %collective-permute-start.19 = (bf16[512,256]{1,0:T(8,128)(2,1)S(1)}, bf16[512,256]{1,0:T(8,128)(2,1)S(1)}, u32[]{:S(2)}, u32[]{:S(2)}) collective-permute-start(bf16[512,256]{1,0:T(8,128)(2,1)S(1)} %get-tuple-element.107), channel_id=1, source_target_pairs={{0,12},{1,13},{2,14},{3,15},{4,0},{5,1},{6,2},{7,3},{8,4},{9,5},{1... | collective-permute-start | bytes 786440 | tf_op jit(solution)/shard_map/ppermute | solution.py:38
  73.1 1.4 %collective-permute-start.23 = (bf16[32,512]{1,0:T(8,128)(2,1)S(1)}, bf16[32,512]{1,0:T(8,128)(2,1)S(1)}, u32[]{:S(2)}, u32[]{:S(2)}) collective-permute-start(bf16[32,512]{1,0:T(8,128)(2,1)S(1)} %multiply_convert_fusion), channel_id=1, source_target_pairs={{0,48},{16,0},{32,16},{48,32},{64,112},{80,64},{96,80},{112,96},{1... | collective-permute-start | bytes 98312 | tf_op jit(solution)/shard_map/ppermute | solution.py:42
  74.6 2.5 %collective-permute-done.19 = bf16[512,256]{1,0:T(8,128)(2,1)S(1)} collective-permute-done((bf16[512,256]{1,0:T(8,128)(2,1)S(1)}, bf16[512,256]{1,0:T(8,128)(2,1)S(1)}, u32[]{:S(2)}, u32[]{:S(2)}) %collective-permute-start.19) | collective-permute-done | bytes 262176 | tf_op jit(solution)/shard_map/ppermute | solution.py:38
  77.1 3.4 %collective-permute-start.22 = (bf16[512,256]{1,0:T(8,128)(2,1)S(1)}, bf16[512,256]{1,0:T(8,128)(2,1)S(1)}, u32[]{:S(2)}, u32[]{:S(2)}) collective-permute-start(bf16[512,256]{1,0:T(8,128)(2,1)S(1)} %get-tuple-element.109), channel_id=1, source_target_pairs={{0,12},{1,13},{2,14},{3,15},{4,0},{5,1},{6,2},{7,3},{8,4},{9,5},{1... | collective-permute-start | bytes 786440 | tf_op jit(solution)/shard_map/ppermute | solution.py:38
  80.5 0.1 add_convert_fusion
  80.5 0.1 collective-permute-start.20
  80.6 0.1 add_convert_fusion.1
  80.7 1.7 %collective-permute-start.18 = (bf16[512,256]{1,0:T(8,128)(2,1)S(1)}, bf16[512,256]{1,0:T(8,128)(2,1)S(1)}, u32[]{:S(2)}, u32[]{:S(2)}) collective-permute-start(bf16[512,256]{1,0:T(8,128)(2,1)S(1)} %add_convert_fusion.1), channel_id=1, source_target_pairs={{0,4},{1,5},{2,6},{3,7},{4,8},{5,9},{6,10},{7,11},{8,12},{9,13},{1... | collective-permute-start | bytes 786440 | tf_op jit(solution)/shard_map/ppermute | solution.py:38
  82.4 0.1 pad_add_fusion.at_ref
  82.5 0.1 collective-permute-start.25
  82.7 5.1 %gradient.1 = (bf16[1024,256]{1,0:T(8,128)(2,1)S(1)}, bf16[1024,256]{1,0:T(8,128)(2,1)S(1)}, bf16[1024,256]{1,0:T(8,128)(2,1)S(1)}, f32[1024,256]{1,0:T(8,128)S(1)}) custom-call(s32[4]{0:T(128)S(1)} %pad_add_fusion.at_ref, bf16[512,8192]{1,0:T(8,128)(2,1)S(1)} %bitcast.53, bf16[512,8192]{1,0:T(8,128)(2,1)} %collective-permute-done.7.acts_ref.sib_ref, ...), custom_call_target="tpu_custom_call" | custom-call | flops 2147483648 | tf_op jit(solution)/shard_map/gradient/pallas_call | solution.py:192
  87.8 1.3 collective-permute-done.20
  89.1 2.3 %collective-permute-done.18 = bf16[512,256]{1,0:T(8,128)(2,1)S(1)} collective-permute-done((bf16[512,256]{1,0:T(8,128)(2,1)S(1)}, bf16[512,256]{1,0:T(8,128)(2,1)S(1)}, u32[]{:S(2)}, u32[]{:S(2)}) %collective-permute-start.18) | collective-permute-done | bytes 262176 | tf_op jit(solution)/shard_map/ppermute | solution.py:38
  91.4 2.7 %collective-permute-start.27 = (bf16[1024,256]{1,0:T(8,128)(2,1)S(1)}, bf16[1024,256]{1,0:T(8,128)(2,1)}, u32[]{:S(2)}, u32[]{:S(2)}) collective-permute-start(bf16[1024,256]{1,0:T(8,128)(2,1)S(1)} %get-tuple-element.127), channel_id=1, source_target_pairs={{0,12},{1,13},{2,14},{3,15},{4,0},{5,1},{6,2},{7,3},{8,4},{9,5},{1... | collective-permute-start | bytes 1572872 | tf_op jit(solution)/shard_map/ppermute | solution.py:38
  94.1 0.1 convert_add_fusion.3
  94.2 0.9 fusion.2
  95.1 5.2 %collective-permute-start.29 = (bf16[1024,256]{1,0:T(8,128)(2,1)}, bf16[1024,256]{1,0:T(8,128)(2,1)S(1)}, u32[]{:S(2)}, u32[]{:S(2)}) collective-permute-start(bf16[1024,256]{1,0:T(8,128)(2,1)} %fusion.2), channel_id=1, source_target_pairs={{0,2},{1,3},{2,0},{3,1},{4,6},{5,7},{6,4},{7,5},{8,10},{9,11},{10,... | collective-permute-start | bytes 1572872 | tf_op jit(solution)/shard_map/ppermute | solution.py:38
  100.5 2.0 %collective-permute-start.30 = (bf16[128,512]{1,0:T(8,128)(2,1)S(1)}, bf16[128,512]{1,0:T(8,128)(2,1)S(1)}, u32[]{:S(2)}, u32[]{:S(2)}) collective-permute-start(bf16[128,512]{1,0:T(8,128)(2,1)S(1)} %pad_maximum_fusion.5), channel_id=1, source_target_pairs={{0,192},{16,208},{32,224},{48,240},{64,0},{80,16},{96,32},{112,48}... | collective-permute-start | bytes 393224 | tf_op jit(solution)/shard_map/ppermute | solution.py:42
  102.4 1.9 %collective-permute-done.26 = bf16[1024,256]{1,0:T(8,128)(2,1)} collective-permute-done((bf16[1024,256]{1,0:T(8,128)(2,1)S(1)}, bf16[1024,256]{1,0:T(8,128)(2,1)}, u32[]{:S(2)}, u32[]{:S(2)}) %collective-permute-start.26) | collective-permute-done | bytes 524320 | tf_op jit(solution)/shard_map/ppermute | solution.py:38
  104.3 2.6 %collective-permute-start.31 = (bf16[128,512]{1,0:T(8,128)(2,1)S(1)}, bf16[128,512]{1,0:T(8,128)(2,1)S(1)}, u32[]{:S(2)}, u32[]{:S(2)}) collective-permute-start(bf16[128,512]{1,0:T(8,128)(2,1)S(1)} %pad_maximum_fusion.5), channel_id=1, source_target_pairs={{0,128},{16,144},{32,160},{48,176},{64,192},{80,208},{96,224},{112... | collective-permute-start | bytes 393224 | tf_op jit(solution)/shard_map/ppermute | solution.py:42
  107.0 6.6 %collective-permute-done.28 = bf16[1024,256]{1,0:T(8,128)(2,1)} collective-permute-done((bf16[1024,256]{1,0:T(8,128)(2,1)S(1)}, bf16[1024,256]{1,0:T(8,128)(2,1)}, u32[]{:S(2)}, u32[]{:S(2)}) %collective-permute-start.28) | collective-permute-done | bytes 524320 | tf_op jit(solution)/shard_map/ppermute | solution.py:38
  113.5 1.6 %convert_add_fusion.5 = (f32[512,256]{1,0:T(8,128)S(1)}, f32[512,256]{1,0:T(8,128)S(1)}) fusion(f32[1024,256]{1,0:T(8,128)S(1)} %get-tuple-element.125, s32[]{:T(128)S(6)} %select_n.250, bf16[1024,256]{1,0:T(8,128)(2,1)} %collective-permute-done.28, bf16[1024,256]{1,0:T(8,128)(2,1)} %collective-permute-done.27, ...), kind=kLoop, calls=%fused_computation.17 | loop fusion | flops 1572864 | bytes 3670024 | tf_op jit(solution)/shard_map/add | solution.py:302
  115.1 0.1 add_bitcast_fusion
  115.2 12.4 %collective-permute-start.33 = (f32[512,256]{1,0:T(8,128)S(1)}, f32[512,256]{1,0:T(8,128)S(1)}, u32[]{:S(2)}, u32[]{:S(2)}) collective-permute-start(f32[512,256]{1,0:T(8,128)S(1)} %get-tuple-element.154), channel_id=1, source_target_pairs={{0,1},{1,0},{2,3},{3,2},{4,5},{5,4},{6,7},{7,6},{8,9},{9,8},{10,11... | collective-permute-start | bytes 1572872 | tf_op jit(solution)/shard_map/ppermute | solution.py:38
  128.3 0.1 pad_maximum_fusion.2
  128.4 3.2 %fusion.1 = (f32[512,512]{1,0:T(8,128)}, f32[512,512]{1,0:T(8,128)}) fusion(f32[2,512,512]{2,1,0:T(8,128)} %param.11, s32[]{:T(128)S(6)} %select_n.261, bf16[128,512]{1,0:T(8,128)(2,1)S(1)} %get-tuple-element.150, bf16[128,512]{1,0:T(8,128)(2,1)S(1)} %get-tuple-element.151, bf16[128,512]{1,0:T(8,128)(2,1)S(1)} %get-tuple-element.152, ...), kind=kLoop, calls=%fused_computation.3 | loop fusion | flops 3670016 | bytes 4718596 | tf_op jit(solution)/shard_map/sub | solution.py:325
  131.6 1.1 maximum_select_fusion
  (46 shorter events, 0.4 us)
Async XLA Ops:
  2.8 4.9 %collective-permute-start = (bf16[1024,256]{1,0:T(8,128)(2,1)S(1)}, bf16[1024,256]{1,0:T(8,128)(2,1)S(1)}, u32[]{:S(2)}, u32[]{:S(2)}) collective-permute-start(bf16[1024,256]{1,0:T(8,128)(2,1)S(1)} %pad_maximum_fusion), channel_id=1, source_target_pairs={{0,1},{1,0},{2,3},{3,2},{4,5},{5,4},{6,7},{7,6},{8,9},{9,8},{10,11... | collective-permute-start | bytes 1572872 | tf_op jit(solution)/shard_map/ppermute | solution.py:38
  7.3 11.1 %collective-permute-start.5 = (bf16[256,512]{1,0:T(8,128)(2,1)S(1)}, bf16[256,512]{1,0:T(8,128)(2,1)S(1)}, u32[]{:S(2)}, u32[]{:S(2)}) collective-permute-start(bf16[256,512]{1,0:T(8,128)(2,1)S(1)} %fusion.3), channel_id=1, source_target_pairs={{0,64},{16,80},{32,96},{48,112},{64,0},{80,16},{96,32},{112,48},{1... | collective-permute-start | bytes 786440 | tf_op jit(solution)/shard_map/ppermute | solution.py:219
  8.0 17.3 %collective-permute-start.1 = (bf16[1024,256]{1,0:T(8,128)(2,1)S(1)}, bf16[1024,256]{1,0:T(8,128)(2,1)S(1)}, u32[]{:S(2)}, u32[]{:S(2)}) collective-permute-start(bf16[1024,256]{1,0:T(8,128)(2,1)S(1)} %maximum_select_fusion.1.refs_3_), channel_id=1, source_target_pairs={{0,8},{1,9},{2,10},{3,11},{4,12},{5,13},{6,14},{7,15},{8,0},{9,1},... | collective-permute-start | bytes 1572872 | tf_op jit(solution)/shard_map/ppermute | solution.py:38
  10.0 23.3 %collective-permute-start.2 = (bf16[1024,256]{1,0:T(8,128)(2,1)S(1)}, bf16[1024,256]{1,0:T(8,128)(2,1)S(1)}, u32[]{:S(2)}, u32[]{:S(2)}) collective-permute-start(bf16[1024,256]{1,0:T(8,128)(2,1)S(1)} %maximum_select_fusion.1.refs_3_), channel_id=1, source_target_pairs={{0,12},{1,13},{2,14},{3,15},{4,0},{5,1},{6,2},{7,3},{8,4},{9,5},{1... | collective-permute-start | bytes 1572872 | tf_op jit(solution)/shard_map/ppermute | solution.py:38
  10.9 23.8 %collective-permute-start.3 = (bf16[1024,256]{1,0:T(8,128)(2,1)S(1)}, bf16[1024,256]{1,0:T(8,128)(2,1)S(1)}, u32[]{:S(2)}, u32[]{:S(2)}) collective-permute-start(bf16[1024,256]{1,0:T(8,128)(2,1)S(1)} %maximum_select_fusion.1.refs_3_), channel_id=1, source_target_pairs={{0,4},{1,5},{2,6},{3,7},{4,8},{5,9},{6,10},{7,11},{8,12},{9,13},{1... | collective-permute-start | bytes 1572872 | tf_op jit(solution)/shard_map/ppermute | solution.py:38
  11.5 23.2 %collective-permute-start.4 = (bf16[1024,256]{1,0:T(8,128)(2,1)S(1)}, bf16[1024,256]{1,0:T(8,128)(2,1)S(1)}, u32[]{:S(2)}, u32[]{:S(2)}) collective-permute-start(bf16[1024,256]{1,0:T(8,128)(2,1)S(1)} %maximum_select_fusion.1.refs_3_), channel_id=1, source_target_pairs={{0,2},{1,3},{2,0},{3,1},{4,6},{5,7},{6,4},{7,5},{8,10},{9,11},{10,... | collective-permute-start | bytes 1572872 | tf_op jit(solution)/shard_map/ppermute | solution.py:38
  19.5 5.7 %collective-permute-start.6 = (bf16[128,512]{1,0:T(8,128)(2,1)S(1)}, bf16[128,512]{1,0:T(8,128)(2,1)S(1)}, u32[]{:S(2)}, u32[]{:S(2)}) collective-permute-start(bf16[128,512]{1,0:T(8,128)(2,1)S(1)} %dynamic-slice_convert_fusion.1), channel_id=1, source_target_pairs={{0,128},{16,144},{32,160},{48,176},{64,192},{80,208},{96,224},{112... | collective-permute-start | bytes 393224 | tf_op jit(solution)/shard_map/ppermute | solution.py:219
  34.7 14.7 %collective-permute-start.7 = (bf16[512,8192]{1,0:T(8,128)(2,1)}, bf16[512,8192]{1,0:T(8,128)(2,1)}, u32[]{:S(2)}, u32[]{:S(2)}) collective-permute-start(bf16[512,8192]{1,0:T(8,128)(2,1)} %own_ref), channel_id=1, source_target_pairs={{0,1},{1,0},{2,3},{3,2},{4,5},{5,4},{6,7},{7,6},{8,9},{9,8},{10,11... | collective-permute-start | bytes 25165832 | tf_op jit(solution)/shard_map/ppermute | solution.py:38
  35.2 11.3 %collective-permute-start.8 = (bf16[512,256]{1,0:T(8,128)(2,1)S(1)}, bf16[512,256]{1,0:T(8,128)(2,1)S(1)}, u32[]{:S(2)}, u32[]{:S(2)}) collective-permute-start(bf16[512,256]{1,0:T(8,128)(2,1)S(1)} %get-tuple-element.102.refs_11_), channel_id=1, source_target_pairs={{0,4},{1,5},{2,6},{3,7},{4,8},{5,9},{6,10},{7,11},{8,12},{9,13},{1... | collective-permute-start | bytes 786440 | tf_op jit(solution)/shard_map/ppermute | solution.py:38
  35.7 10.8 %collective-permute-start.10 = (bf16[512,256]{1,0:T(8,128)(2,1)S(1)}, bf16[512,256]{1,0:T(8,128)(2,1)}, u32[]{:S(2)}, u32[]{:S(2)}) collective-permute-start(bf16[512,256]{1,0:T(8,128)(2,1)S(1)} %get-tuple-element.103.refs_12_), channel_id=1, source_target_pairs={{0,12},{1,13},{2,14},{3,15},{4,0},{5,1},{6,2},{7,3},{8,4},{9,5},{1... | collective-permute-start | bytes 786440 | tf_op jit(solution)/shard_map/ppermute | solution.py:38
  38.0 19.8 %collective-permute-start.12 = (bf16[512,256]{1,0:T(8,128)(2,1)S(1)}, bf16[512,256]{1,0:T(8,128)(2,1)S(1)}, u32[]{:S(2)}, u32[]{:S(2)}) collective-permute-start(bf16[512,256]{1,0:T(8,128)(2,1)S(1)} %get-tuple-element.102.refs_11_), channel_id=1, source_target_pairs={{0,12},{1,13},{2,14},{3,15},{4,0},{5,1},{6,2},{7,3},{8,4},{9,5},{1... | collective-permute-start | bytes 786440 | tf_op jit(solution)/shard_map/ppermute | solution.py:38
  38.5 20.2 %collective-permute-start.13 = (bf16[512,256]{1,0:T(8,128)(2,1)S(1)}, bf16[512,256]{1,0:T(8,128)(2,1)S(1)}, u32[]{:S(2)}, u32[]{:S(2)}) collective-permute-start(bf16[512,256]{1,0:T(8,128)(2,1)S(1)} %get-tuple-element.103.refs_12_), channel_id=1, source_target_pairs={{0,4},{1,5},{2,6},{3,7},{4,8},{5,9},{6,10},{7,11},{8,12},{9,13},{1... | collective-permute-start | bytes 786440 | tf_op jit(solution)/shard_map/ppermute | solution.py:38
  39.5 3.4 %copy-start = (bf16[512,8192]{1,0:T(8,128)(2,1)S(1)}, bf16[512,8192]{1,0:T(8,128)(2,1)}, u32[]{:S(2)}) copy-start(bf16[512,8192]{1,0:T(8,128)(2,1)} %own_ref) | copy-start | bytes 25165828
  42.9 6.4 %copy-start.1 = (f32[128,512]{1,0:T(8,128)S(1)}, f32[128,512]{1,0:T(8,128)}, u32[]{:S(2)}) copy-start(f32[128,512]{1,0:T(8,128)} %constant_dynamic-slice_fusion.4) | copy-start | bytes 786436
  46.5 18.5 %collective-permute-start.9 = (bf16[512,256]{1,0:T(8,128)(2,1)S(1)}, bf16[512,256]{1,0:T(8,128)(2,1)S(1)}, u32[]{:S(2)}, u32[]{:S(2)}) collective-permute-start(bf16[512,256]{1,0:T(8,128)(2,1)S(1)} %collective-permute-done.8.refs_9_), channel_id=1, source_target_pairs={{0,4},{1,5},{2,6},{3,7},{4,8},{5,9},{6,10},{7,11},{8,12},{9,13},{1... | collective-permute-start | bytes 786440 | tf_op jit(solution)/shard_map/ppermute | solution.py:38
  46.6 18.4 %collective-permute-start.11 = (bf16[512,256]{1,0:T(8,128)(2,1)}, bf16[512,256]{1,0:T(8,128)(2,1)S(1)}, u32[]{:S(2)}, u32[]{:S(2)}) collective-permute-start(bf16[512,256]{1,0:T(8,128)(2,1)} %collective-permute-done.10.refs_8_), channel_id=1, source_target_pairs={{0,12},{1,13},{2,14},{3,15},{4,0},{5,1},{6,2},{7,3},{8,4},{9,5},{1... | collective-permute-start | bytes 786440 | tf_op jit(solution)/shard_map/ppermute | solution.py:38
  49.3 15.6 %collective-permute-start.14 = (f32[32,512]{1,0:T(8,128)S(1)}, f32[32,512]{1,0:T(8,128)S(1)}, u32[]{:S(2)}, u32[]{:S(2)}) collective-permute-start(f32[32,512]{1,0:T(8,128)S(1)} %get-tuple-element.165), channel_id=1, source_target_pairs={{0,16},{16,32},{32,48},{48,0},{64,80},{80,96},{96,112},{112,64},{1... | collective-permute-start | bytes 196616 | tf_op jit(solution)/shard_map/ppermute | solution.py:42
  57.8 7.2 %collective-permute-start.15 = (f32[32,512]{1,0:T(8,128)S(1)}, f32[32,512]{1,0:T(8,128)S(1)}, u32[]{:S(2)}, u32[]{:S(2)}) collective-permute-start(f32[32,512]{1,0:T(8,128)S(1)} %get-tuple-element.164), channel_id=1, source_target_pairs={{0,32},{16,48},{32,0},{48,16},{64,96},{80,112},{96,64},{112,80},{1... | collective-permute-start | bytes 196616 | tf_op jit(solution)/shard_map/ppermute | solution.py:42
  58.7 6.3 %collective-permute-start.16 = (f32[32,512]{1,0:T(8,128)S(1)}, f32[32,512]{1,0:T(8,128)S(1)}, u32[]{:S(2)}, u32[]{:S(2)}) collective-permute-start(f32[32,512]{1,0:T(8,128)S(1)} %get-tuple-element.163), channel_id=1, source_target_pairs={{0,48},{16,0},{32,16},{48,32},{64,112},{80,64},{96,80},{112,96},{1... | collective-permute-start | bytes 196616 | tf_op jit(solution)/shard_map/ppermute | solution.py:42
  65.0 17.6 %slice-start = ((s8[8388608]{0:T(1024)(128)(4,1)}), s8[4194304]{0:T(1024)(128)(4,1)S(1)}, s32[]{:S(2)}) async-start(s8[8388608]{0:T(1024)(128)(4,1)} %bitcast.52), calls=%async_computation | async-start | bytes 8388608
  65.1 17.6 %slice-start.1 = ((s8[8388608]{0:T(1024)(128)(4,1)}), s8[4194304]{0:T(1024)(128)(4,1)S(1)}, s32[]{:S(2)}) async-start(s8[8388608]{0:T(1024)(128)(4,1)} %bitcast.52), calls=%async_computation.1 | async-start | bytes 8388608
  71.3 5.8 %collective-permute-start.19 = (bf16[512,256]{1,0:T(8,128)(2,1)S(1)}, bf16[512,256]{1,0:T(8,128)(2,1)S(1)}, u32[]{:S(2)}, u32[]{:S(2)}) collective-permute-start(bf16[512,256]{1,0:T(8,128)(2,1)S(1)} %get-tuple-element.107), channel_id=1, source_target_pairs={{0,12},{1,13},{2,14},{3,15},{4,0},{5,1},{6,2},{7,3},{8,4},{9,5},{1... | collective-permute-start | bytes 786440 | tf_op jit(solution)/shard_map/ppermute | solution.py:38
  73.1 7.4 %collective-permute-start.17 = (bf16[512,256]{1,0:T(8,128)(2,1)S(1)}, bf16[512,256]{1,0:T(8,128)(2,1)S(1)}, u32[]{:S(2)}, u32[]{:S(2)}) collective-permute-start(bf16[512,256]{1,0:T(8,128)(2,1)S(1)} %get-tuple-element.105), channel_id=1, source_target_pairs={{0,4},{1,5},{2,6},{3,7},{4,8},{5,9},{6,10},{7,11},{8,12},{9,13},{1... | collective-permute-start | bytes 786440 | tf_op jit(solution)/shard_map/ppermute | solution.py:38
  73.1 7.5 %collective-permute-start.23 = (bf16[32,512]{1,0:T(8,128)(2,1)S(1)}, bf16[32,512]{1,0:T(8,128)(2,1)S(1)}, u32[]{:S(2)}, u32[]{:S(2)}) collective-permute-start(bf16[32,512]{1,0:T(8,128)(2,1)S(1)} %multiply_convert_fusion), channel_id=1, source_target_pairs={{0,48},{16,0},{32,16},{48,32},{64,112},{80,64},{96,80},{112,96},{1... | collective-permute-start | bytes 98312 | tf_op jit(solution)/shard_map/ppermute | solution.py:42
  74.6 7.9 %collective-permute-start.24 = (bf16[32,512]{1,0:T(8,128)(2,1)S(1)}, bf16[32,512]{1,0:T(8,128)(2,1)S(1)}, u32[]{:S(2)}, u32[]{:S(2)}) collective-permute-start(bf16[32,512]{1,0:T(8,128)(2,1)S(1)} %multiply_convert_fusion), channel_id=1, source_target_pairs={{0,32},{16,48},{32,0},{48,16},{64,96},{80,112},{96,64},{112,80},{1... | collective-permute-start | bytes 98312 | tf_op jit(solution)/shard_map/ppermute | solution.py:42
  74.6 13.2 %collective-permute-start.21 = (bf16[512,256]{1,0:T(8,128)(2,1)S(1)}, bf16[512,256]{1,0:T(8,128)(2,1)S(1)}, u32[]{:S(2)}, u32[]{:S(2)}) collective-permute-start(bf16[512,256]{1,0:T(8,128)(2,1)S(1)} %get-tuple-element.108), channel_id=1, source_target_pairs={{0,4},{1,5},{2,6},{3,7},{4,8},{5,9},{6,10},{7,11},{8,12},{9,13},{1... | collective-permute-start | bytes 786440 | tf_op jit(solution)/shard_map/ppermute | solution.py:38
  77.1 10.8 %collective-permute-start.22 = (bf16[512,256]{1,0:T(8,128)(2,1)S(1)}, bf16[512,256]{1,0:T(8,128)(2,1)S(1)}, u32[]{:S(2)}, u32[]{:S(2)}) collective-permute-start(bf16[512,256]{1,0:T(8,128)(2,1)S(1)} %get-tuple-element.109), channel_id=1, source_target_pairs={{0,12},{1,13},{2,14},{3,15},{4,0},{5,1},{6,2},{7,3},{8,4},{9,5},{1... | collective-permute-start | bytes 786440 | tf_op jit(solution)/shard_map/ppermute | solution.py:38
  80.5 8.6 %collective-permute-start.20 = (bf16[512,256]{1,0:T(8,128)(2,1)S(1)}, bf16[512,256]{1,0:T(8,128)(2,1)S(1)}, u32[]{:S(2)}, u32[]{:S(2)}) collective-permute-start(bf16[512,256]{1,0:T(8,128)(2,1)S(1)} %add_convert_fusion), channel_id=1, source_target_pairs={{0,12},{1,13},{2,14},{3,15},{4,0},{5,1},{6,2},{7,3},{8,4},{9,5},{1... | collective-permute-start | bytes 786440 | tf_op jit(solution)/shard_map/ppermute | solution.py:38
  80.7 10.7 %collective-permute-start.18 = (bf16[512,256]{1,0:T(8,128)(2,1)S(1)}, bf16[512,256]{1,0:T(8,128)(2,1)S(1)}, u32[]{:S(2)}, u32[]{:S(2)}) collective-permute-start(bf16[512,256]{1,0:T(8,128)(2,1)S(1)} %add_convert_fusion.1), channel_id=1, source_target_pairs={{0,4},{1,5},{2,6},{3,7},{4,8},{5,9},{6,10},{7,11},{8,12},{9,13},{1... | collective-permute-start | bytes 786440 | tf_op jit(solution)/shard_map/ppermute | solution.py:38
  82.5 5.3 %collective-permute-start.25 = (bf16[32,512]{1,0:T(8,128)(2,1)S(1)}, bf16[32,512]{1,0:T(8,128)(2,1)S(1)}, u32[]{:S(2)}, u32[]{:S(2)}) collective-permute-start(bf16[32,512]{1,0:T(8,128)(2,1)S(1)} %multiply_convert_fusion), channel_id=1, source_target_pairs={{0,16},{16,32},{32,48},{48,0},{64,80},{80,96},{96,112},{112,64},{1... | collective-permute-start | bytes 98312 | tf_op jit(solution)/shard_map/ppermute | solution.py:42
  91.4 12.9 %collective-permute-start.26 = (bf16[1024,256]{1,0:T(8,128)(2,1)S(1)}, bf16[1024,256]{1,0:T(8,128)(2,1)}, u32[]{:S(2)}, u32[]{:S(2)}) collective-permute-start(bf16[1024,256]{1,0:T(8,128)(2,1)S(1)} %get-tuple-element.126), channel_id=1, source_target_pairs={{0,4},{1,5},{2,6},{3,7},{4,8},{5,9},{6,10},{7,11},{8,12},{9,13},{1... | collective-permute-start | bytes 1572872 | tf_op jit(solution)/shard_map/ppermute | solution.py:38
  91.4 15.5 %collective-permute-start.27 = (bf16[1024,256]{1,0:T(8,128)(2,1)S(1)}, bf16[1024,256]{1,0:T(8,128)(2,1)}, u32[]{:S(2)}, u32[]{:S(2)}) collective-permute-start(bf16[1024,256]{1,0:T(8,128)(2,1)S(1)} %get-tuple-element.127), channel_id=1, source_target_pairs={{0,12},{1,13},{2,14},{3,15},{4,0},{5,1},{6,2},{7,3},{8,4},{9,5},{1... | collective-permute-start | bytes 1572872 | tf_op jit(solution)/shard_map/ppermute | solution.py:38
  94.1 19.4 %collective-permute-start.28 = (bf16[1024,256]{1,0:T(8,128)(2,1)S(1)}, bf16[1024,256]{1,0:T(8,128)(2,1)}, u32[]{:S(2)}, u32[]{:S(2)}) collective-permute-start(bf16[1024,256]{1,0:T(8,128)(2,1)S(1)} %get-tuple-element.128), channel_id=1, source_target_pairs={{0,8},{1,9},{2,10},{3,11},{4,12},{5,13},{6,14},{7,15},{8,0},{9,1},... | collective-permute-start | bytes 1572872 | tf_op jit(solution)/shard_map/ppermute | solution.py:38
  95.1 20.0 %collective-permute-start.29 = (bf16[1024,256]{1,0:T(8,128)(2,1)}, bf16[1024,256]{1,0:T(8,128)(2,1)S(1)}, u32[]{:S(2)}, u32[]{:S(2)}) collective-permute-start(bf16[1024,256]{1,0:T(8,128)(2,1)} %fusion.2), channel_id=1, source_target_pairs={{0,2},{1,3},{2,0},{3,1},{4,6},{5,7},{6,4},{7,5},{8,10},{9,11},{10,... | collective-permute-start | bytes 1572872 | tf_op jit(solution)/shard_map/ppermute | solution.py:38
  100.5 14.6 %collective-permute-start.30 = (bf16[128,512]{1,0:T(8,128)(2,1)S(1)}, bf16[128,512]{1,0:T(8,128)(2,1)S(1)}, u32[]{:S(2)}, u32[]{:S(2)}) collective-permute-start(bf16[128,512]{1,0:T(8,128)(2,1)S(1)} %pad_maximum_fusion.5), channel_id=1, source_target_pairs={{0,192},{16,208},{32,224},{48,240},{64,0},{80,16},{96,32},{112,48}... | collective-permute-start | bytes 393224 | tf_op jit(solution)/shard_map/ppermute | solution.py:42
  104.3 10.8 %collective-permute-start.31 = (bf16[128,512]{1,0:T(8,128)(2,1)S(1)}, bf16[128,512]{1,0:T(8,128)(2,1)S(1)}, u32[]{:S(2)}, u32[]{:S(2)}) collective-permute-start(bf16[128,512]{1,0:T(8,128)(2,1)S(1)} %pad_maximum_fusion.5), channel_id=1, source_target_pairs={{0,128},{16,144},{32,160},{48,176},{64,192},{80,208},{96,224},{112... | collective-permute-start | bytes 393224 | tf_op jit(solution)/shard_map/ppermute | solution.py:42
  106.9 8.2 %collective-permute-start.32 = (bf16[128,512]{1,0:T(8,128)(2,1)S(1)}, bf16[128,512]{1,0:T(8,128)(2,1)S(1)}, u32[]{:S(2)}, u32[]{:S(2)}) collective-permute-start(bf16[128,512]{1,0:T(8,128)(2,1)S(1)} %pad_maximum_fusion.5), channel_id=1, source_target_pairs={{0,64},{16,80},{32,96},{48,112},{64,128},{80,144},{96,160},{112,17... | collective-permute-start | bytes 393224 | tf_op jit(solution)/shard_map/ppermute | solution.py:42
  115.2 16.4 %collective-permute-start.33 = (f32[512,256]{1,0:T(8,128)S(1)}, f32[512,256]{1,0:T(8,128)S(1)}, u32[]{:S(2)}, u32[]{:S(2)}) collective-permute-start(f32[512,256]{1,0:T(8,128)S(1)} %get-tuple-element.154), channel_id=1, source_target_pairs={{0,1},{1,0},{2,3},{3,2},{4,5},{5,4},{6,7},{7,6},{8,9},{9,8},{10,11... | collective-permute-start | bytes 1572872 | tf_op jit(solution)/shard_map/ppermute | solution.py:38

commit v3 on v2

--- a/solution.py
+++ b/solution.py
@@ -264,9 +264,9 @@
     def in_order(own, other):
         return jnp.where(core == 0, jnp.concatenate([own, other]), jnp.concatenate([other, own]))
 
-    from_sib = send(jnp.concatenate([theirs(weight), theirs(key_cotangent)]), dc=1)
-    cots = jnp.concatenate([mine(key_cotangent), from_sib[rows:]])
-    here = in_order(mine(weight), from_sib[:rows])
+    here = in_order(mine(weight), send(theirs(weight), dc=1))
+    here, given = tie(here, theirs(key_cotangent))
+    cots = jnp.concatenate([mine(key_cotangent), send(given, dc=1)])
 
     def spread(piece):
         return {0: piece, 3: send(piece, dx=1), 1: send(piece, dx=-1), 2: send(piece, dx=2)}

time: 133 us -> 134 us (level)
  starting transfers between devices: 69.1 us -> 71.1 us
    ppermute x23 -> x24, starting transfers between devices: 48.5 us -> 50.4 us  [send(): return lax.ppermute(value, 'fsdp', fsdp_perm(**kw))]
    ppermute x23 -> x24, waiting for transfers between devices: 24.3 us -> 22.7 us  [send(): return lax.ppermute(value, 'fsdp', fsdp_perm(**kw))]
    unnamed x8 -> x10, local copies, waits for them, and re-layouts: 3.4 us -> 3.4 us
  transfers between devices with their start and end apart: 34 -> 35, of which waited for: 9 -> 9; matrix products, arithmetic and copies ran while one was open for 7% -> 8% of each run, Pallas kernels for 10% -> 10%
where the time goes in v3:
time: 134 us; the launch traced here: 133 us
  starting transfers between devices  71.1 us (53%)
  waiting for transfers between devices  25.5 us (19%)
  Pallas kernels  18.9 us (14%)
  local copies, waits for them, and re-layouts  8.36 us (6%)
  other arithmetic  7.75 us (6%)
  between operations  1.69 us (1%)
    ppermute x24, starting transfers between devices, send(): return lax.ppermute(value, 'fsdp', fsdp_perm(**kw))  50.4 us
    ppermute x24, waiting for transfers between devices, send(): return lax.ppermute(value, 'fsdp', fsdp_perm(**kw))  22.7 us
    ppermute x9, starting transfers between devices, rep_send(): return lax.ppermute(value, 'rep', rep_perm(**kw))  18.1 us
    pallas_call x2, Pallas kernels, forward_call(): pl.pallas_call(forward_kernel, in_specs=[pl.BlockSpec(memory_space=pltpu....  7.63 us
    pallas_call x1, Pallas kernels, middle_call(): pl.pallas_call(middle_kernel, in_specs=[vmem] * 13, out_specs=[vmem] * 8,...  6.21 us
    pallas_call x1, Pallas kernels, gradient_call(): pl.pallas_call(gradient_kernel, in_specs=[pl.BlockSpec(memory_space=pltpu...  5.11 us
    unnamed x10, local copies, waits for them, and re-layouts  3.4 us
    sub x1, other arithmetic, per_device(): new_global = old_params - 0.7 * (average + 0.9 * new_momentum)  3.22 us
  transfers between devices with their start and end apart: 35, of which 9 were waited for; matrix products, arithmetic and copies ran while one was open for 8% of the time, Pallas kernels for 10%

profile of v3, /device:TPU:1, one launch (start us, length us, event | category | flops | bytes accessed | tf_op | source)
XLA Modules:
  0.0 133.4 jit_solution(6962252948142888155)
XLA Ops:
  0.6 0.0 copy-start.2
  0.7 1.2 dynamic-slice_bitcast_fusion.1
  1.8 3.3 %collective-permute-start = (bf16[512,256]{1,0:T(8,128)(2,1)S(1)}, bf16[512,256]{1,0:T(8,128)(2,1)S(1)}, u32[]{:S(2)}, u32[]{:S(2)}) collective-permute-start(bf16[512,256]{1,0:T(8,128)(2,1)S(1)} %get-tuple-element.164), channel_id=1, source_target_pairs={{0,1},{1,0},{2,3},{3,2},{4,5},{5,4},{6,7},{7,6},{8,9},{9,8},{10,11... | collective-permute-start | bytes 786440 | tf_op jit(solution)/shard_map/ppermute | solution.py:38
  5.1 1.8 %fusion.3 = bf16[256,512]{1,0:T(8,128)(2,1)} fusion(f32[1,512,512]{2,1,0:T(8,128)} %param.10, s32[]{:T(128)S(6)} %select_n.236), kind=kLoop, calls=%fused_computation.21 | loop fusion | bytes 524292 | tf_op jit(solution)/shard_map/convert_element_type | solution.py:212
  6.9 0.0 collective-permute-start.6
  6.9 1.1 constant_dynamic-slice_fusion.5
  8.0 0.0 collective-permute-done
  8.0 0.2 maximum_select_fusion.1.refs_3_
  8.2 2.4 %collective-permute-start.1 = (bf16[1024,256]{1,0:T(8,128)(2,1)S(1)}, bf16[1024,256]{1,0:T(8,128)(2,1)S(1)}, u32[]{:S(2)}, u32[]{:S(2)}) collective-permute-start(bf16[1024,256]{1,0:T(8,128)(2,1)S(1)} %maximum_select_fusion.1.refs_3_), channel_id=1, source_target_pairs={{0,8},{1,9},{2,10},{3,11},{4,12},{5,13},{6,14},{7,15},{8,0},{9,1},... | collective-permute-start | bytes 1572872 | tf_op jit(solution)/shard_map/ppermute | solution.py:38
  10.6 0.9 collective-permute-start.2
  11.5 0.6 collective-permute-start.3
  12.1 6.9 %collective-permute-start.4 = (bf16[1024,256]{1,0:T(8,128)(2,1)S(1)}, bf16[1024,256]{1,0:T(8,128)(2,1)S(1)}, u32[]{:S(2)}, u32[]{:S(2)}) collective-permute-start(bf16[1024,256]{1,0:T(8,128)(2,1)S(1)} %maximum_select_fusion.1.refs_3_), channel_id=1, source_target_pairs={{0,2},{1,3},{2,0},{3,1},{4,6},{5,7},{6,4},{7,5},{8,10},{9,11},{10,... | collective-permute-start | bytes 1572872 | tf_op jit(solution)/shard_map/ppermute | solution.py:38
  19.0 0.0 collective-permute-done.6
  19.0 1.5 %collective-permute-start.5 = (bf16[512,256]{1,0:T(8,128)(2,1)S(1)}, bf16[512,256]{1,0:T(8,128)(2,1)S(1)}, u32[]{:S(2)}, u32[]{:S(2)}) collective-permute-start(bf16[512,256]{1,0:T(8,128)(2,1)S(1)} %get-tuple-element.77), channel_id=1, source_target_pairs={{0,1},{1,0},{2,3},{3,2},{4,5},{5,4},{6,7},{7,6},{8,9},{9,8},{10,11... | collective-permute-start | bytes 786440 | tf_op jit(solution)/shard_map/ppermute | solution.py:38
  20.5 0.1 bitcast_add_fusion
  20.6 1.0 collective-permute-done.5
  21.6 2.6 %collective-permute-start.7 = (bf16[128,512]{1,0:T(8,128)(2,1)S(1)}, bf16[128,512]{1,0:T(8,128)(2,1)S(1)}, u32[]{:S(2)}, u32[]{:S(2)}) collective-permute-start(bf16[128,512]{1,0:T(8,128)(2,1)S(1)} %dynamic-slice_convert_fusion.1), channel_id=1, source_target_pairs={{0,128},{16,144},{32,160},{48,176},{64,192},{80,208},{96,224},{112... | collective-permute-start | bytes 393224 | tf_op jit(solution)/shard_map/ppermute | solution.py:219
  24.3 0.7 constant_dynamic-slice_fusion.4
  25.0 2.8 %collective-permute-done.7 = bf16[128,512]{1,0:T(8,128)(2,1)S(1)} collective-permute-done((bf16[128,512]{1,0:T(8,128)(2,1)S(1)}, bf16[128,512]{1,0:T(8,128)(2,1)S(1)}, u32[]{:S(2)}, u32[]{:S(2)}) %collective-permute-start.7) | collective-permute-done | bytes 131104 | tf_op jit(solution)/shard_map/ppermute | solution.py:219
  27.9 6.1 %collective-permute-done.2.refs_1_ = bf16[1024,256]{1,0:T(8,128)(2,1)S(1)} collective-permute-done((bf16[1024,256]{1,0:T(8,128)(2,1)S(1)}, bf16[1024,256]{1,0:T(8,128)(2,1)S(1)}, u32[]{:S(2)}, u32[]{:S(2)}) %collective-permute-start.2) | collective-permute-done | bytes 524320 | tf_op jit(solution)/shard_map/ppermute | solution.py:38
  33.9 1.0 collective-permute-done.3.refs_2_
  34.9 0.5 collective-permute-start.8
  35.4 0.9 collective-permute-start.9
  36.4 1.8 %collective-permute-start.11 = (bf16[512,256]{1,0:T(8,128)(2,1)S(1)}, bf16[512,256]{1,0:T(8,128)(2,1)}, u32[]{:S(2)}, u32[]{:S(2)}) collective-permute-start(bf16[512,256]{1,0:T(8,128)(2,1)S(1)} %get-tuple-element.107.refs_12_), channel_id=1, source_target_pairs={{0,12},{1,13},{2,14},{3,15},{4,0},{5,1},{6,2},{7,3},{8,4},{9,5},{1... | collective-permute-start | bytes 786440 | tf_op jit(solution)/shard_map/ppermute | solution.py:38
  38.2 0.1 concatenate.45.at_ref
  38.3 0.8 collective-permute-start.13
  39.1 0.6 collective-permute-start.14
  39.8 3.4 %copy-done = bf16[512,8192]{1,0:T(8,128)(2,1)S(1)} copy-done((bf16[512,8192]{1,0:T(8,128)(2,1)S(1)}, bf16[512,8192]{1,0:T(8,128)(2,1)}, u32[]{:S(2)}) %copy-start) | copy-done | bytes 8388632
  43.2 3.6 %own_forward.2 = (f32[512,256]{1,0:T(8,128)S(1)}, bf16[4,512,1024]{2,1,0:T(8,128)(2,1)S(1)}) custom-call(s32[8]{0:T(128)S(1)} %concatenate.45.at_ref, bf16[512,8192]{1,0:T(8,128)(2,1)S(1)} %copy-done, bf16[1024,256]{1,0:T(8,128)(2,1)S(1)} %collective-permute-done.1.refs_0_, bf16[1024,256]{1,0:T(8,128)(2,1)S(1)} %collective-permute-done.2.refs_1_, ...), custom_call_target="tpu_custom_call" | custom-call | flops 1073741824 | tf_op jit(solution)/shard_map/own_forward/pallas_call | solution.py:95
  46.8 0.1 collective-permute-start.10
  46.9 2.7 %collective-permute-start.12 = (bf16[512,256]{1,0:T(8,128)(2,1)}, bf16[512,256]{1,0:T(8,128)(2,1)S(1)}, u32[]{:S(2)}, u32[]{:S(2)}) collective-permute-start(bf16[512,256]{1,0:T(8,128)(2,1)} %collective-permute-done.11.refs_8_), channel_id=1, source_target_pairs={{0,12},{1,13},{2,14},{3,15},{4,0},{5,1},{6,2},{7,3},{8,4},{9,5},{1... | collective-permute-start | bytes 786440 | tf_op jit(solution)/shard_map/ppermute | solution.py:38
  49.6 8.8 %collective-permute-start.15 = (f32[32,512]{1,0:T(8,128)S(1)}, f32[32,512]{1,0:T(8,128)S(1)}, u32[]{:S(2)}, u32[]{:S(2)}) collective-permute-start(f32[32,512]{1,0:T(8,128)S(1)} %get-tuple-element.167), channel_id=1, source_target_pairs={{0,16},{16,32},{32,48},{48,0},{64,80},{80,96},{96,112},{112,64},{1... | collective-permute-start | bytes 196616 | tf_op jit(solution)/shard_map/ppermute | solution.py:42
  58.4 0.8 collective-permute-start.16
  59.3 2.3 %collective-permute-start.17 = (f32[32,512]{1,0:T(8,128)S(1)}, f32[32,512]{1,0:T(8,128)S(1)}, u32[]{:S(2)}, u32[]{:S(2)}) collective-permute-start(f32[32,512]{1,0:T(8,128)S(1)} %get-tuple-element.165), channel_id=1, source_target_pairs={{0,48},{16,0},{32,16},{48,32},{64,112},{80,64},{96,80},{112,96},{1... | collective-permute-start | bytes 196616 | tf_op jit(solution)/shard_map/ppermute | solution.py:42
  61.6 4.0 %own_forward.3 = (f32[512,256]{1,0:T(8,128)S(1)}, bf16[4,512,1024]{2,1,0:T(8,128)(2,1)S(1)}) custom-call(s32[8]{0:T(128)S(1)} %concatenate.45.at_ref, bf16[512,8192]{1,0:T(8,128)(2,1)} %collective-permute-done.8.acts_ref.sib_ref, bf16[1024,256]{1,0:T(8,128)(2,1)S(1)} %collective-permute-done.1.refs_0_, bf16[1024,256]{1,0:T(8,128)(2,1)S(1)} %collective-permute-done.2.refs_1_, ...), custom_call_target="tpu_custom_call" | custom-call | flops 1073741824 | tf_op jit(solution)/shard_map/own_forward/pallas_call | solution.py:95
  65.7 0.0 slice-start
  65.7 6.2 %middle.1 = (bf16[1024,256]{1,0:T(8,128)(2,1)S(1)}, bf16[512,256]{1,0:T(8,128)(2,1)S(1)}, bf16[512,256]{1,0:T(8,128)(2,1)S(1)}, f32[512,256]{1,0:T(8,128)S(1)}, ...) custom-call(bf16[4,512,1024]{2,1,0:T(8,128)(2,1)S(1)} %get-tuple-ele, ...), custom_call_target="tpu_custom_call" | custom-call | flops 4294967296 | tf_op jit(solution)/shard_map/middle/pallas_call | solution.py:152
  71.9 1.8 %collective-permute-start.20 = (bf16[512,256]{1,0:T(8,128)(2,1)S(1)}, bf16[512,256]{1,0:T(8,128)(2,1)S(1)}, u32[]{:S(2)}, u32[]{:S(2)}) collective-permute-start(bf16[512,256]{1,0:T(8,128)(2,1)S(1)} %get-tuple-element.111), channel_id=1, source_target_pairs={{0,12},{1,13},{2,14},{3,15},{4,0},{5,1},{6,2},{7,3},{8,4},{9,5},{1... | collective-permute-start | bytes 786440 | tf_op jit(solution)/shard_map/ppermute | solution.py:38
  73.8 1.4 %collective-permute-start.24 = (bf16[32,512]{1,0:T(8,128)(2,1)S(1)}, bf16[32,512]{1,0:T(8,128)(2,1)S(1)}, u32[]{:S(2)}, u32[]{:S(2)}) collective-permute-start(bf16[32,512]{1,0:T(8,128)(2,1)S(1)} %multiply_convert_fusion), channel_id=1, source_target_pairs={{0,48},{16,0},{32,16},{48,32},{64,112},{80,64},{96,80},{112,96},{1... | collective-permute-start | bytes 98312 | tf_op jit(solution)/shard_map/ppermute | solution.py:42
  75.2 2.5 %collective-permute-done.20 = bf16[512,256]{1,0:T(8,128)(2,1)S(1)} collective-permute-done((bf16[512,256]{1,0:T(8,128)(2,1)S(1)}, bf16[512,256]{1,0:T(8,128)(2,1)S(1)}, u32[]{:S(2)}, u32[]{:S(2)}) %collective-permute-start.20) | collective-permute-done | bytes 262176 | tf_op jit(solution)/shard_map/ppermute | solution.py:38
  77.7 3.4 %collective-permute-start.23 = (bf16[512,256]{1,0:T(8,128)(2,1)S(1)}, bf16[512,256]{1,0:T(8,128)(2,1)S(1)}, u32[]{:S(2)}, u32[]{:S(2)}) collective-permute-start(bf16[512,256]{1,0:T(8,128)(2,1)S(1)} %get-tuple-element.113), channel_id=1, source_target_pairs={{0,12},{1,13},{2,14},{3,15},{4,0},{5,1},{6,2},{7,3},{8,4},{9,5},{1... | collective-permute-start | bytes 786440 | tf_op jit(solution)/shard_map/ppermute | solution.py:38
  81.1 0.1 add_convert_fusion
  81.2 0.3 collective-permute-start.21
  81.5 0.1 add_convert_fusion.1
  81.5 1.5 %collective-permute-start.19 = (bf16[512,256]{1,0:T(8,128)(2,1)S(1)}, bf16[512,256]{1,0:T(8,128)(2,1)S(1)}, u32[]{:S(2)}, u32[]{:S(2)}) collective-permute-start(bf16[512,256]{1,0:T(8,128)(2,1)S(1)} %add_convert_fusion.1), channel_id=1, source_target_pairs={{0,4},{1,5},{2,6},{3,7},{4,8},{5,9},{6,10},{7,11},{8,12},{9,13},{1... | collective-permute-start | bytes 786440 | tf_op jit(solution)/shard_map/ppermute | solution.py:38
  83.1 0.1 pad_add_fusion.at_ref
  83.1 0.1 collective-permute-start.26
  83.3 5.1 %gradient.1 = (bf16[1024,256]{1,0:T(8,128)(2,1)S(1)}, bf16[1024,256]{1,0:T(8,128)(2,1)S(1)}, bf16[1024,256]{1,0:T(8,128)(2,1)S(1)}, f32[1024,256]{1,0:T(8,128)S(1)}) custom-call(s32[4]{0:T(128)S(1)} %pad_add_fusion.at_ref, bf16[512,8192]{1,0:T(8,128)(2,1)S(1)} %bitcast.53, bf16[512,8192]{1,0:T(8,128)(2,1)} %collective-permute-done.8.acts_ref.sib_ref, ...), custom_call_target="tpu_custom_call" | custom-call | flops 2147483648 | tf_op jit(solution)/shard_map/gradient/pallas_call | solution.py:192
  88.4 1.3 %collective-permute-done.21 = bf16[512,256]{1,0:T(8,128)(2,1)S(1)} collective-permute-done((bf16[512,256]{1,0:T(8,128)(2,1)S(1)}, bf16[512,256]{1,0:T(8,128)(2,1)S(1)}, u32[]{:S(2)}, u32[]{:S(2)}) %collective-permute-start.21) | collective-permute-done | bytes 262176 | tf_op jit(solution)/shard_map/ppermute | solution.py:38
  89.8 2.3 %collective-permute-done.19 = bf16[512,256]{1,0:T(8,128)(2,1)S(1)} collective-permute-done((bf16[512,256]{1,0:T(8,128)(2,1)S(1)}, bf16[512,256]{1,0:T(8,128)(2,1)S(1)}, u32[]{:S(2)}, u32[]{:S(2)}) %collective-permute-start.19) | collective-permute-done | bytes 262176 | tf_op jit(solution)/shard_map/ppermute | solution.py:38
  92.0 2.7 %collective-permute-start.28 = (bf16[1024,256]{1,0:T(8,128)(2,1)S(1)}, bf16[1024,256]{1,0:T(8,128)(2,1)}, u32[]{:S(2)}, u32[]{:S(2)}) collective-permute-start(bf16[1024,256]{1,0:T(8,128)(2,1)S(1)} %get-tuple-element.131), channel_id=1, source_target_pairs={{0,12},{1,13},{2,14},{3,15},{4,0},{5,1},{6,2},{7,3},{8,4},{9,5},{1... | collective-permute-start | bytes 1572872 | tf_op jit(solution)/shard_map/ppermute | solution.py:38
  94.7 0.1 convert_add_fusion.3
  94.8 0.9 fusion.2
  95.8 5.2 %collective-permute-start.30 = (bf16[1024,256]{1,0:T(8,128)(2,1)}, bf16[1024,256]{1,0:T(8,128)(2,1)S(1)}, u32[]{:S(2)}, u32[]{:S(2)}) collective-permute-start(bf16[1024,256]{1,0:T(8,128)(2,1)} %fusion.2), channel_id=1, source_target_pairs={{0,2},{1,3},{2,0},{3,1},{4,6},{5,7},{6,4},{7,5},{8,10},{9,11},{10,... | collective-permute-start | bytes 1572872 | tf_op jit(solution)/shard_map/ppermute | solution.py:38
  101.1 2.0 %collective-permute-start.31 = (bf16[128,512]{1,0:T(8,128)(2,1)S(1)}, bf16[128,512]{1,0:T(8,128)(2,1)S(1)}, u32[]{:S(2)}, u32[]{:S(2)}) collective-permute-start(bf16[128,512]{1,0:T(8,128)(2,1)S(1)} %pad_maximum_fusion.4), channel_id=1, source_target_pairs={{0,192},{16,208},{32,224},{48,240},{64,0},{80,16},{96,32},{112,48}... | collective-permute-start | bytes 393224 | tf_op jit(solution)/shard_map/ppermute | solution.py:42
  103.0 1.9 %collective-permute-done.27 = bf16[1024,256]{1,0:T(8,128)(2,1)} collective-permute-done((bf16[1024,256]{1,0:T(8,128)(2,1)S(1)}, bf16[1024,256]{1,0:T(8,128)(2,1)}, u32[]{:S(2)}, u32[]{:S(2)}) %collective-permute-start.27) | collective-permute-done | bytes 524320 | tf_op jit(solution)/shard_map/ppermute | solution.py:38
  104.9 2.6 %collective-permute-start.32 = (bf16[128,512]{1,0:T(8,128)(2,1)S(1)}, bf16[128,512]{1,0:T(8,128)(2,1)S(1)}, u32[]{:S(2)}, u32[]{:S(2)}) collective-permute-start(bf16[128,512]{1,0:T(8,128)(2,1)S(1)} %pad_maximum_fusion.4), channel_id=1, source_target_pairs={{0,128},{16,144},{32,160},{48,176},{64,192},{80,208},{96,224},{112... | collective-permute-start | bytes 393224 | tf_op jit(solution)/shard_map/ppermute | solution.py:42
  107.6 6.6 %collective-permute-done.29 = bf16[1024,256]{1,0:T(8,128)(2,1)} collective-permute-done((bf16[1024,256]{1,0:T(8,128)(2,1)S(1)}, bf16[1024,256]{1,0:T(8,128)(2,1)}, u32[]{:S(2)}, u32[]{:S(2)}) %collective-permute-start.29) | collective-permute-done | bytes 524320 | tf_op jit(solution)/shard_map/ppermute | solution.py:38
  114.1 1.6 %convert_add_fusion.5 = (f32[512,256]{1,0:T(8,128)S(1)}, f32[512,256]{1,0:T(8,128)S(1)}) fusion(f32[1024,256]{1,0:T(8,128)S(1)} %get-tuple-element.129, s32[]{:T(128)S(6)} %select_n.250, bf16[1024,256]{1,0:T(8,128)(2,1)} %collective-permute-done.29, bf16[1024,256]{1,0:T(8,128)(2,1)} %collective-permute-done.28, ...), kind=kLoop, calls=%fused_computation.16 | loop fusion | flops 1572864 | bytes 3670024 | tf_op jit(solution)/shard_map/add | solution.py:302
  115.7 0.1 add_bitcast_fusion
  115.9 12.4 %collective-permute-start.34 = (f32[512,256]{1,0:T(8,128)S(1)}, f32[512,256]{1,0:T(8,128)S(1)}, u32[]{:S(2)}, u32[]{:S(2)}) collective-permute-start(f32[512,256]{1,0:T(8,128)S(1)} %get-tuple-element.158), channel_id=1, source_target_pairs={{0,1},{1,0},{2,3},{3,2},{4,5},{5,4},{6,7},{7,6},{8,9},{9,8},{10,11... | collective-permute-start | bytes 1572872 | tf_op jit(solution)/shard_map/ppermute | solution.py:38
  128.9 0.1 pad_maximum_fusion.1
  129.0 3.2 %fusion.1 = (f32[512,512]{1,0:T(8,128)}, f32[512,512]{1,0:T(8,128)}) fusion(f32[2,512,512]{2,1,0:T(8,128)} %param.11, s32[]{:T(128)S(6)} %select_n.261, bf16[128,512]{1,0:T(8,128)(2,1)S(1)} %get-tuple-element.154, bf16[128,512]{1,0:T(8,128)(2,1)S(1)} %get-tuple-element.155, bf16[128,512]{1,0:T(8,128)(2,1)S(1)} %get-tuple-element.156, ...), kind=kLoop, calls=%fused_computation.3 | loop fusion | flops 3670016 | bytes 4718596 | tf_op jit(solution)/shard_map/sub | solution.py:325
  132.3 1.1 maximum_select_fusion
  (48 shorter events, 0.4 us)
Async XLA Ops:
  0.6 19.8 %copy-start.2 = (f32[1,512,512]{2,1,0:T(8,128)S(1)}, f32[1,512,512]{2,1,0:T(8,128)}, u32[]{:S(2)}) copy-start(f32[1,512,512]{2,1,0:T(8,128)} %param.10) | copy-start | bytes 3145732
  1.8 6.2 %collective-permute-start = (bf16[512,256]{1,0:T(8,128)(2,1)S(1)}, bf16[512,256]{1,0:T(8,128)(2,1)S(1)}, u32[]{:S(2)}, u32[]{:S(2)}) collective-permute-start(bf16[512,256]{1,0:T(8,128)(2,1)S(1)} %get-tuple-element.164), channel_id=1, source_target_pairs={{0,1},{1,0},{2,3},{3,2},{4,5},{5,4},{6,7},{7,6},{8,9},{9,8},{10,11... | collective-permute-start | bytes 786440 | tf_op jit(solution)/shard_map/ppermute | solution.py:38
  6.9 12.1 %collective-permute-start.6 = (bf16[256,512]{1,0:T(8,128)(2,1)}, bf16[256,512]{1,0:T(8,128)(2,1)S(1)}, u32[]{:S(2)}, u32[]{:S(2)}) collective-permute-start(bf16[256,512]{1,0:T(8,128)(2,1)} %fusion.3), channel_id=1, source_target_pairs={{0,64},{16,80},{32,96},{48,112},{64,0},{80,16},{96,32},{112,48},{1... | collective-permute-start | bytes 786440 | tf_op jit(solution)/shard_map/ppermute | solution.py:219
  8.2 19.6 %collective-permute-start.1 = (bf16[1024,256]{1,0:T(8,128)(2,1)S(1)}, bf16[1024,256]{1,0:T(8,128)(2,1)S(1)}, u32[]{:S(2)}, u32[]{:S(2)}) collective-permute-start(bf16[1024,256]{1,0:T(8,128)(2,1)S(1)} %maximum_select_fusion.1.refs_3_), channel_id=1, source_target_pairs={{0,8},{1,9},{2,10},{3,11},{4,12},{5,13},{6,14},{7,15},{8,0},{9,1},... | collective-permute-start | bytes 1572872 | tf_op jit(solution)/shard_map/ppermute | solution.py:38
  10.6 23.3 %collective-permute-start.2 = (bf16[1024,256]{1,0:T(8,128)(2,1)S(1)}, bf16[1024,256]{1,0:T(8,128)(2,1)S(1)}, u32[]{:S(2)}, u32[]{:S(2)}) collective-permute-start(bf16[1024,256]{1,0:T(8,128)(2,1)S(1)} %maximum_select_fusion.1.refs_3_), channel_id=1, source_target_pairs={{0,12},{1,13},{2,14},{3,15},{4,0},{5,1},{6,2},{7,3},{8,4},{9,5},{1... | collective-permute-start | bytes 1572872 | tf_op jit(solution)/shard_map/ppermute | solution.py:38
  11.5 23.4 %collective-permute-start.3 = (bf16[1024,256]{1,0:T(8,128)(2,1)S(1)}, bf16[1024,256]{1,0:T(8,128)(2,1)S(1)}, u32[]{:S(2)}, u32[]{:S(2)}) collective-permute-start(bf16[1024,256]{1,0:T(8,128)(2,1)S(1)} %maximum_select_fusion.1.refs_3_), channel_id=1, source_target_pairs={{0,4},{1,5},{2,6},{3,7},{4,8},{5,9},{6,10},{7,11},{8,12},{9,13},{1... | collective-permute-start | bytes 1572872 | tf_op jit(solution)/shard_map/ppermute | solution.py:38
  12.1 22.8 %collective-permute-start.4 = (bf16[1024,256]{1,0:T(8,128)(2,1)S(1)}, bf16[1024,256]{1,0:T(8,128)(2,1)S(1)}, u32[]{:S(2)}, u32[]{:S(2)}) collective-permute-start(bf16[1024,256]{1,0:T(8,128)(2,1)S(1)} %maximum_select_fusion.1.refs_3_), channel_id=1, source_target_pairs={{0,2},{1,3},{2,0},{3,1},{4,6},{5,7},{6,4},{7,5},{8,10},{9,11},{10,... | collective-permute-start | bytes 1572872 | tf_op jit(solution)/shard_map/ppermute | solution.py:38
  19.0 2.6 %collective-permute-start.5 = (bf16[512,256]{1,0:T(8,128)(2,1)S(1)}, bf16[512,256]{1,0:T(8,128)(2,1)S(1)}, u32[]{:S(2)}, u32[]{:S(2)}) collective-permute-start(bf16[512,256]{1,0:T(8,128)(2,1)S(1)} %get-tuple-element.77), channel_id=1, source_target_pairs={{0,1},{1,0},{2,3},{3,2},{4,5},{5,4},{6,7},{7,6},{8,9},{9,8},{10,11... | collective-permute-start | bytes 786440 | tf_op jit(solution)/shard_map/ppermute | solution.py:38
  21.6 6.2 %collective-permute-start.7 = (bf16[128,512]{1,0:T(8,128)(2,1)S(1)}, bf16[128,512]{1,0:T(8,128)(2,1)S(1)}, u32[]{:S(2)}, u32[]{:S(2)}) collective-permute-start(bf16[128,512]{1,0:T(8,128)(2,1)S(1)} %dynamic-slice_convert_fusion.1), channel_id=1, source_target_pairs={{0,128},{16,144},{32,160},{48,176},{64,192},{80,208},{96,224},{112... | collective-permute-start | bytes 393224 | tf_op jit(solution)/shard_map/ppermute | solution.py:219
  34.9 14.7 %collective-permute-start.8 = (bf16[512,8192]{1,0:T(8,128)(2,1)}, bf16[512,8192]{1,0:T(8,128)(2,1)}, u32[]{:S(2)}, u32[]{:S(2)}) collective-permute-start(bf16[512,8192]{1,0:T(8,128)(2,1)} %own_ref), channel_id=1, source_target_pairs={{0,1},{1,0},{2,3},{3,2},{4,5},{5,4},{6,7},{7,6},{8,9},{9,8},{10,11... | collective-permute-start | bytes 25165832 | tf_op jit(solution)/shard_map/ppermute | solution.py:38
  35.4 11.3 %collective-permute-start.9 = (bf16[512,256]{1,0:T(8,128)(2,1)S(1)}, bf16[512,256]{1,0:T(8,128)(2,1)S(1)}, u32[]{:S(2)}, u32[]{:S(2)}) collective-permute-start(bf16[512,256]{1,0:T(8,128)(2,1)S(1)} %get-tuple-element.106.refs_11_), channel_id=1, source_target_pairs={{0,4},{1,5},{2,6},{3,7},{4,8},{5,9},{6,10},{7,11},{8,12},{9,13},{1... | collective-permute-start | bytes 786440 | tf_op jit(solution)/shard_map/ppermute | solution.py:38
  36.4 10.5 %collective-permute-start.11 = (bf16[512,256]{1,0:T(8,128)(2,1)S(1)}, bf16[512,256]{1,0:T(8,128)(2,1)}, u32[]{:S(2)}, u32[]{:S(2)}) collective-permute-start(bf16[512,256]{1,0:T(8,128)(2,1)S(1)} %get-tuple-element.107.refs_12_), channel_id=1, source_target_pairs={{0,12},{1,13},{2,14},{3,15},{4,0},{5,1},{6,2},{7,3},{8,4},{9,5},{1... | collective-permute-start | bytes 786440 | tf_op jit(solution)/shard_map/ppermute | solution.py:38
  38.3 20.2 %collective-permute-start.13 = (bf16[512,256]{1,0:T(8,128)(2,1)S(1)}, bf16[512,256]{1,0:T(8,128)(2,1)S(1)}, u32[]{:S(2)}, u32[]{:S(2)}) collective-permute-start(bf16[512,256]{1,0:T(8,128)(2,1)S(1)} %get-tuple-element.106.refs_11_), channel_id=1, source_target_pairs={{0,12},{1,13},{2,14},{3,15},{4,0},{5,1},{6,2},{7,3},{8,4},{9,5},{1... | collective-permute-start | bytes 786440 | tf_op jit(solution)/shard_map/ppermute | solution.py:38
  39.1 20.2 %collective-permute-start.14 = (bf16[512,256]{1,0:T(8,128)(2,1)S(1)}, bf16[512,256]{1,0:T(8,128)(2,1)S(1)}, u32[]{:S(2)}, u32[]{:S(2)}) collective-permute-start(bf16[512,256]{1,0:T(8,128)(2,1)S(1)} %get-tuple-element.107.refs_12_), channel_id=1, source_target_pairs={{0,4},{1,5},{2,6},{3,7},{4,8},{5,9},{6,10},{7,11},{8,12},{9,13},{1... | collective-permute-start | bytes 786440 | tf_op jit(solution)/shard_map/ppermute | solution.py:38
  39.8 3.4 %copy-start = (bf16[512,8192]{1,0:T(8,128)(2,1)S(1)}, bf16[512,8192]{1,0:T(8,128)(2,1)}, u32[]{:S(2)}) copy-start(bf16[512,8192]{1,0:T(8,128)(2,1)} %own_ref) | copy-start | bytes 25165828
  43.1 6.4 %copy-start.1 = (f32[128,512]{1,0:T(8,128)S(1)}, f32[128,512]{1,0:T(8,128)}, u32[]{:S(2)}) copy-start(f32[128,512]{1,0:T(8,128)} %constant_dynamic-slice_fusion.4) | copy-start | bytes 786436
  46.8 18.9 %collective-permute-start.10 = (bf16[512,256]{1,0:T(8,128)(2,1)S(1)}, bf16[512,256]{1,0:T(8,128)(2,1)S(1)}, u32[]{:S(2)}, u32[]{:S(2)}) collective-permute-start(bf16[512,256]{1,0:T(8,128)(2,1)S(1)} %collective-permute-done.9.refs_9_), channel_id=1, source_target_pairs={{0,4},{1,5},{2,6},{3,7},{4,8},{5,9},{6,10},{7,11},{8,12},{9,13},{1... | collective-permute-start | bytes 786440 | tf_op jit(solution)/shard_map/ppermute | solution.py:38
  46.9 18.8 %collective-permute-start.12 = (bf16[512,256]{1,0:T(8,128)(2,1)}, bf16[512,256]{1,0:T(8,128)(2,1)S(1)}, u32[]{:S(2)}, u32[]{:S(2)}) collective-permute-start(bf16[512,256]{1,0:T(8,128)(2,1)} %collective-permute-done.11.refs_8_), channel_id=1, source_target_pairs={{0,12},{1,13},{2,14},{3,15},{4,0},{5,1},{6,2},{7,3},{8,4},{9,5},{1... | collective-permute-start | bytes 786440 | tf_op jit(solution)/shard_map/ppermute | solution.py:38
  49.6 16.0 %collective-permute-start.15 = (f32[32,512]{1,0:T(8,128)S(1)}, f32[32,512]{1,0:T(8,128)S(1)}, u32[]{:S(2)}, u32[]{:S(2)}) collective-permute-start(f32[32,512]{1,0:T(8,128)S(1)} %get-tuple-element.167), channel_id=1, source_target_pairs={{0,16},{16,32},{32,48},{48,0},{64,80},{80,96},{96,112},{112,64},{1... | collective-permute-start | bytes 196616 | tf_op jit(solution)/shard_map/ppermute | solution.py:42
  58.4 7.2 %collective-permute-start.16 = (f32[32,512]{1,0:T(8,128)S(1)}, f32[32,512]{1,0:T(8,128)S(1)}, u32[]{:S(2)}, u32[]{:S(2)}) collective-permute-start(f32[32,512]{1,0:T(8,128)S(1)} %get-tuple-element.166), channel_id=1, source_target_pairs={{0,32},{16,48},{32,0},{48,16},{64,96},{80,112},{96,64},{112,80},{1... | collective-permute-start | bytes 196616 | tf_op jit(solution)/shard_map/ppermute | solution.py:42
  59.3 6.3 %collective-permute-start.17 = (f32[32,512]{1,0:T(8,128)S(1)}, f32[32,512]{1,0:T(8,128)S(1)}, u32[]{:S(2)}, u32[]{:S(2)}) collective-permute-start(f32[32,512]{1,0:T(8,128)S(1)} %get-tuple-element.165), channel_id=1, source_target_pairs={{0,48},{16,0},{32,16},{48,32},{64,112},{80,64},{96,80},{112,96},{1... | collective-permute-start | bytes 196616 | tf_op jit(solution)/shard_map/ppermute | solution.py:42
  65.7 17.6 %slice-start = ((s8[8388608]{0:T(1024)(128)(4,1)}), s8[4194304]{0:T(1024)(128)(4,1)S(1)}, s32[]{:S(2)}) async-start(s8[8388608]{0:T(1024)(128)(4,1)} %bitcast.52), calls=%async_computation | async-start | bytes 8388608
  65.7 17.6 %slice-start.1 = ((s8[8388608]{0:T(1024)(128)(4,1)}), s8[4194304]{0:T(1024)(128)(4,1)S(1)}, s32[]{:S(2)}) async-start(s8[8388608]{0:T(1024)(128)(4,1)} %bitcast.52), calls=%async_computation.1 | async-start | bytes 8388608
  71.9 5.8 %collective-permute-start.20 = (bf16[512,256]{1,0:T(8,128)(2,1)S(1)}, bf16[512,256]{1,0:T(8,128)(2,1)S(1)}, u32[]{:S(2)}, u32[]{:S(2)}) collective-permute-start(bf16[512,256]{1,0:T(8,128)(2,1)S(1)} %get-tuple-element.111), channel_id=1, source_target_pairs={{0,12},{1,13},{2,14},{3,15},{4,0},{5,1},{6,2},{7,3},{8,4},{9,5},{1... | collective-permute-start | bytes 786440 | tf_op jit(solution)/shard_map/ppermute | solution.py:38
  73.7 7.4 %collective-permute-start.18 = (bf16[512,256]{1,0:T(8,128)(2,1)S(1)}, bf16[512,256]{1,0:T(8,128)(2,1)S(1)}, u32[]{:S(2)}, u32[]{:S(2)}) collective-permute-start(bf16[512,256]{1,0:T(8,128)(2,1)S(1)} %get-tuple-element.109), channel_id=1, source_target_pairs={{0,4},{1,5},{2,6},{3,7},{4,8},{5,9},{6,10},{7,11},{8,12},{9,13},{1... | collective-permute-start | bytes 786440 | tf_op jit(solution)/shard_map/ppermute | solution.py:38
  73.8 7.8 %collective-permute-start.24 = (bf16[32,512]{1,0:T(8,128)(2,1)S(1)}, bf16[32,512]{1,0:T(8,128)(2,1)S(1)}, u32[]{:S(2)}, u32[]{:S(2)}) collective-permute-start(bf16[32,512]{1,0:T(8,128)(2,1)S(1)} %multiply_convert_fusion), channel_id=1, source_target_pairs={{0,48},{16,0},{32,16},{48,32},{64,112},{80,64},{96,80},{112,96},{1... | collective-permute-start | bytes 98312 | tf_op jit(solution)/shard_map/ppermute | solution.py:42
  75.2 7.9 %collective-permute-start.25 = (bf16[32,512]{1,0:T(8,128)(2,1)S(1)}, bf16[32,512]{1,0:T(8,128)(2,1)S(1)}, u32[]{:S(2)}, u32[]{:S(2)}) collective-permute-start(bf16[32,512]{1,0:T(8,128)(2,1)S(1)} %multiply_convert_fusion), channel_id=1, source_target_pairs={{0,32},{16,48},{32,0},{48,16},{64,96},{80,112},{96,64},{112,80},{1... | collective-permute-start | bytes 98312 | tf_op jit(solution)/shard_map/ppermute | solution.py:42
  75.2 13.2 %collective-permute-start.22 = (bf16[512,256]{1,0:T(8,128)(2,1)S(1)}, bf16[512,256]{1,0:T(8,128)(2,1)S(1)}, u32[]{:S(2)}, u32[]{:S(2)}) collective-permute-start(bf16[512,256]{1,0:T(8,128)(2,1)S(1)} %get-tuple-element.112), channel_id=1, source_target_pairs={{0,4},{1,5},{2,6},{3,7},{4,8},{5,9},{6,10},{7,11},{8,12},{9,13},{1... | collective-permute-start | bytes 786440 | tf_op jit(solution)/shard_map/ppermute | solution.py:38
  77.7 10.8 %collective-permute-start.23 = (bf16[512,256]{1,0:T(8,128)(2,1)S(1)}, bf16[512,256]{1,0:T(8,128)(2,1)S(1)}, u32[]{:S(2)}, u32[]{:S(2)}) collective-permute-start(bf16[512,256]{1,0:T(8,128)(2,1)S(1)} %get-tuple-element.113), channel_id=1, source_target_pairs={{0,12},{1,13},{2,14},{3,15},{4,0},{5,1},{6,2},{7,3},{8,4},{9,5},{1... | collective-permute-start | bytes 786440 | tf_op jit(solution)/shard_map/ppermute | solution.py:38
  81.2 8.6 %collective-permute-start.21 = (bf16[512,256]{1,0:T(8,128)(2,1)S(1)}, bf16[512,256]{1,0:T(8,128)(2,1)S(1)}, u32[]{:S(2)}, u32[]{:S(2)}) collective-permute-start(bf16[512,256]{1,0:T(8,128)(2,1)S(1)} %add_convert_fusion), channel_id=1, source_target_pairs={{0,12},{1,13},{2,14},{3,15},{4,0},{5,1},{6,2},{7,3},{8,4},{9,5},{1... | collective-permute-start | bytes 786440 | tf_op jit(solution)/shard_map/ppermute | solution.py:38
  81.5 10.5 %collective-permute-start.19 = (bf16[512,256]{1,0:T(8,128)(2,1)S(1)}, bf16[512,256]{1,0:T(8,128)(2,1)S(1)}, u32[]{:S(2)}, u32[]{:S(2)}) collective-permute-start(bf16[512,256]{1,0:T(8,128)(2,1)S(1)} %add_convert_fusion.1), channel_id=1, source_target_pairs={{0,4},{1,5},{2,6},{3,7},{4,8},{5,9},{6,10},{7,11},{8,12},{9,13},{1... | collective-permute-start | bytes 786440 | tf_op jit(solution)/shard_map/ppermute | solution.py:38
  83.1 5.3 %collective-permute-start.26 = (bf16[32,512]{1,0:T(8,128)(2,1)S(1)}, bf16[32,512]{1,0:T(8,128)(2,1)S(1)}, u32[]{:S(2)}, u32[]{:S(2)}) collective-permute-start(bf16[32,512]{1,0:T(8,128)(2,1)S(1)} %multiply_convert_fusion), channel_id=1, source_target_pairs={{0,16},{16,32},{32,48},{48,0},{64,80},{80,96},{96,112},{112,64},{1... | collective-permute-start | bytes 98312 | tf_op jit(solution)/shard_map/ppermute | solution.py:42
  92.0 12.9 %collective-permute-start.27 = (bf16[1024,256]{1,0:T(8,128)(2,1)S(1)}, bf16[1024,256]{1,0:T(8,128)(2,1)}, u32[]{:S(2)}, u32[]{:S(2)}) collective-permute-start(bf16[1024,256]{1,0:T(8,128)(2,1)S(1)} %get-tuple-element.130), channel_id=1, source_target_pairs={{0,4},{1,5},{2,6},{3,7},{4,8},{5,9},{6,10},{7,11},{8,12},{9,13},{1... | collective-permute-start | bytes 1572872 | tf_op jit(solution)/shard_map/ppermute | solution.py:38
  92.0 15.5 %collective-permute-start.28 = (bf16[1024,256]{1,0:T(8,128)(2,1)S(1)}, bf16[1024,256]{1,0:T(8,128)(2,1)}, u32[]{:S(2)}, u32[]{:S(2)}) collective-permute-start(bf16[1024,256]{1,0:T(8,128)(2,1)S(1)} %get-tuple-element.131), channel_id=1, source_target_pairs={{0,12},{1,13},{2,14},{3,15},{4,0},{5,1},{6,2},{7,3},{8,4},{9,5},{1... | collective-permute-start | bytes 1572872 | tf_op jit(solution)/shard_map/ppermute | solution.py:38
  94.7 19.4 %collective-permute-start.29 = (bf16[1024,256]{1,0:T(8,128)(2,1)S(1)}, bf16[1024,256]{1,0:T(8,128)(2,1)}, u32[]{:S(2)}, u32[]{:S(2)}) collective-permute-start(bf16[1024,256]{1,0:T(8,128)(2,1)S(1)} %get-tuple-element.132), channel_id=1, source_target_pairs={{0,8},{1,9},{2,10},{3,11},{4,12},{5,13},{6,14},{7,15},{8,0},{9,1},... | collective-permute-start | bytes 1572872 | tf_op jit(solution)/shard_map/ppermute | solution.py:38
  95.8 20.0 %collective-permute-start.30 = (bf16[1024,256]{1,0:T(8,128)(2,1)}, bf16[1024,256]{1,0:T(8,128)(2,1)S(1)}, u32[]{:S(2)}, u32[]{:S(2)}) collective-permute-start(bf16[1024,256]{1,0:T(8,128)(2,1)} %fusion.2), channel_id=1, source_target_pairs={{0,2},{1,3},{2,0},{3,1},{4,6},{5,7},{6,4},{7,5},{8,10},{9,11},{10,... | collective-permute-start | bytes 1572872 | tf_op jit(solution)/shard_map/ppermute | solution.py:38
  101.1 14.6 %collective-permute-start.31 = (bf16[128,512]{1,0:T(8,128)(2,1)S(1)}, bf16[128,512]{1,0:T(8,128)(2,1)S(1)}, u32[]{:S(2)}, u32[]{:S(2)}) collective-permute-start(bf16[128,512]{1,0:T(8,128)(2,1)S(1)} %pad_maximum_fusion.4), channel_id=1, source_target_pairs={{0,192},{16,208},{32,224},{48,240},{64,0},{80,16},{96,32},{112,48}... | collective-permute-start | bytes 393224 | tf_op jit(solution)/shard_map/ppermute | solution.py:42
  104.9 10.8 %collective-permute-start.32 = (bf16[128,512]{1,0:T(8,128)(2,1)S(1)}, bf16[128,512]{1,0:T(8,128)(2,1)S(1)}, u32[]{:S(2)}, u32[]{:S(2)}) collective-permute-start(bf16[128,512]{1,0:T(8,128)(2,1)S(1)} %pad_maximum_fusion.4), channel_id=1, source_target_pairs={{0,128},{16,144},{32,160},{48,176},{64,192},{80,208},{96,224},{112... | collective-permute-start | bytes 393224 | tf_op jit(solution)/shard_map/ppermute | solution.py:42
  107.6 8.2 %collective-permute-start.33 = (bf16[128,512]{1,0:T(8,128)(2,1)S(1)}, bf16[128,512]{1,0:T(8,128)(2,1)S(1)}, u32[]{:S(2)}, u32[]{:S(2)}) collective-permute-start(bf16[128,512]{1,0:T(8,128)(2,1)S(1)} %pad_maximum_fusion.4), channel_id=1, source_target_pairs={{0,64},{16,80},{32,96},{48,112},{64,128},{80,144},{96,160},{112,17... | collective-permute-start | bytes 393224 | tf_op jit(solution)/shard_map/ppermute | solution.py:42
  115.9 16.4 %collective-permute-start.34 = (f32[512,256]{1,0:T(8,128)S(1)}, f32[512,256]{1,0:T(8,128)S(1)}, u32[]{:S(2)}, u32[]{:S(2)}) collective-permute-start(f32[512,256]{1,0:T(8,128)S(1)} %get-tuple-element.158), channel_id=1, source_target_pairs={{0,1},{1,0},{2,3},{3,2},{4,5},{5,4},{6,7},{7,6},{8,9},{9,8},{10,11... | collective-permute-start | bytes 1572872 | tf_op jit(solution)/shard_map/ppermute | solution.py:38
